TPU v7x, 768 devices: a whole 4x8x12 slice. The times are simulated.
768 devices in a mesh: node: 32 (over x, y), local: 24 (over z, core).
Axes of the slice: x: 4, y: 8, z: 12, core: 2. Of those that a mesh axis runs over, the one named last changes fastest.
Arguments:
- grads: bfloat16 [98304, 5376], P(('node', 'local')), may hold values from -6 to 6
- token_slot: int32 [98304], P(('node', 'local')), may hold values from 0 to 383, as said below
- node_ids: int32 [32, 384], P('node', 'local'), may hold values from 0 to 262135, as said below
- touched_ids: int32 [12288], P(('node', 'local')), may hold values from -1 to 262135, as said below
- owner_map: int32 [768, 32, 2], P(('node', 'local')), may hold values from -1 to 15, as said below
- moment: float32 [12288, 5376], P(('node', 'local')), may hold values from -4 to 4
- second: float32 [12288, 5376], P(('node', 'local')), may hold values from 0.01 to 1
- master: float32 [12288, 5376], P(('node', 'local')), may hold values from -0.12 to 0.12
Outputs:
- token_rows: bfloat16 [98304, 5376], P(('node', 'local'))
- moment_out: float32 [12288, 5376], P(('node', 'local'))
- second_out: float32 [12288, 5376], P(('node', 'local'))
- master_out: float32 [12288, 5376], P(('node', 'local'))
Inputs may be any that keep to these rules, and one draw needn't show every extreme that they name: `node_ids`: within one device's 16 entries the ids are distinct and at most 2 of them share an owner node id // 8192; for each local index one owner node receives exactly 2 ids from every node's device of that local index. `token_slot`: every entry of a node's list is used by some token of that node. `touched_ids`: on device (o, j) the entries that are not -1 are distinct ids with owner node o, and they are exactly the ids that devices of local index j list with owner node o. `owner_map`: on device (o, j), entry [n, c] is the position in this device's touched_ids of the c-th id, in list order, that device (n, j) lists with owner node o, and -1 where device (n, j) lists fewer than c + 1 such ids.
All inputs are finite; a program needn't handle non-finite values.
Results may differ from a plain program's by a relative error of at most 0.014.
Values may be sent and summed in bfloat16 or wider, within the bound.
No kernel may reach another device: no remote copies, remote signals or barrier semaphores. Data moves between devices by JAX's collectives and lax.ppermute only.
A program may use at most 32 MiB of HBM per device.

v0:
```python
import jax
import jax.numpy as jnp
from jax import lax
from jax.sharding import PartitionSpec as P

VOCAB = 262144
STEP = 100


BETA_ONE = 0.9
BETA_TWO = 0.999
LEARN_RATE = 0.01
EPSILON = 1e-08


def adam_rows(gradient, moment, second, master, alive_rows):
    corr_one = 1.0 - BETA_ONE**STEP
    corr_two = 1.0 - BETA_TWO**STEP
    moment_new = BETA_ONE * moment + (1.0 - BETA_ONE) * gradient
    second_new = BETA_TWO * second + (1.0 - BETA_TWO) * gradient * gradient
    master_new = master - LEARN_RATE * (moment_new / corr_one) / (
        jnp.sqrt(second_new / corr_two) + EPSILON
    )
    kept = alive_rows[:, None]
    return (
        jnp.where(kept, moment_new, moment),
        jnp.where(kept, second_new, second),
        jnp.where(kept, master_new, master),
    )


def on_device(grads, token_slot, node_ids, touched_ids, owner_map, moment, second, master):
    slot_dev = node_ids.shape[1]
    width = grads.shape[1]
    node_count = lax.axis_size("node")
    capacity = owner_map.shape[2]
    touch_cap = touched_ids.shape[0]
    wanted = lax.iota(jnp.int32, slot_dev * lax.axis_size("local"))
    selector = (wanted[:, None] == token_slot[None, :]).astype(jnp.bfloat16)
    node_sum = lax.psum_scatter(
        jnp.dot(selector, grads, preferred_element_type=jnp.float32).astype(jnp.bfloat16),
        "local",
        scatter_dimension=0,
        tiled=True,
    )
    owner_node = node_ids[0] // (VOCAB // node_count)
    same_owner = owner_node[:, None] == owner_node[None, :]
    positions = lax.iota(jnp.int32, slot_dev)
    earlier = positions[None, :] < positions[:, None]
    rank_slot = jnp.sum((same_owner & earlier).astype(jnp.int32), axis=1)
    send_slot = owner_node * capacity + rank_slot
    route_map = (lax.iota(jnp.int32, node_count * capacity)[:, None] == send_slot[None, :]).astype(
        jnp.bfloat16
    )
    outgoing = jnp.dot(route_map, node_sum, preferred_element_type=jnp.float32).astype(jnp.bfloat16)
    incoming = lax.all_to_all(
        outgoing.reshape(node_count, capacity, width),
        "node",
        split_axis=0,
        concat_axis=0,
        tiled=True,
    )
    position_map = owner_map.reshape(-1)
    collect = (lax.iota(jnp.int32, touch_cap)[:, None] == position_map[None, :]).astype(
        jnp.bfloat16
    )
    gradient = jnp.dot(
        collect, incoming.reshape(node_count * capacity, width), preferred_element_type=jnp.float32
    )
    moment_out, second_out, master_out = adam_rows(
        gradient, moment, second, master, touched_ids >= 0
    )
    fresh_rows = master_out.astype(jnp.bfloat16)
    reply_rows = lax.dot_general(
        collect, fresh_rows, (((0,), (0,)), ((), ())), preferred_element_type=jnp.float32
    ).astype(jnp.bfloat16)
    returned = lax.all_to_all(
        reply_rows.reshape(node_count, capacity, width),
        "node",
        split_axis=0,
        concat_axis=0,
        tiled=True,
    )
    listed_rows = lax.dot_general(
        route_map,
        returned.reshape(node_count * capacity, width),
        (((0,), (0,)), ((), ())),
        preferred_element_type=jnp.float32,
    ).astype(jnp.bfloat16)
    shard_rows = lax.all_gather(listed_rows, "local", axis=0, tiled=True)
    wanted = lax.iota(jnp.int32, shard_rows.shape[0])
    selector = (token_slot[:, None] == wanted[None, :]).astype(jnp.bfloat16)
    token_rows = jnp.dot(selector, shard_rows, preferred_element_type=jnp.float32)
    return (token_rows.astype(jnp.bfloat16), moment_out, second_out, master_out)


def solution(mesh):
    placed = (
        P(("node", "local"), None),
        P(("node", "local")),
        P("node", "local"),
        P(("node", "local")),
        P(("node", "local"), None, None),
        P(("node", "local"), None),
        P(("node", "local"), None),
        P(("node", "local"), None),
    )
    return jax.shard_map(
        on_device,
        mesh=mesh,
        in_specs=placed,
        out_specs=(
            P(("node", "local"), None),
            P(("node", "local"), None),
            P(("node", "local"), None),
            P(("node", "local"), None),
        ),
        check_vma=False,
    )
```

profile of v0, /device:TPU:1, one launch (start us, length us, event | category | flops | bytes accessed | tf_op | source)
XLA Modules:
  0.0 243.3 jit_solution(18265223356112892192)
XLA Ops:
  7.2 0.0 copy-start
  7.2 0.0 reduce-scatter.2.cloned.1.call-start
  7.2 1.3 copy-done
  8.5 3.8 %convolution_convert_fusion = bf16[384,5376]{1,0:T(8,128)(2,1)} fusion(bf16[128,5376]{1,0:T(8,128)(2,1)S(1)} %copy-done, s32[128]{0:T(128)} %param.9), kind=kOutput, calls=%fused_computation | convolution fusion | flops 530595840 | bytes 5505536 | tf_op jit(solution)/shard_map/dot_general | solution.py:41
  12.3 0.0 reduce-scatter.2.cloned.1.call-update
  12.3 0.6 copy-done.6
  13.0 0.2 convert_reduce_fusion
  13.2 95.8 %reduce-scatter.2.cloned.1.call-done = bf16[16,5376]{1,0:T(8,128)(2,1)} async-done(((bf16[384,5376]{1,0:T(8,128)(2,1)}), bf16[16,5376]{1,0:T(8,128)(2,1)}) %reduce-scatter.2.cloned.1.call-update) | async-done | bytes 172048 | tf_op jit(solution)/shard_map/reduce_scatter | solution.py:40
  109.0 1.2 convolution_convert_fusion.3
  110.2 1.1 reshape.53
  111.3 9.2 %all-to-all-start = ((bf16[32,2,5376]{2,1,0:T(2,128)(2,1)}), bf16[32,2,5376]{2,1,0:T(2,128)(2,1)S(1)}, u32[]{:S(2)}, u32[]{:S(2)}) async-start(bf16[32,2,5376]{2,1,0:T(2,128)(2,1)} %reshape.53), calls=%async_computation.1 | async-start | bytes 1376256 | tf_op jit(solution)/shard_map/all_to_all | solution.py:56
  120.5 0.0 all-gather.2.cloned.1.call-start
  120.5 0.0 copy-done.3
  120.5 0.1 copy.14
  120.6 0.1 eq.83
  120.7 0.0 copy-done.7
  120.7 13.9 %all-to-all-done = bf16[32,2,5376]{2,1,0:T(2,128)(2,1)S(1)} async-done(((bf16[32,2,5376]{2,1,0:T(2,128)(2,1)}), bf16[32,2,5376]{2,1,0:T(2,128)(2,1)S(1)}, u32[]{:S(2)}, u32[]{:S(2)}) %all-to-all-start) | async-done | bytes 688160 | tf_op jit(solution)/shard_map/all_to_all | solution.py:56
  134.7 0.3 reshape.54
  134.9 0.0 copy-done.4
  134.9 0.0 copy-done.5
  134.9 2.2 fusion.2
  137.2 0.7 copy-done.1
  137.9 0.4 convolution_convert_fusion.2
  138.3 0.0 copy-start.2
  138.3 0.3 reshape.55
  138.6 21.9 %all_to_all.10 = bf16[32,2,5376]{2,1,0:T(2,128)(2,1)S(1)} all-to-all(bf16[32,2,5376]{2,1,0:T(2,128)(2,1)S(1)} %reshape.55), channel_id=1, replica_groups=mesh['node'=32,'local'=24] {'node'}, dimensions={0} | all-to-all | bytes 1376256 | tf_op jit(solution)/shard_map/all_to_all | solution.py:77
  160.5 0.3 reshape.56
  160.8 0.9 convolution_convert_fusion.4
  161.7 0.0 all-gather.2.cloned.1.call-update
  161.7 70.6 %all-gather.2.cloned.1.call-done = bf16[384,5376]{1,0:T(8,128)(2,1)} async-done(((bf16[16,5376]{1,0:T(8,128)(2,1)}), bf16[384,5376]{1,0:T(8,128)(2,1)}) %all-gather.2.cloned.1.call-update) | async-done | bytes 4128784 | tf_op jit(solution)/shard_map/all_gather | solution.py:90
  232.3 0.0 copy-done.2
  232.3 4.2 %convolution_convert_fusion.1 = bf16[128,5376]{1,0:T(8,128)(2,1)} fusion(bf16[384,5376]{1,0:T(8,128)(2,1)} %all-gather.2.cloned.1.call-done, s32[128]{0:T(128)S(1)} %copy-done.2), kind=kOutput, calls=%fused_computation.1 | convolution fusion | flops 529219584 | bytes 5505536 | tf_op jit(solution)/shard_map/dot_general | solution.py:93
  (10 shorter events, 0.0 us)
Async XLA Ops:
  7.2 1.3 copy-start
  7.2 101.8 %reduce-scatter.2.cloned.1.call-start = ((), (), s32[]{:S(2)}) async-start(), calls=%async_computation.3 | async-start | bytes 4300800 | tf_op jit(solution)/shard_map/reduce_scatter | solution.py:40
  12.3 0.7 copy-start.6
  13.0 107.6 %copy-start.3 = (s32[1,32,2]{1,2,0:T(2,128)S(1)}, s32[1,32,2]{1,2,0:T(2,128)}, u32[]{:S(2)}) copy-start(s32[1,32,2]{1,2,0:T(2,128)} %param.12) | copy-start | bytes 772
  13.0 107.8 %copy-start.7 = (s32[16]{0:T(128)S(1)}, s32[16]{0:T(128)}, u32[]{:S(2)}) copy-start(s32[16]{0:T(128)} %param.11) | copy-start | bytes 196
  13.0 122.0 %copy-start.4 = (f32[16,5376]{1,0:T(8,128)S(1)}, f32[16,5376]{1,0:T(8,128)}, u32[]{:S(2)}) copy-start(f32[16,5376]{1,0:T(8,128)} %param.14) | copy-start | bytes 1032196
  13.0 122.0 %copy-start.5 = (f32[16,5376]{1,0:T(8,128)S(1)}, f32[16,5376]{1,0:T(8,128)}, u32[]{:S(2)}) copy-start(f32[16,5376]{1,0:T(8,128)} %param.15) | copy-start | bytes 1032196
  111.3 23.4 %all-to-all-start = ((bf16[32,2,5376]{2,1,0:T(2,128)(2,1)}), bf16[32,2,5376]{2,1,0:T(2,128)(2,1)S(1)}, u32[]{:S(2)}, u32[]{:S(2)}) async-start(bf16[32,2,5376]{2,1,0:T(2,128)(2,1)} %reshape.53), calls=%async_computation.1 | async-start | bytes 1376256 | tf_op jit(solution)/shard_map/all_to_all | solution.py:56
  120.5 111.8 %all-gather.2.cloned.1.call-start = ((), (), s32[]{:S(2)}) async-start(), calls=%async_computation.4 | async-start | bytes 4300800 | tf_op jit(solution)/shard_map/all_gather | solution.py:90
  137.2 0.7 copy-start.1
  138.3 94.0 %copy-start.2 = (s32[128]{0:T(128)S(1)}, s32[128]{0:T(128)}, u32[]{:S(2)}) copy-start(s32[128]{0:T(128)} %param.9) | copy-start | bytes 1540
Sparse Core Ops, SparseCore 0:
  12.4 96.4 reduce-scatter.1
  161.9 70.3 all-gather.1
where the time goes:
time: 244 us; the launch traced here: 243 us
  waiting for transfers between devices  180 us (74%)
  blocking collectives  21.9 us (9%)
  between operations  14.2 us (6%)
  matrix products  12.7 us (5%)
  starting transfers between devices  9.24 us (4%)
  local copies, waits for them, and re-layouts  4.75 us (2%)
    reduce_scatter x1, waiting for transfers between devices, on_device(): lax.psum_scatter(jnp.dot(selector, grads, preferred_element_type=jnp.floa...  95.8 us
    all_gather x1, waiting for transfers between devices, on_device(): shard_rows = lax.all_gather(listed_rows, 'local', axis=0, tiled=True)  70.6 us
    all_to_all x1, blocking collectives, on_device(): lax.all_to_all(reply_rows.reshape(node_count, capacity, width), 'node', s...  21.9 us
    all_to_all x1, waiting for transfers between devices, on_device(): lax.all_to_all(outgoing.reshape(node_count, capacity, width), 'node', spl...  13.9 us
    all_to_all x1, starting transfers between devices, on_device(): lax.all_to_all(outgoing.reshape(node_count, capacity, width), 'node', spl...  9.16 us
  transfers between devices with their start and end apart: 3, of which 3 were waited for; matrix products, arithmetic and copies ran while one was open for 0% of the time, Pallas kernels for 0%

commit v1 on v0

v1 whole, which is shorter than its diff:
```python
import jax
import jax.numpy as jnp
from jax import lax
from jax.sharding import Mesh
from jax.sharding import PartitionSpec as P

VOCAB = 262144
STEP = 100


BETA_ONE = 0.9
BETA_TWO = 0.999
LEARN_RATE = 0.01
EPSILON = 1e-08

X_SIZE, Y_SIZE, Z_SIZE, CORES = 4, 8, 12, 2
FIRST_COLS = 2816

SWAP = [(0, 1), (1, 0)]


def adam_rows(gradient, moment, second, master, alive_rows):
    corr_one = 1.0 - BETA_ONE**STEP
    corr_two = 1.0 - BETA_TWO**STEP
    moment_new = BETA_ONE * moment + (1.0 - BETA_ONE) * gradient
    second_new = BETA_TWO * second + (1.0 - BETA_TWO) * gradient * gradient
    master_new = master - LEARN_RATE * (moment_new / corr_one) / (
        jnp.sqrt(second_new / corr_two) + EPSILON
    )
    kept = alive_rows[:, None]
    return (
        jnp.where(kept, moment_new, moment),
        jnp.where(kept, second_new, second),
        jnp.where(kept, master_new, master),
    )


def matches(rows, columns):
    return (rows[:, None] == columns[None, :]).astype(jnp.bfloat16)


def dot32(a, b):
    return jnp.dot(a, b, preferred_element_type=jnp.float32)


def on_device(grads, token_slot, node_ids, touched_ids, owner_map, moment, second, master):
    slot_dev = node_ids.shape[1]
    node_count = X_SIZE * Y_SIZE
    capacity = owner_map.shape[2]
    touch_cap = touched_ids.shape[0]
    core = lax.axis_index("c")
    place = lax.axis_index("z")

    other_slot = lax.ppermute(token_slot, "c", SWAP)

    def listed(z_of_row, core_index):
        k = lax.rem(lax.iota(jnp.int32, z_of_row.shape[0]), slot_dev)
        return (z_of_row * CORES + core_index) * slot_dev + k

    def partial_sum(rows, own, other):
        return (
            dot32(matches(rows, token_slot), own) + dot32(matches(rows, other_slot), other)
        ).astype(jnp.bfloat16)

    all_z = lax.div(lax.iota(jnp.int32, Z_SIZE * slot_dev), slot_dev)

    owner_node = node_ids[0] // (VOCAB // node_count)
    same_owner = owner_node[:, None] == owner_node[None, :]
    positions = lax.iota(jnp.int32, slot_dev)
    earlier = positions[None, :] < positions[:, None]
    rank_slot = jnp.sum((same_owner & earlier).astype(jnp.int32), axis=1)
    send_slot = owner_node * capacity + rank_slot
    route_map = matches(lax.iota(jnp.int32, node_count * capacity), send_slot)
    collect = matches(lax.iota(jnp.int32, touch_cap), owner_map.reshape(-1))

    def exchange(rows):
        width = rows.shape[1]
        return lax.all_to_all(
            rows.reshape(node_count, capacity, width),
            ("x", "y"),
            split_axis=0,
            concat_axis=0,
            tiled=True,
        ).reshape(node_count * capacity, width)

    def update(node_sum, columns):
        outgoing = dot32(route_map, node_sum).astype(jnp.bfloat16)
        gradient = dot32(collect, exchange(outgoing))
        states = adam_rows(
            gradient,
            moment[:, columns],
            second[:, columns],
            master[:, columns],
            touched_ids >= 0,
        )
        fresh_rows = states[2].astype(jnp.bfloat16)
        reply_rows = lax.dot_general(
            collect, fresh_rows, (((0,), (0,)), ((), ())), preferred_element_type=jnp.float32
        ).astype(jnp.bfloat16)
        returned = exchange(reply_rows)
        rows = lax.dot_general(
            route_map, returned, (((0,), (0,)), ((), ())), preferred_element_type=jnp.float32
        ).astype(jnp.bfloat16)
        return rows, states

    width = grads.shape[1]
    cols_a, cols_b = slice(0, FIRST_COLS), slice(FIRST_COLS, width)
    grads_a, grads_b = grads[:, cols_a], grads[:, cols_b]
    other_b = lax.ppermute(grads_b, "c", SWAP)
    other_a = lax.ppermute(grads_a, "c", SWAP)

    part_b = partial_sum(listed(all_z, core), grads_b, other_b)
    part_b, grads_a = lax.optimization_barrier((part_b, grads_a))
    sum_b = lax.psum_scatter(part_b, "z", scatter_dimension=0, tiled=True)

    part_a = partial_sum(listed(all_z, core), grads_a, other_a)
    blocks = lax.all_to_all(
        part_a.reshape(Z_SIZE, slot_dev, part_a.shape[1]),
        "z",
        split_axis=0,
        concat_axis=0,
        tiled=True,
    )
    sum_a = jnp.sum(blocks.astype(jnp.float32), axis=0).astype(jnp.bfloat16)

    rows_a, states_a = update(sum_a, cols_a)
    gathered_a = lax.all_gather(rows_a, ("z", "c"), axis=0, tiled=True)
    rows_b, states_b = update(sum_b, cols_b)
    own_b = lax.all_gather(rows_b, "z", axis=0, tiled=True)
    swapped_b = lax.ppermute(own_b, "c", SWAP)

    whole = lax.iota(jnp.int32, Z_SIZE * CORES * slot_dev)
    tokens_a = dot32(matches(token_slot, whole), gathered_a).astype(jnp.bfloat16)
    tokens_b = (
        dot32(matches(token_slot, listed(all_z, core)), own_b)
        + dot32(matches(token_slot, listed(all_z, 1 - core)), swapped_b)
    ).astype(jnp.bfloat16)
    moment_out, second_out, master_out = (
        jnp.concatenate([a, b], axis=1) for a, b in zip(states_a, states_b)
    )
    return (
        jnp.concatenate([tokens_a, tokens_b], axis=1),
        moment_out,
        second_out,
        master_out,
    )


def solution(mesh):
    axes = ("x", "y", "z", "c")
    fine = Mesh(mesh.devices.reshape(X_SIZE, Y_SIZE, Z_SIZE, CORES), axes)
    rows = P(axes, None)
    return jax.shard_map(
        on_device,
        mesh=fine,
        in_specs=(
            rows,
            P(axes),
            P(("x", "y"), ("z", "c")),
            P(axes),
            P(axes, None, None),
            rows,
            rows,
            rows,
        ),
        out_specs=(rows, rows, rows, rows),
        check_vma=False,
    )
```

time: 244 us -> 208 us (0.85)
  waiting for transfers between devices: 180 us -> 79.5 us
  starting transfers between devices: 9.24 us -> 59.1 us
  blocking collectives: 21.9 us -> 32.1 us
  other arithmetic: 0.22 us -> 3.19 us
    reduce_scatter x1, waiting for transfers between devices: 95.8 us -> 0.02 us  [on_device(): sum_b = lax.psum_scatter(part_b, 'z', scatter_dimension=0, tiled=True)]
    all_gather x1, waiting for transfers between devices: 70.6 us -> 0.03 us  [on_device(): gathered_a = lax.all_gather(rows_a, ('z', 'c'), axis=0, tiled=True)]
    all_to_all x1 -> x5, waiting for transfers between devices: 13.9 us -> 78.9 us  [the longest x1 42.2 us: on_device(): lax.all_to_all(part_a.reshape(Z_SIZE, slot_dev, part_a.shape[1]), 'z', sp...]
    all_gather x0 -> x1, blocking collectives: none -> 32.1 us  [on_device(): own_b = lax.all_gather(rows_b, 'z', axis=0, tiled=True)]
    ppermute x0 -> x4, starting transfers between devices: none -> 28.2 us  [the longest x1 12.4 us: on_device(): other_b = lax.ppermute(grads_b, 'c', SWAP)]
    all_to_all x1 -> x0, blocking collectives: 21.9 us -> none  [on_device(): lax.all_to_all(reply_rows.reshape(node_count, capacity, width), 'node', s...]
    all_to_all x1 -> x5, starting transfers between devices: 9.16 us -> 30.9 us  [the longest x4 24.9 us: exchange(): lax.all_to_all(rows.reshape(node_count, capacity, width), ('x', 'y'), spl...]
    concatenate x0 -> x3, other arithmetic: none -> 2.81 us  [the longest x2 1.64 us: on_device(): jnp.concatenate([a, b], axis=1)]
  transfers between devices with their start and end apart: 3 -> 11, of which waited for: 3 -> 6; matrix products, arithmetic and copies ran while one was open for 0% -> 7% of each run, Pallas kernels for 0% -> 0%
where the time goes in v1:
time: 208 us
  waiting for transfers between devices  79.5 us (38%)
  starting transfers between devices  59.1 us (28%)
  blocking collectives  32.1 us (15%)
  between operations  15.8 us (8%)
  matrix products  11.4 us (5%)
  local copies, waits for them, and re-layouts  6.49 us (3%)
  other arithmetic  3.19 us (2%)
    all_to_all x1, waiting for transfers between devices, on_device(): lax.all_to_all(part_a.reshape(Z_SIZE, slot_dev, part_a.shape[1]), 'z', sp...  42.2 us
    all_to_all x4, waiting for transfers between devices, exchange(): lax.all_to_all(rows.reshape(node_count, capacity, width), ('x', 'y'), spl...  36.6 us
    all_gather x1, blocking collectives, on_device(): own_b = lax.all_gather(rows_b, 'z', axis=0, tiled=True)  32.1 us
    all_to_all x4, starting transfers between devices, exchange(): lax.all_to_all(rows.reshape(node_count, capacity, width), ('x', 'y'), spl...  24.9 us
    ppermute x1, starting transfers between devices, on_device(): other_b = lax.ppermute(grads_b, 'c', SWAP)  12.4 us
    ppermute x1, starting transfers between devices, on_device(): swapped_b = lax.ppermute(own_b, 'c', SWAP)  11.4 us
    dot_general x11, matrix products, dot32(): return jnp.dot(a, b, preferred_element_type=jnp.float32)  9.77 us
    all_to_all x1, starting transfers between devices, on_device(): lax.all_to_all(part_a.reshape(Z_SIZE, slot_dev, part_a.shape[1]), 'z', sp...  6 us
  transfers between devices with their start and end apart: 11, of which 6 were waited for; matrix products, arithmetic and copies ran while one was open for 7% of the time, Pallas kernels for 0%

profile of v1, /device:TPU:1, one launch (start us, length us, event | category | flops | bytes accessed | tf_op | source)
XLA Modules:
  0.0 207.7 jit_solution(14701657738251445959)
XLA Ops:
  8.0 1.1 slice.26
  9.1 12.4 %collective-permute-start.1 = (bf16[128,2560]{1,0:T(8,128)(2,1)S(1)}, bf16[128,2560]{1,0:T(8,128)(2,1)S(1)}, u32[]{:S(2)}, u32[]{:S(2)}) collective-permute-start(bf16[128,2560]{1,0:T(8,128)(2,1)S(1)} %slice.26), channel_id=1, source_target_pairs={{0,1},{1,0},{2,3},{3,2},{4,5},{5,4},{6,7},{7,6},{8,9},{9,8},{10,11... | collective-permute-start | bytes 1966088 | tf_op jit(solution)/shard_map/ppermute | solution.py:109
  21.6 1.9 collective-permute-start
  23.5 1.2 slice.27
  24.7 2.4 %collective-permute-start.2 = (bf16[128,2816]{1,0:T(8,128)(2,1)S(1)}, bf16[128,2816]{1,0:T(8,128)(2,1)S(1)}, u32[]{:S(2)}, u32[]{:S(2)}) collective-permute-start(bf16[128,2816]{1,0:T(8,128)(2,1)S(1)} %slice.27), channel_id=1, source_target_pairs={{0,1},{1,0},{2,3},{3,2},{4,5},{5,4},{6,7},{7,6},{8,9},{9,8},{10,11... | collective-permute-start | bytes 2162696 | tf_op jit(solution)/shard_map/ppermute | solution.py:110
  27.1 1.5 fusion.12
  28.7 1.4 fusion.1
  30.1 0.5 fusion.10
  30.6 1.5 fusion
  32.1 6.0 %all-to-all-start = ((bf16[12,16,2816]{2,1,0:T(8,128)(2,1)}), bf16[12,16,2816]{2,1,0:T(8,128)(2,1)S(1)}, u32[]{:S(2)}, u32[]{:S(2)}) async-start(bf16[12,16,2816]{2,1,0:T(8,128)(2,1)} %bitcast.4), calls=%async_computation | async-start | bytes 2162688 | tf_op jit(solution)/shard_map/all_to_all | solution.py:117
  38.4 0.4 reduce-scatter.2.cloned.1.call-update
  38.9 42.2 %all-to-all-done = bf16[12,16,2816]{2,1,0:T(8,128)(2,1)S(1)} async-done(((bf16[12,16,2816]{2,1,0:T(8,128)(2,1)}), bf16[12,16,2816]{2,1,0:T(8,128)(2,1)S(1)}, u32[]{:S(2)}, u32[]{:S(2)}) %all-to-all-start) | async-done | bytes 1081376 | tf_op jit(solution)/shard_map/all_to_all | solution.py:117
  81.5 0.9 reshape.101
  82.4 9.7 %all-to-all-start.1 = ((bf16[32,2,2816]{2,1,0:T(2,128)(2,1)}), bf16[32,2,2816]{2,1,0:T(2,128)(2,1)S(1)}, u32[]{:S(2)}, u32[]{:S(2)}) async-start(bf16[32,2,2816]{2,1,0:T(2,128)(2,1)} %reshape.101), calls=%async_computation.1 | async-start | bytes 720896 | tf_op jit(solution)/shard_map/all_to_all | solution.py:78
  92.4 9.8 %all-to-all-done.1 = bf16[32,2,2816]{2,1,0:T(2,128)(2,1)S(1)} async-done(((bf16[32,2,2816]{2,1,0:T(2,128)(2,1)}), bf16[32,2,2816]{2,1,0:T(2,128)(2,1)S(1)}, u32[]{:S(2)}, u32[]{:S(2)}) %all-to-all-start.1) | async-done | bytes 360480 | tf_op jit(solution)/shard_map/all_to_all | solution.py:78
  103.0 0.9 reshape.103
  103.8 5.3 %all-to-all-start.2 = ((bf16[32,2,2816]{2,1,0:T(2,128)(2,1)}), bf16[32,2,2816]{2,1,0:T(2,128)(2,1)S(1)}, u32[]{:S(2)}, u32[]{:S(2)}) async-start(bf16[32,2,2816]{2,1,0:T(2,128)(2,1)} %reshape.103), calls=%async_computation.2 | async-start | bytes 720896 | tf_op jit(solution)/shard_map/all_to_all | solution.py:78
  109.2 1.1 convolution_convert_fusion.3
  110.3 0.8 reshape.105
  111.1 8.1 %all-to-all-done.2 = bf16[32,2,2816]{2,1,0:T(2,128)(2,1)S(1)} async-done(((bf16[32,2,2816]{2,1,0:T(2,128)(2,1)}), bf16[32,2,2816]{2,1,0:T(2,128)(2,1)S(1)}, u32[]{:S(2)}, u32[]{:S(2)}) %all-to-all-start.2) | async-done | bytes 360480 | tf_op jit(solution)/shard_map/all_to_all | solution.py:78
  119.2 5.0 %all-to-all-start.3 = ((bf16[32,2,2560]{2,1,0:T(2,128)(2,1)}), bf16[32,2,2560]{2,1,0:T(2,128)(2,1)S(1)}, u32[]{:S(2)}, u32[]{:S(2)}) async-start(bf16[32,2,2560]{2,1,0:T(2,128)(2,1)} %reshape.105), calls=%async_computation.4 | async-start | bytes 655360 | tf_op jit(solution)/shard_map/all_to_all | solution.py:78
  124.4 0.9 convolution_convert_fusion.6
  125.3 8.8 %all-to-all-done.3 = bf16[32,2,2560]{2,1,0:T(2,128)(2,1)S(1)} async-done(((bf16[32,2,2560]{2,1,0:T(2,128)(2,1)}), bf16[32,2,2560]{2,1,0:T(2,128)(2,1)S(1)}, u32[]{:S(2)}, u32[]{:S(2)}) %all-to-all-start.3) | async-done | bytes 327712 | tf_op jit(solution)/shard_map/all_to_all | solution.py:78
  134.9 0.9 reshape.107
  135.7 4.8 %all-to-all-start.4 = ((bf16[32,2,2560]{2,1,0:T(2,128)(2,1)}), bf16[32,2,2560]{2,1,0:T(2,128)(2,1)S(1)}, u32[]{:S(2)}, u32[]{:S(2)}) async-start(bf16[32,2,2560]{2,1,0:T(2,128)(2,1)} %reshape.107), calls=%async_computation.5 | async-start | bytes 655360 | tf_op jit(solution)/shard_map/all_to_all | solution.py:78
  140.5 9.9 %all-to-all-done.4 = bf16[32,2,2560]{2,1,0:T(2,128)(2,1)S(1)} async-done(((bf16[32,2,2560]{2,1,0:T(2,128)(2,1)}), bf16[32,2,2560]{2,1,0:T(2,128)(2,1)S(1)}, u32[]{:S(2)}, u32[]{:S(2)}) %all-to-all-start.4) | async-done | bytes 327712 | tf_op jit(solution)/shard_map/all_to_all | solution.py:78
  150.8 32.1 %all_gather.7 = bf16[192,2560]{1,0:T(8,128)(2,1)S(1)} all-gather(bf16[16,2560]{1,0:T(8,128)(2,1)S(1)} %convolution_convert_fusion.5), channel_id=1, replica_groups=mesh['x'=4,'y'=8,'z'=12,'c'=2] {'z'}, dimensions={0}, use_global_device_ids=true | all-gather | bytes 1064960 | tf_op jit(solution)/shard_map/all_gather | solution.py:129
  182.8 11.4 %collective-permute-start.3 = (bf16[192,2560]{1,0:T(8,128)(2,1)S(1)}, bf16[192,2560]{1,0:T(8,128)(2,1)S(1)}, u32[]{:S(2)}, u32[]{:S(2)}) collective-permute-start(bf16[192,2560]{1,0:T(8,128)(2,1)S(1)} %all_gather.7), channel_id=1, source_target_pairs={{0,1},{1,0},{2,3},{3,2},{4,5},{5,4},{6,7},{7,6},{8,9},{9,8},{10,11... | collective-permute-start | bytes 2949128 | tf_op jit(solution)/shard_map/ppermute | solution.py:130
  194.7 0.8 pad_maximum_fusion.3
  195.4 0.9 pad_maximum_fusion.1
  196.9 2.2 %convolution_convert_fusion = bf16[128,2816]{1,0:T(8,128)(2,1)S(1)} fusion(bf16[384,2816]{1,0:T(8,128)(2,1)} %all-gather.2.cloned.1.call-done, s32[128]{0:T(128)S(1)} %copy-done), kind=kOutput, calls=%fused_computation.6 | convolution fusion | flops 277233664 | bytes 2884096 | tf_op jit(solution)/shard_map/dot_general | solution.py:43
  199.1 1.2 pad_maximum_fusion
  (45 shorter events, 3.8 us)
Async XLA Ops:
  8.0 19.1 %copy-start = (s32[128]{0:T(128)S(1)}, s32[128]{0:T(128)}, u32[]{:S(2)}) copy-start(s32[128]{0:T(128)} %param.9) | copy-start | bytes 1540
  9.1 19.5 %collective-permute-start.1 = (bf16[128,2560]{1,0:T(8,128)(2,1)S(1)}, bf16[128,2560]{1,0:T(8,128)(2,1)S(1)}, u32[]{:S(2)}, u32[]{:S(2)}) collective-permute-start(bf16[128,2560]{1,0:T(8,128)(2,1)S(1)} %slice.26), channel_id=1, source_target_pairs={{0,1},{1,0},{2,3},{3,2},{4,5},{5,4},{6,7},{7,6},{8,9},{9,8},{10,11... | collective-permute-start | bytes 1966088 | tf_op jit(solution)/shard_map/ppermute | solution.py:109
  21.6 7.1 %collective-permute-start = (s32[128]{0:T(128)}, s32[128]{0:T(128)S(1)}, u32[]{:S(2)}, u32[]{:S(2)}) collective-permute-start(s32[128]{0:T(128)} %param.9), channel_id=1, source_target_pairs={{0,1},{1,0},{2,3},{3,2},{4,5},{5,4},{6,7},{7,6},{8,9},{9,8},{10,11... | collective-permute-start | bytes 1544 | tf_op jit(solution)/shard_map/ppermute | solution.py:54
  24.7 5.9 %collective-permute-start.2 = (bf16[128,2816]{1,0:T(8,128)(2,1)S(1)}, bf16[128,2816]{1,0:T(8,128)(2,1)S(1)}, u32[]{:S(2)}, u32[]{:S(2)}) collective-permute-start(bf16[128,2816]{1,0:T(8,128)(2,1)S(1)} %slice.27), channel_id=1, source_target_pairs={{0,1},{1,0},{2,3},{3,2},{4,5},{5,4},{6,7},{7,6},{8,9},{9,8},{10,11... | collective-permute-start | bytes 2162696 | tf_op jit(solution)/shard_map/ppermute | solution.py:110
  32.1 6.1 %copy-start.5 = (s32[1,16]{1,0:T(1,128)S(1)}, s32[1,16]{1,0:T(1,128)}, u32[]{:S(2)}) copy-start(s32[1,16]{1,0:T(1,128)} %param.10) | copy-start | bytes 196
  32.1 49.0 %all-to-all-start = ((bf16[12,16,2816]{2,1,0:T(8,128)(2,1)}), bf16[12,16,2816]{2,1,0:T(8,128)(2,1)S(1)}, u32[]{:S(2)}, u32[]{:S(2)}) async-start(bf16[12,16,2816]{2,1,0:T(8,128)(2,1)} %bitcast.4), calls=%async_computation | async-start | bytes 2162688 | tf_op jit(solution)/shard_map/all_to_all | solution.py:117
  38.1 71.0 %reduce-scatter.2.cloned.1.call-start = ((), (), s32[]{:S(2)}) async-start(), calls=%async_computation.7 | async-start | bytes 1064960 | tf_op jit(solution)/shard_map/reduce_scatter | solution.py:114
  38.4 53.8 %copy-start.1 = (s32[1,32,2]{1,2,0:T(2,128)S(1)}, s32[1,32,2]{1,2,0:T(2,128)}, u32[]{:S(2)}) copy-start(s32[1,32,2]{1,2,0:T(2,128)} %param.12) | copy-start | bytes 772
  38.4 54.0 %copy-start.6 = (s32[16]{0:T(128)S(1)}, s32[16]{0:T(128)}, u32[]{:S(2)}) copy-start(s32[16]{0:T(128)} %param.11) | copy-start | bytes 196
  38.8 63.5 %copy-start.2 = (f32[16,5376]{1,0:T(8,128)S(1)}, f32[16,5376]{1,0:T(8,128)}, u32[]{:S(2)}) copy-start(f32[16,5376]{1,0:T(8,128)} %param.14) | copy-start | bytes 1032196
  38.9 63.5 %copy-start.3 = (f32[16,5376]{1,0:T(8,128)S(1)}, f32[16,5376]{1,0:T(8,128)}, u32[]{:S(2)}) copy-start(f32[16,5376]{1,0:T(8,128)} %param.13) | copy-start | bytes 1032196
  38.9 63.5 %copy-start.4 = (f32[16,5376]{1,0:T(8,128)S(1)}, f32[16,5376]{1,0:T(8,128)}, u32[]{:S(2)}) copy-start(f32[16,5376]{1,0:T(8,128)} %param.15) | copy-start | bytes 1032196
  82.4 19.8 %all-to-all-start.1 = ((bf16[32,2,2816]{2,1,0:T(2,128)(2,1)}), bf16[32,2,2816]{2,1,0:T(2,128)(2,1)S(1)}, u32[]{:S(2)}, u32[]{:S(2)}) async-start(bf16[32,2,2816]{2,1,0:T(2,128)(2,1)} %reshape.101), calls=%async_computation.1 | async-start | bytes 720896 | tf_op jit(solution)/shard_map/all_to_all | solution.py:78
  103.8 15.3 %all-to-all-start.2 = ((bf16[32,2,2816]{2,1,0:T(2,128)(2,1)}), bf16[32,2,2816]{2,1,0:T(2,128)(2,1)S(1)}, u32[]{:S(2)}, u32[]{:S(2)}) async-start(bf16[32,2,2816]{2,1,0:T(2,128)(2,1)} %reshape.103), calls=%async_computation.2 | async-start | bytes 720896 | tf_op jit(solution)/shard_map/all_to_all | solution.py:78
  119.2 15.0 %all-to-all-start.3 = ((bf16[32,2,2560]{2,1,0:T(2,128)(2,1)}), bf16[32,2,2560]{2,1,0:T(2,128)(2,1)S(1)}, u32[]{:S(2)}, u32[]{:S(2)}) async-start(bf16[32,2,2560]{2,1,0:T(2,128)(2,1)} %reshape.105), calls=%async_computation.4 | async-start | bytes 655360 | tf_op jit(solution)/shard_map/all_to_all | solution.py:78
  124.2 72.6 %all-gather.2.cloned.1.call-start = ((), (), s32[]{:S(2)}) async-start(), calls=%async_computation.6 | async-start | bytes 2252800 | tf_op jit(solution)/shard_map/all_gather | solution.py:127
  135.7 14.7 %all-to-all-start.4 = ((bf16[32,2,2560]{2,1,0:T(2,128)(2,1)}), bf16[32,2,2560]{2,1,0:T(2,128)(2,1)S(1)}, u32[]{:S(2)}, u32[]{:S(2)}) async-start(bf16[32,2,2560]{2,1,0:T(2,128)(2,1)} %reshape.107), calls=%async_computation.5 | async-start | bytes 655360 | tf_op jit(solution)/shard_map/all_to_all | solution.py:78
  182.8 13.6 %collective-permute-start.3 = (bf16[192,2560]{1,0:T(8,128)(2,1)S(1)}, bf16[192,2560]{1,0:T(8,128)(2,1)S(1)}, u32[]{:S(2)}, u32[]{:S(2)}) collective-permute-start(bf16[192,2560]{1,0:T(8,128)(2,1)S(1)} %all_gather.7), channel_id=1, source_target_pairs={{0,1},{1,0},{2,3},{3,2},{4,5},{5,4},{6,7},{7,6},{8,9},{9,8},{10,11... | collective-permute-start | bytes 2949128 | tf_op jit(solution)/shard_map/ppermute | solution.py:130
Sparse Core Ops, SparseCore 0:
  42.1 58.8 reduce-scatter.1
Sparse Core Ops, SparseCore 1:
  127.7 65.2 all-gather.1

commit v2 on v1

v2 whole, which is shorter than its diff:
```python
import jax
import jax.numpy as jnp
from jax import lax
from jax.sharding import Mesh
from jax.sharding import PartitionSpec as P

VOCAB = 262144
STEP = 100


BETA_ONE = 0.9
BETA_TWO = 0.999
LEARN_RATE = 0.01
EPSILON = 1e-08

X_SIZE, Y_SIZE, Z_SIZE, CORES = 4, 8, 12, 2
APART = 3
GROUP = Z_SIZE // APART
CHUNKS = 2

SWAP = [(0, 1), (1, 0)]


def shifted(steps):
    return [(i, (i + steps) % Z_SIZE) for i in range(Z_SIZE)]


def adam_rows(gradient, moment, second, master, alive_rows):
    corr_one = 1.0 - BETA_ONE**STEP
    corr_two = 1.0 - BETA_TWO**STEP
    moment_new = BETA_ONE * moment + (1.0 - BETA_ONE) * gradient
    second_new = BETA_TWO * second + (1.0 - BETA_TWO) * gradient * gradient
    master_new = master - LEARN_RATE * (moment_new / corr_one) / (
        jnp.sqrt(second_new / corr_two) + EPSILON
    )
    kept = alive_rows[:, None]
    return (
        jnp.where(kept, moment_new, moment),
        jnp.where(kept, second_new, second),
        jnp.where(kept, master_new, master),
    )


def matches(rows, columns):
    return (rows[:, None] == columns[None, :]).astype(jnp.bfloat16)


def dot32(a, b):
    return jnp.dot(a, b, preferred_element_type=jnp.float32)


def on_device(grads, token_slot, node_ids, touched_ids, owner_map, moment, second, master):
    slot_dev = node_ids.shape[1]
    node_count = X_SIZE * Y_SIZE
    capacity = owner_map.shape[2]
    touch_cap = touched_ids.shape[0]
    core = lax.axis_index("c")
    place = lax.axis_index("z")

    other_grads = lax.ppermute(grads, "c", SWAP)
    other_slot = lax.ppermute(token_slot, "c", SWAP)

    def rows_of(shift):
        row = lax.iota(jnp.int32, GROUP * slot_dev)
        z_of_row = lax.rem(place + (shift + Z_SIZE) + lax.div(row, slot_dev) * APART, Z_SIZE)
        return (z_of_row * CORES + core) * slot_dev + lax.rem(row, slot_dev)

    rows_here, rows_up, rows_down = rows_of(0), rows_of(1), rows_of(-1)

    def partial_sum(rows, columns):
        return (
            dot32(matches(rows, token_slot), grads[:, columns])
            + dot32(matches(rows, other_slot), other_grads[:, columns])
        ).astype(jnp.bfloat16)

    def node_sums(columns):
        from_down = lax.ppermute(partial_sum(rows_up, columns), "z", shifted(1))
        from_up = lax.ppermute(partial_sum(rows_down, columns), "z", shifted(-1))
        near = (
            partial_sum(rows_here, columns).astype(jnp.float32)
            + from_down.astype(jnp.float32)
            + from_up.astype(jnp.float32)
        ).astype(jnp.bfloat16)
        total = near[:slot_dev].astype(jnp.float32)
        for i in range(1, GROUP):
            block = near[i * slot_dev : (i + 1) * slot_dev]
            total = total + lax.ppermute(block, "z", shifted(i * APART)).astype(jnp.float32)
        return total.astype(jnp.bfloat16)

    owner_node = node_ids[0] // (VOCAB // node_count)
    same_owner = owner_node[:, None] == owner_node[None, :]
    positions = lax.iota(jnp.int32, slot_dev)
    earlier = positions[None, :] < positions[:, None]
    rank_slot = jnp.sum((same_owner & earlier).astype(jnp.int32), axis=1)
    position_map = owner_map.reshape(node_count, capacity)

    def send_places(kinds, kind):
        return (owner_node * kinds + kind) * capacity + rank_slot

    def touched_places(kinds, kind):
        unused = jnp.full_like(position_map, -1)
        return jnp.concatenate(
            [position_map if i == kind else unused for i in range(kinds)], axis=1
        ).reshape(-1)

    def exchange(rows):
        return lax.all_to_all(
            rows.reshape(node_count, -1, rows.shape[1]),
            ("x", "y"),
            split_axis=0,
            concat_axis=0,
            tiled=True,
        ).reshape(rows.shape)

    def to_owners(kinds, kind):
        places = lax.iota(jnp.int32, node_count * kinds * capacity)
        return matches(places, send_places(kinds, kind))

    def to_listers(kinds, kind):
        return matches(touched_places(kinds, kind), lax.iota(jnp.int32, touch_cap))

    def at_owner(received, kinds, kind):
        collect = matches(lax.iota(jnp.int32, touch_cap), touched_places(kinds, kind))
        return dot32(collect, received)

    def at_lister(received, kinds, kind):
        places = lax.iota(jnp.int32, node_count * kinds * capacity)
        return dot32(matches(send_places(kinds, kind), places), received).astype(jnp.bfloat16)

    def update(gradient, columns):
        states = adam_rows(
            gradient,
            moment[:, columns],
            second[:, columns],
            master[:, columns],
            touched_ids >= 0,
        )
        return states[2].astype(jnp.bfloat16), states

    listed = jnp.concatenate([rows_here, rows_down, rows_up])
    own_tokens = matches(token_slot, listed)
    other_tokens = matches(other_slot, listed)

    def token_parts(rows):
        here = jnp.concatenate(
            [rows] + [lax.ppermute(rows, "z", shifted(-i * APART)) for i in range(1, GROUP)]
        )
        from_down = lax.ppermute(here, "z", shifted(1))
        from_up = lax.ppermute(here, "z", shifted(-1))
        gathered = jnp.concatenate([here, from_down, from_up])
        theirs = dot32(other_tokens, gathered).astype(jnp.bfloat16)
        return dot32(own_tokens, gathered).astype(jnp.bfloat16) + lax.ppermute(theirs, "c", SWAP)

    step = grads.shape[1] // CHUNKS
    cols_a, cols_b = (slice(i * step, (i + 1) * step) for i in range(CHUNKS))

    sum_a = node_sums(cols_a)
    sum_b = node_sums(cols_b)
    received_a = exchange(dot32(to_owners(1, 0), sum_a).astype(jnp.bfloat16))
    fresh_a, states_a = update(at_owner(received_a, 1, 0), cols_a)
    received_both = exchange(
        (dot32(to_listers(2, 0), fresh_a) + dot32(to_owners(2, 1), sum_b)).astype(jnp.bfloat16)
    )
    tokens_a = token_parts(at_lister(received_both, 2, 0))
    fresh_b, states_b = update(at_owner(received_both, 2, 1), cols_b)
    received_b = exchange(dot32(to_listers(1, 0), fresh_b).astype(jnp.bfloat16))
    tokens_b = token_parts(at_lister(received_b, 1, 0))

    moment_out, second_out, master_out = (
        jnp.concatenate(parts, axis=1) for parts in zip(states_a, states_b)
    )
    return jnp.concatenate([tokens_a, tokens_b], axis=1), moment_out, second_out, master_out


def solution(mesh):
    axes = ("x", "y", "z", "c")
    fine = Mesh(mesh.devices.reshape(X_SIZE, Y_SIZE, Z_SIZE, CORES), axes)
    rows = P(axes, None)
    return jax.shard_map(
        on_device,
        mesh=fine,
        in_specs=(
            rows,
            P(axes),
            P(("x", "y"), ("z", "c")),
            P(axes),
            P(axes, None, None),
            rows,
            rows,
            rows,
        ),
        out_specs=(rows, rows, rows, rows),
        check_vma=False,
    )
```

time: 208 us -> 211 us (1.014)
  starting transfers between devices: 59.1 us -> 138 us
  waiting for transfers between devices: 79.5 us -> 46.1 us
  blocking collectives: 32.1 us -> 0 us
  between operations: 15.8 us -> 1.31 us
  matrix products: 11.4 us -> 15.2 us
  local copies, waits for them, and re-layouts: 6.49 us -> 4.02 us
    ppermute x3 -> x23, starting transfers between devices: 26.3 us -> 99.7 us  [the longest x6 31.2 us: token_parts(): lax.ppermute(rows, 'z', shifted(-i * APART))]
    all_to_all x5 -> x3, waiting for transfers between devices: 78.9 us -> 17 us  [exchange(): lax.all_to_all(rows.reshape(node_count, -1, rows.shape[1]), ('x', 'y'), s...]
    all_gather x1 -> x0, blocking collectives: 32.1 us -> none  [on_device(): own_b = lax.all_gather(rows_b, 'z', axis=0, tiled=True)]
    ppermute x3 -> x23, waiting for transfers between devices: 0.14 us -> 29.2 us  [the longest x6 13.7 us: node_sums(): lax.ppermute(block, 'z', shifted(i * APART)).astype(jnp.float32)]
    ppermute x1, starting transfers between devices: 1.92 us -> 12.6 us  [on_device(): other_slot = lax.ppermute(token_slot, 'c', SWAP)]
    dot_general x11 -> x24, matrix products: 9.77 us -> 15.2 us  [dot32(): return jnp.dot(a, b, preferred_element_type=jnp.float32)]
    all_to_all x5 -> x3, starting transfers between devices: 30.9 us -> 26 us  [exchange(): lax.all_to_all(rows.reshape(node_count, -1, rows.shape[1]), ('x', 'y'), s...]
    slice x2, local copies, waits for them, and re-layouts: 2.3 us -> 0.04 us  [node_sums(): block = near[i * slot_dev:(i + 1) * slot_dev]]
  transfers between devices with their start and end apart: 11 -> 27, of which waited for: 6 -> 11; matrix products, arithmetic and copies ran while one was open for 7% -> 8% of each run, Pallas kernels for 0% -> 0%
where the time goes in v2:
time: 211 us; the launch traced here: 209 us
  starting transfers between devices  138 us (65%)
  waiting for transfers between devices  46.1 us (22%)
  matrix products  15.2 us (7%)
  other arithmetic  4.54 us (2%)
  local copies, waits for them, and re-layouts  4.02 us (2%)
    ppermute x6, starting transfers between devices, token_parts(): lax.ppermute(rows, 'z', shifted(-i * APART))  31.2 us
    ppermute x6, starting transfers between devices, node_sums(): lax.ppermute(block, 'z', shifted(i * APART)).astype(jnp.float32)  29 us
    all_to_all x3, starting transfers between devices, exchange(): lax.all_to_all(rows.reshape(node_count, -1, rows.shape[1]), ('x', 'y'), s...  26 us
    all_to_all x3, waiting for transfers between devices, exchange(): lax.all_to_all(rows.reshape(node_count, -1, rows.shape[1]), ('x', 'y'), s...  17 us
    dot_general x24, matrix products, dot32(): return jnp.dot(a, b, preferred_element_type=jnp.float32)  15.2 us
    ppermute x6, waiting for transfers between devices, node_sums(): lax.ppermute(block, 'z', shifted(i * APART)).astype(jnp.float32)  13.7 us
    ppermute x1, starting transfers between devices, on_device(): other_slot = lax.ppermute(token_slot, 'c', SWAP)  12.6 us
    ppermute x2, starting transfers between devices, token_parts(): lax.ppermute(theirs, 'c', SWAP)  10.6 us
  transfers between devices with their start and end apart: 27, of which 11 were waited for; matrix products, arithmetic and copies ran while one was open for 8% of the time, Pallas kernels for 0%

profile of v2, /device:TPU:1, one launch (start us, length us, event | category | flops | bytes accessed | tf_op | source)
XLA Modules:
  0.0 209.5 jit_solution(7672133521142085183)
XLA Ops:
  0.7 12.6 %collective-permute-start = (s32[128]{0:T(128)}, s32[128]{0:T(128)S(1)}, u32[]{:S(2)}, u32[]{:S(2)}) collective-permute-start(s32[128]{0:T(128)} %param.9), channel_id=1, source_target_pairs={{0,1},{1,0},{2,3},{3,2},{4,5},{5,4},{6,7},{7,6},{8,9},{9,8},{10,11... | collective-permute-start | bytes 1544 | tf_op jit(solution)/shard_map/ppermute | solution.py:61
  13.2 1.9 collective-permute-start.1
  16.5 2.3 %fusion.31 = f32[64,2688]{1,0:T(8,128)} fusion(bf16[128,5376]{1,0:T(8,128)(2,1)} %param.8, s32[128]{0:T(128)} %param.9, s32[64]{0:T(128)S(1)} %multiply_add_fusion.4), kind=kOutput, calls=%fused_computation.47 | convolution fusion | flops 44048384 | bytes 1377024 | tf_op jit(solution)/shard_map/dot_general | solution.py:49
  26.0 2.1 collective-permute-start.2
  28.4 5.4 %collective-permute-start.3 = (bf16[64,2688]{1,0:T(8,128)(2,1)S(1)}, bf16[64,2688]{1,0:T(8,128)(2,1)S(1)}, u32[]{:S(2)}, u32[]{:S(2)}) collective-permute-start(bf16[64,2688]{1,0:T(8,128)(2,1)S(1)} %fusion.9), channel_id=1, source_target_pairs={{0,22},{2,0},{4,2},{6,4},{8,6},{10,8},{12,10},{14,12},{16,14},{18,... | collective-permute-start | bytes 1032200 | tf_op jit(solution)/shard_map/ppermute | solution.py:78
  34.2 1.9 collective-permute-start.7
  36.4 4.6 %collective-permute-start.8 = (bf16[64,2688]{1,0:T(8,128)(2,1)S(1)}, bf16[64,2688]{1,0:T(8,128)(2,1)S(1)}, u32[]{:S(2)}, u32[]{:S(2)}) collective-permute-start(bf16[64,2688]{1,0:T(8,128)(2,1)S(1)} %fusion.16), channel_id=1, source_target_pairs={{0,22},{2,0},{4,2},{6,4},{8,6},{10,8},{12,10},{14,12},{16,14},{18,... | collective-permute-start | bytes 1032200 | tf_op jit(solution)/shard_map/ppermute | solution.py:78
  43.3 8.9 %collective-permute-start.5 = (bf16[16,2688]{1,0:T(8,128)(2,1)S(1)}, bf16[16,2688]{1,0:T(8,128)(2,1)S(1)}, u32[]{:S(2)}, u32[]{:S(2)}) collective-permute-start(bf16[16,2688]{1,0:T(8,128)(2,1)S(1)} %get-tuple-element.15), channel_id=1, source_target_pairs={{0,12},{2,14},{4,16},{6,18},{8,20},{10,22},{12,0},{14,2},{16,4},{1... | collective-permute-start | bytes 258056 | tf_op jit(solution)/shard_map/ppermute | solution.py:87
  52.2 2.8 %collective-permute-start.6 = (bf16[16,2688]{1,0:T(8,128)(2,1)S(1)}, bf16[16,2688]{1,0:T(8,128)(2,1)S(1)}, u32[]{:S(2)}, u32[]{:S(2)}) collective-permute-start(bf16[16,2688]{1,0:T(8,128)(2,1)S(1)} %get-tuple-element.14), channel_id=1, source_target_pairs={{0,18},{2,20},{4,22},{6,0},{8,2},{10,4},{12,6},{14,8},{16,10},{18,... | collective-permute-start | bytes 258056 | tf_op jit(solution)/shard_map/ppermute | solution.py:87
  55.3 2.3 %collective-permute-done.5 = bf16[16,2688]{1,0:T(8,128)(2,1)S(1)} collective-permute-done((bf16[16,2688]{1,0:T(8,128)(2,1)S(1)}, bf16[16,2688]{1,0:T(8,128)(2,1)S(1)}, u32[]{:S(2)}, u32[]{:S(2)}) %collective-permute-start.5) | collective-permute-done | bytes 86048 | tf_op jit(solution)/shard_map/ppermute | solution.py:87
  57.6 6.0 %collective-permute-done.6 = bf16[16,2688]{1,0:T(8,128)(2,1)S(1)} collective-permute-done((bf16[16,2688]{1,0:T(8,128)(2,1)S(1)}, bf16[16,2688]{1,0:T(8,128)(2,1)S(1)}, u32[]{:S(2)}, u32[]{:S(2)}) %collective-permute-start.6) | collective-permute-done | bytes 86048 | tf_op jit(solution)/shard_map/ppermute | solution.py:87
  64.7 9.4 %all-to-all-start = ((bf16[32,2,2688]{2,1,0:T(2,128)(2,1)}), bf16[32,2,2688]{2,1,0:T(2,128)(2,1)S(1)}, u32[]{:S(2)}, u32[]{:S(2)}) async-start(bf16[32,2,2688]{2,1,0:T(2,128)(2,1)} %reshape.125), calls=%async_computation | async-start | bytes 688128 | tf_op jit(solution)/shard_map/all_to_all | solution.py:107
  74.2 4.6 %collective-permute-start.10 = (bf16[16,2688]{1,0:T(8,128)(2,1)S(1)}, bf16[16,2688]{1,0:T(8,128)(2,1)S(1)}, u32[]{:S(2)}, u32[]{:S(2)}) collective-permute-start(bf16[16,2688]{1,0:T(8,128)(2,1)S(1)} %get-tuple-element.12), channel_id=1, source_target_pairs={{0,12},{2,14},{4,16},{6,18},{8,20},{10,22},{12,0},{14,2},{16,4},{1... | collective-permute-start | bytes 258056 | tf_op jit(solution)/shard_map/ppermute | solution.py:87
  78.8 6.0 %collective-permute-start.11 = (bf16[16,2688]{1,0:T(8,128)(2,1)S(1)}, bf16[16,2688]{1,0:T(8,128)(2,1)S(1)}, u32[]{:S(2)}, u32[]{:S(2)}) collective-permute-start(bf16[16,2688]{1,0:T(8,128)(2,1)S(1)} %get-tuple-element.11), channel_id=1, source_target_pairs={{0,18},{2,20},{4,22},{6,0},{8,2},{10,4},{12,6},{14,8},{16,10},{18,... | collective-permute-start | bytes 258056 | tf_op jit(solution)/shard_map/ppermute | solution.py:87
  84.8 4.9 %collective-permute-start.9 = (bf16[16,2688]{1,0:T(8,128)(2,1)S(1)}, bf16[16,2688]{1,0:T(8,128)(2,1)S(1)}, u32[]{:S(2)}, u32[]{:S(2)}) collective-permute-start(bf16[16,2688]{1,0:T(8,128)(2,1)S(1)} %get-tuple-element.10), channel_id=1, source_target_pairs={{0,6},{2,8},{4,10},{6,12},{8,14},{10,16},{12,18},{14,20},{16,22},{... | collective-permute-start | bytes 258056 | tf_op jit(solution)/shard_map/ppermute | solution.py:87
  90.5 4.7 %collective-permute-done.11 = bf16[16,2688]{1,0:T(8,128)(2,1)S(1)} collective-permute-done((bf16[16,2688]{1,0:T(8,128)(2,1)S(1)}, bf16[16,2688]{1,0:T(8,128)(2,1)S(1)}, u32[]{:S(2)}, u32[]{:S(2)}) %collective-permute-start.11) | collective-permute-done | bytes 86048 | tf_op jit(solution)/shard_map/ppermute | solution.py:87
  97.3 9.0 %all-to-all-start.1 = ((bf16[32,4,2688]{2,1,0:T(4,128)(2,1)}), bf16[32,4,2688]{2,1,0:T(4,128)(2,1)S(1)}, u32[]{:S(2)}, u32[]{:S(2)}) async-start(bf16[32,4,2688]{2,1,0:T(4,128)(2,1)} %reshape.127), calls=%async_computation.1 | async-start | bytes 1376256 | tf_op jit(solution)/shard_map/all_to_all | solution.py:107
  106.5 17.0 %all-to-all-done.1 = bf16[32,4,2688]{2,1,0:T(4,128)(2,1)S(1)} async-done(((bf16[32,4,2688]{2,1,0:T(4,128)(2,1)}), bf16[32,4,2688]{2,1,0:T(4,128)(2,1)S(1)}, u32[]{:S(2)}, u32[]{:S(2)}) %all-to-all-start.1) | async-done | bytes 688160 | tf_op jit(solution)/shard_map/all_to_all | solution.py:107
  123.9 7.0 %collective-permute-start.12 = (bf16[16,2688]{1,0:T(8,128)(2,1)S(1)}, bf16[16,2688]{1,0:T(8,128)(2,1)S(1)}, u32[]{:S(2)}, u32[]{:S(2)}) collective-permute-start(bf16[16,2688]{1,0:T(8,128)(2,1)S(1)} %get-tuple-element.25), channel_id=1, source_target_pairs={{0,18},{2,20},{4,22},{6,0},{8,2},{10,4},{12,6},{14,8},{16,10},{18,... | collective-permute-start | bytes 258056 | tf_op jit(solution)/shard_map/ppermute | solution.py:146
  130.9 5.2 %collective-permute-start.13 = (bf16[16,2688]{1,0:T(8,128)(2,1)S(1)}, bf16[16,2688]{1,0:T(8,128)(2,1)S(1)}, u32[]{:S(2)}, u32[]{:S(2)}) collective-permute-start(bf16[16,2688]{1,0:T(8,128)(2,1)S(1)} %get-tuple-element.25), channel_id=1, source_target_pairs={{0,12},{2,14},{4,16},{6,18},{8,20},{10,22},{12,0},{14,2},{16,4},{1... | collective-permute-start | bytes 258056 | tf_op jit(solution)/shard_map/ppermute | solution.py:146
  136.1 2.9 %collective-permute-start.14 = (bf16[16,2688]{1,0:T(8,128)(2,1)S(1)}, bf16[16,2688]{1,0:T(8,128)(2,1)S(1)}, u32[]{:S(2)}, u32[]{:S(2)}) collective-permute-start(bf16[16,2688]{1,0:T(8,128)(2,1)S(1)} %get-tuple-element.25), channel_id=1, source_target_pairs={{0,6},{2,8},{4,10},{6,12},{8,14},{10,16},{12,18},{14,20},{16,22},{... | collective-permute-start | bytes 258056 | tf_op jit(solution)/shard_map/ppermute | solution.py:146
  141.6 7.5 %all-to-all-start.2 = ((bf16[32,2,2688]{2,1,0:T(2,128)(2,1)}), bf16[32,2,2688]{2,1,0:T(2,128)(2,1)S(1)}, u32[]{:S(2)}, u32[]{:S(2)}) async-start(bf16[32,2,2688]{2,1,0:T(2,128)(2,1)} %reshape.129), calls=%async_computation.2 | async-start | bytes 688128 | tf_op jit(solution)/shard_map/all_to_all | solution.py:107
  150.1 1.9 collective-permute-start.15
  152.0 4.6 %collective-permute-start.16 = (bf16[64,2688]{1,0:T(8,128)(2,1)S(1)}, bf16[64,2688]{1,0:T(8,128)(2,1)S(1)}, u32[]{:S(2)}, u32[]{:S(2)}) collective-permute-start(bf16[64,2688]{1,0:T(8,128)(2,1)S(1)} %pad_maximum_fusion.1), channel_id=1, source_target_pairs={{0,22},{2,0},{4,2},{6,4},{8,6},{10,8},{12,10},{14,12},{16,14},{18,... | collective-permute-start | bytes 1032200 | tf_op jit(solution)/shard_map/ppermute | solution.py:149
  156.7 2.9 %collective-permute-done.15 = bf16[64,2688]{1,0:T(8,128)(2,1)S(1)} collective-permute-done((bf16[64,2688]{1,0:T(8,128)(2,1)S(1)}, bf16[64,2688]{1,0:T(8,128)(2,1)S(1)}, u32[]{:S(2)}, u32[]{:S(2)}) %collective-permute-start.15) | collective-permute-done | bytes 344096 | tf_op jit(solution)/shard_map/ppermute | solution.py:148
  161.2 6.1 %collective-permute-start.18 = (bf16[16,2688]{1,0:T(8,128)(2,1)S(1)}, bf16[16,2688]{1,0:T(8,128)(2,1)S(1)}, u32[]{:S(2)}, u32[]{:S(2)}) collective-permute-start(bf16[16,2688]{1,0:T(8,128)(2,1)S(1)} %get-tuple-element.23), channel_id=1, source_target_pairs={{0,18},{2,20},{4,22},{6,0},{8,2},{10,4},{12,6},{14,8},{16,10},{18,... | collective-permute-start | bytes 258056 | tf_op jit(solution)/shard_map/ppermute | solution.py:146
  167.3 8.0 %collective-permute-start.19 = (bf16[16,2688]{1,0:T(8,128)(2,1)S(1)}, bf16[16,2688]{1,0:T(8,128)(2,1)S(1)}, u32[]{:S(2)}, u32[]{:S(2)}) collective-permute-start(bf16[16,2688]{1,0:T(8,128)(2,1)S(1)} %get-tuple-element.23), channel_id=1, source_target_pairs={{0,12},{2,14},{4,16},{6,18},{8,20},{10,22},{12,0},{14,2},{16,4},{1... | collective-permute-start | bytes 258056 | tf_op jit(solution)/shard_map/ppermute | solution.py:146
  177.7 5.5 %collective-permute-start.17 = (bf16[128,2688]{1,0:T(8,128)(2,1)S(1)}, bf16[128,2688]{1,0:T(8,128)(2,1)S(1)}, u32[]{:S(2)}, u32[]{:S(2)}) collective-permute-start(bf16[128,2688]{1,0:T(8,128)(2,1)S(1)} %convolution_convert_fusion.2), channel_id=1, source_target_pairs={{0,1},{1,0},{2,3},{3,2},{4,5},{5,4},{6,7},{7,6},{8,9},{9,8},{10,11... | collective-permute-start | bytes 2064392 | tf_op jit(solution)/shard_map/ppermute | solution.py:152
  183.2 5.8 %collective-permute-done.20 = bf16[16,2688]{1,0:T(8,128)(2,1)S(1)} collective-permute-done((bf16[16,2688]{1,0:T(8,128)(2,1)S(1)}, bf16[16,2688]{1,0:T(8,128)(2,1)S(1)}, u32[]{:S(2)}, u32[]{:S(2)}) %collective-permute-start.20) | collective-permute-done | bytes 86048 | tf_op jit(solution)/shard_map/ppermute | solution.py:146
  190.9 4.6 %collective-permute-start.22 = (bf16[64,2688]{1,0:T(8,128)(2,1)S(1)}, bf16[64,2688]{1,0:T(8,128)(2,1)S(1)}, u32[]{:S(2)}, u32[]{:S(2)}) collective-permute-start(bf16[64,2688]{1,0:T(8,128)(2,1)S(1)} %pad_maximum_fusion.2), channel_id=1, source_target_pairs={{0,22},{2,0},{4,2},{6,4},{8,6},{10,8},{12,10},{14,12},{16,14},{18,... | collective-permute-start | bytes 1032200 | tf_op jit(solution)/shard_map/ppermute | solution.py:149
  195.6 4.1 %collective-permute-done.21 = bf16[64,2688]{1,0:T(8,128)(2,1)S(1)} collective-permute-done((bf16[64,2688]{1,0:T(8,128)(2,1)S(1)}, bf16[64,2688]{1,0:T(8,128)(2,1)S(1)}, u32[]{:S(2)}, u32[]{:S(2)}) %collective-permute-start.21) | collective-permute-done | bytes 344096 | tf_op jit(solution)/shard_map/ppermute | solution.py:148
  201.1 5.1 %collective-permute-start.23 = (bf16[128,2688]{1,0:T(8,128)(2,1)S(1)}, bf16[128,2688]{1,0:T(8,128)(2,1)S(1)}, u32[]{:S(2)}, u32[]{:S(2)}) collective-permute-start(bf16[128,2688]{1,0:T(8,128)(2,1)S(1)} %convolution_convert_fusion), channel_id=1, source_target_pairs={{0,1},{1,0},{2,3},{3,2},{4,5},{5,4},{6,7},{7,6},{8,9},{9,8},{10,11... | collective-permute-start | bytes 2064392 | tf_op jit(solution)/shard_map/ppermute | solution.py:152
  (109 shorter events, 30.6 us)
Async XLA Ops:
  0.6 18.2 %copy-start.5 = (s32[128]{0:T(128)S(1)}, s32[128]{0:T(128)}, u32[]{:S(2)}) copy-start(s32[128]{0:T(128)} %param.9) | copy-start | bytes 1540
  0.6 18.2 %copy-start = (bf16[128,5376]{1,0:T(8,128)(2,1)S(1)}, bf16[128,5376]{1,0:T(8,128)(2,1)}, u32[]{:S(2)}) copy-start(bf16[128,5376]{1,0:T(8,128)(2,1)} %param.8) | copy-start | bytes 4128772
  0.7 23.9 %collective-permute-start = (s32[128]{0:T(128)}, s32[128]{0:T(128)S(1)}, u32[]{:S(2)}, u32[]{:S(2)}) collective-permute-start(s32[128]{0:T(128)} %param.9), channel_id=1, source_target_pairs={{0,1},{1,0},{2,3},{3,2},{4,5},{5,4},{6,7},{7,6},{8,9},{9,8},{10,11... | collective-permute-start | bytes 1544 | tf_op jit(solution)/shard_map/ppermute | solution.py:61
  13.2 11.3 %collective-permute-start.1 = (bf16[128,5376]{1,0:T(8,128)(2,1)}, bf16[128,5376]{1,0:T(8,128)(2,1)S(1)}, u32[]{:S(2)}, u32[]{:S(2)}) collective-permute-start(bf16[128,5376]{1,0:T(8,128)(2,1)} %param.8), channel_id=1, source_target_pairs={{0,1},{1,0},{2,3},{3,2},{4,5},{5,4},{6,7},{7,6},{8,9},{9,8},{10,11... | collective-permute-start | bytes 4128776 | tf_op jit(solution)/shard_map/ppermute | solution.py:60
  26.0 15.0 %collective-permute-start.2 = (bf16[64,2688]{1,0:T(8,128)(2,1)S(1)}, bf16[64,2688]{1,0:T(8,128)(2,1)S(1)}, u32[]{:S(2)}, u32[]{:S(2)}) collective-permute-start(bf16[64,2688]{1,0:T(8,128)(2,1)S(1)} %fusion.8), channel_id=1, source_target_pairs={{0,2},{2,4},{4,6},{6,8},{8,10},{10,12},{12,14},{14,16},{16,18},{18... | collective-permute-start | bytes 1032200 | tf_op jit(solution)/shard_map/ppermute | solution.py:77
  28.4 12.6 %collective-permute-start.3 = (bf16[64,2688]{1,0:T(8,128)(2,1)S(1)}, bf16[64,2688]{1,0:T(8,128)(2,1)S(1)}, u32[]{:S(2)}, u32[]{:S(2)}) collective-permute-start(bf16[64,2688]{1,0:T(8,128)(2,1)S(1)} %fusion.9), channel_id=1, source_target_pairs={{0,22},{2,0},{4,2},{6,4},{8,6},{10,8},{12,10},{14,12},{16,14},{18,... | collective-permute-start | bytes 1032200 | tf_op jit(solution)/shard_map/ppermute | solution.py:78
  34.2 20.8 %collective-permute-start.7 = (bf16[64,2688]{1,0:T(8,128)(2,1)S(1)}, bf16[64,2688]{1,0:T(8,128)(2,1)S(1)}, u32[]{:S(2)}, u32[]{:S(2)}) collective-permute-start(bf16[64,2688]{1,0:T(8,128)(2,1)S(1)} %fusion.15), channel_id=1, source_target_pairs={{0,2},{2,4},{4,6},{6,8},{8,10},{10,12},{12,14},{14,16},{16,18},{18... | collective-permute-start | bytes 1032200 | tf_op jit(solution)/shard_map/ppermute | solution.py:77
  36.4 18.6 %collective-permute-start.8 = (bf16[64,2688]{1,0:T(8,128)(2,1)S(1)}, bf16[64,2688]{1,0:T(8,128)(2,1)S(1)}, u32[]{:S(2)}, u32[]{:S(2)}) collective-permute-start(bf16[64,2688]{1,0:T(8,128)(2,1)S(1)} %fusion.16), channel_id=1, source_target_pairs={{0,22},{2,0},{4,2},{6,4},{8,6},{10,8},{12,10},{14,12},{16,14},{18,... | collective-permute-start | bytes 1032200 | tf_op jit(solution)/shard_map/ppermute | solution.py:78
  41.4 13.9 %collective-permute-start.4 = (bf16[16,2688]{1,0:T(8,128)(2,1)S(1)}, bf16[16,2688]{1,0:T(8,128)(2,1)S(1)}, u32[]{:S(2)}, u32[]{:S(2)}) collective-permute-start(bf16[16,2688]{1,0:T(8,128)(2,1)S(1)} %get-tuple-element.13), channel_id=1, source_target_pairs={{0,6},{2,8},{4,10},{6,12},{8,14},{10,16},{12,18},{14,20},{16,22},{... | collective-permute-start | bytes 258056 | tf_op jit(solution)/shard_map/ppermute | solution.py:87
  43.3 14.3 %collective-permute-start.5 = (bf16[16,2688]{1,0:T(8,128)(2,1)S(1)}, bf16[16,2688]{1,0:T(8,128)(2,1)S(1)}, u32[]{:S(2)}, u32[]{:S(2)}) collective-permute-start(bf16[16,2688]{1,0:T(8,128)(2,1)S(1)} %get-tuple-element.15), channel_id=1, source_target_pairs={{0,12},{2,14},{4,16},{6,18},{8,20},{10,22},{12,0},{14,2},{16,4},{1... | collective-permute-start | bytes 258056 | tf_op jit(solution)/shard_map/ppermute | solution.py:87
  52.2 11.4 %collective-permute-start.6 = (bf16[16,2688]{1,0:T(8,128)(2,1)S(1)}, bf16[16,2688]{1,0:T(8,128)(2,1)S(1)}, u32[]{:S(2)}, u32[]{:S(2)}) collective-permute-start(bf16[16,2688]{1,0:T(8,128)(2,1)S(1)} %get-tuple-element.14), channel_id=1, source_target_pairs={{0,18},{2,20},{4,22},{6,0},{8,2},{10,4},{12,6},{14,8},{16,10},{18,... | collective-permute-start | bytes 258056 | tf_op jit(solution)/shard_map/ppermute | solution.py:87
  63.8 26.0 %copy-start.8 = (f32[16,5376]{1,0:T(8,128)S(1)}, f32[16,5376]{1,0:T(8,128)}, u32[]{:S(2)}) copy-start(f32[16,5376]{1,0:T(8,128)} %param.14) | copy-start | bytes 1032196
  63.8 26.0 %copy-start.9 = (f32[16,5376]{1,0:T(8,128)S(1)}, f32[16,5376]{1,0:T(8,128)}, u32[]{:S(2)}) copy-start(f32[16,5376]{1,0:T(8,128)} %param.13) | copy-start | bytes 1032196
  63.8 26.0 %copy-start.10 = (f32[16,5376]{1,0:T(8,128)S(1)}, f32[16,5376]{1,0:T(8,128)}, u32[]{:S(2)}) copy-start(f32[16,5376]{1,0:T(8,128)} %param.15) | copy-start | bytes 1032196
  64.7 25.0 %all-to-all-start = ((bf16[32,2,2688]{2,1,0:T(2,128)(2,1)}), bf16[32,2,2688]{2,1,0:T(2,128)(2,1)S(1)}, u32[]{:S(2)}, u32[]{:S(2)}) async-start(bf16[32,2,2688]{2,1,0:T(2,128)(2,1)} %reshape.125), calls=%async_computation | async-start | bytes 688128 | tf_op jit(solution)/shard_map/all_to_all | solution.py:107
  74.2 16.3 %collective-permute-start.10 = (bf16[16,2688]{1,0:T(8,128)(2,1)S(1)}, bf16[16,2688]{1,0:T(8,128)(2,1)S(1)}, u32[]{:S(2)}, u32[]{:S(2)}) collective-permute-start(bf16[16,2688]{1,0:T(8,128)(2,1)S(1)} %get-tuple-element.12), channel_id=1, source_target_pairs={{0,12},{2,14},{4,16},{6,18},{8,20},{10,22},{12,0},{14,2},{16,4},{1... | collective-permute-start | bytes 258056 | tf_op jit(solution)/shard_map/ppermute | solution.py:87
  78.8 16.5 %collective-permute-start.11 = (bf16[16,2688]{1,0:T(8,128)(2,1)S(1)}, bf16[16,2688]{1,0:T(8,128)(2,1)S(1)}, u32[]{:S(2)}, u32[]{:S(2)}) collective-permute-start(bf16[16,2688]{1,0:T(8,128)(2,1)S(1)} %get-tuple-element.11), channel_id=1, source_target_pairs={{0,18},{2,20},{4,22},{6,0},{8,2},{10,4},{12,6},{14,8},{16,10},{18,... | collective-permute-start | bytes 258056 | tf_op jit(solution)/shard_map/ppermute | solution.py:87
  84.8 11.2 %collective-permute-start.9 = (bf16[16,2688]{1,0:T(8,128)(2,1)S(1)}, bf16[16,2688]{1,0:T(8,128)(2,1)S(1)}, u32[]{:S(2)}, u32[]{:S(2)}) collective-permute-start(bf16[16,2688]{1,0:T(8,128)(2,1)S(1)} %get-tuple-element.10), channel_id=1, source_target_pairs={{0,6},{2,8},{4,10},{6,12},{8,14},{10,16},{12,18},{14,20},{16,22},{... | collective-permute-start | bytes 258056 | tf_op jit(solution)/shard_map/ppermute | solution.py:87
  97.3 26.2 %all-to-all-start.1 = ((bf16[32,4,2688]{2,1,0:T(4,128)(2,1)}), bf16[32,4,2688]{2,1,0:T(4,128)(2,1)S(1)}, u32[]{:S(2)}, u32[]{:S(2)}) async-start(bf16[32,4,2688]{2,1,0:T(4,128)(2,1)} %reshape.127), calls=%async_computation.1 | async-start | bytes 1376256 | tf_op jit(solution)/shard_map/all_to_all | solution.py:107
  123.9 26.2 %collective-permute-start.12 = (bf16[16,2688]{1,0:T(8,128)(2,1)S(1)}, bf16[16,2688]{1,0:T(8,128)(2,1)S(1)}, u32[]{:S(2)}, u32[]{:S(2)}) collective-permute-start(bf16[16,2688]{1,0:T(8,128)(2,1)S(1)} %get-tuple-element.25), channel_id=1, source_target_pairs={{0,18},{2,20},{4,22},{6,0},{8,2},{10,4},{12,6},{14,8},{16,10},{18,... | collective-permute-start | bytes 258056 | tf_op jit(solution)/shard_map/ppermute | solution.py:146
  130.9 19.1 %collective-permute-start.13 = (bf16[16,2688]{1,0:T(8,128)(2,1)S(1)}, bf16[16,2688]{1,0:T(8,128)(2,1)S(1)}, u32[]{:S(2)}, u32[]{:S(2)}) collective-permute-start(bf16[16,2688]{1,0:T(8,128)(2,1)S(1)} %get-tuple-element.25), channel_id=1, source_target_pairs={{0,12},{2,14},{4,16},{6,18},{8,20},{10,22},{12,0},{14,2},{16,4},{1... | collective-permute-start | bytes 258056 | tf_op jit(solution)/shard_map/ppermute | solution.py:146
  136.1 13.9 %collective-permute-start.14 = (bf16[16,2688]{1,0:T(8,128)(2,1)S(1)}, bf16[16,2688]{1,0:T(8,128)(2,1)S(1)}, u32[]{:S(2)}, u32[]{:S(2)}) collective-permute-start(bf16[16,2688]{1,0:T(8,128)(2,1)S(1)} %get-tuple-element.25), channel_id=1, source_target_pairs={{0,6},{2,8},{4,10},{6,12},{8,14},{10,16},{12,18},{14,20},{16,22},{... | collective-permute-start | bytes 258056 | tf_op jit(solution)/shard_map/ppermute | solution.py:146
  141.6 19.2 %all-to-all-start.2 = ((bf16[32,2,2688]{2,1,0:T(2,128)(2,1)}), bf16[32,2,2688]{2,1,0:T(2,128)(2,1)S(1)}, u32[]{:S(2)}, u32[]{:S(2)}) async-start(bf16[32,2,2688]{2,1,0:T(2,128)(2,1)} %reshape.129), calls=%async_computation.2 | async-start | bytes 688128 | tf_op jit(solution)/shard_map/all_to_all | solution.py:107
  150.1 9.5 %collective-permute-start.15 = (bf16[64,2688]{1,0:T(8,128)(2,1)S(1)}, bf16[64,2688]{1,0:T(8,128)(2,1)S(1)}, u32[]{:S(2)}, u32[]{:S(2)}) collective-permute-start(bf16[64,2688]{1,0:T(8,128)(2,1)S(1)} %pad_maximum_fusion.1), channel_id=1, source_target_pairs={{0,2},{2,4},{4,6},{6,8},{8,10},{10,12},{12,14},{14,16},{16,18},{18... | collective-permute-start | bytes 1032200 | tf_op jit(solution)/shard_map/ppermute | solution.py:148
  152.0 8.8 %collective-permute-start.16 = (bf16[64,2688]{1,0:T(8,128)(2,1)S(1)}, bf16[64,2688]{1,0:T(8,128)(2,1)S(1)}, u32[]{:S(2)}, u32[]{:S(2)}) collective-permute-start(bf16[64,2688]{1,0:T(8,128)(2,1)S(1)} %pad_maximum_fusion.1), channel_id=1, source_target_pairs={{0,22},{2,0},{4,2},{6,4},{8,6},{10,8},{12,10},{14,12},{16,14},{18,... | collective-permute-start | bytes 1032200 | tf_op jit(solution)/shard_map/ppermute | solution.py:149
  161.2 22.0 %collective-permute-start.18 = (bf16[16,2688]{1,0:T(8,128)(2,1)S(1)}, bf16[16,2688]{1,0:T(8,128)(2,1)S(1)}, u32[]{:S(2)}, u32[]{:S(2)}) collective-permute-start(bf16[16,2688]{1,0:T(8,128)(2,1)S(1)} %get-tuple-element.23), channel_id=1, source_target_pairs={{0,18},{2,20},{4,22},{6,0},{8,2},{10,4},{12,6},{14,8},{16,10},{18,... | collective-permute-start | bytes 258056 | tf_op jit(solution)/shard_map/ppermute | solution.py:146
  167.3 15.8 %collective-permute-start.19 = (bf16[16,2688]{1,0:T(8,128)(2,1)S(1)}, bf16[16,2688]{1,0:T(8,128)(2,1)S(1)}, u32[]{:S(2)}, u32[]{:S(2)}) collective-permute-start(bf16[16,2688]{1,0:T(8,128)(2,1)S(1)} %get-tuple-element.23), channel_id=1, source_target_pairs={{0,12},{2,14},{4,16},{6,18},{8,20},{10,22},{12,0},{14,2},{16,4},{1... | collective-permute-start | bytes 258056 | tf_op jit(solution)/shard_map/ppermute | solution.py:146
  175.3 13.7 %collective-permute-start.20 = (bf16[16,2688]{1,0:T(8,128)(2,1)S(1)}, bf16[16,2688]{1,0:T(8,128)(2,1)S(1)}, u32[]{:S(2)}, u32[]{:S(2)}) collective-permute-start(bf16[16,2688]{1,0:T(8,128)(2,1)S(1)} %get-tuple-element.23), channel_id=1, source_target_pairs={{0,6},{2,8},{4,10},{6,12},{8,14},{10,16},{12,18},{14,20},{16,22},{... | collective-permute-start | bytes 258056 | tf_op jit(solution)/shard_map/ppermute | solution.py:146
  177.7 29.2 %collective-permute-start.17 = (bf16[128,2688]{1,0:T(8,128)(2,1)S(1)}, bf16[128,2688]{1,0:T(8,128)(2,1)S(1)}, u32[]{:S(2)}, u32[]{:S(2)}) collective-permute-start(bf16[128,2688]{1,0:T(8,128)(2,1)S(1)} %convolution_convert_fusion.2), channel_id=1, source_target_pairs={{0,1},{1,0},{2,3},{3,2},{4,5},{5,4},{6,7},{7,6},{8,9},{9,8},{10,11... | collective-permute-start | bytes 2064392 | tf_op jit(solution)/shard_map/ppermute | solution.py:152
  189.0 10.7 %collective-permute-start.21 = (bf16[64,2688]{1,0:T(8,128)(2,1)S(1)}, bf16[64,2688]{1,0:T(8,128)(2,1)S(1)}, u32[]{:S(2)}, u32[]{:S(2)}) collective-permute-start(bf16[64,2688]{1,0:T(8,128)(2,1)S(1)} %pad_maximum_fusion.2), channel_id=1, source_target_pairs={{0,2},{2,4},{4,6},{6,8},{8,10},{10,12},{12,14},{14,16},{16,18},{18... | collective-permute-start | bytes 1032200 | tf_op jit(solution)/shard_map/ppermute | solution.py:148
  190.9 9.7 %collective-permute-start.22 = (bf16[64,2688]{1,0:T(8,128)(2,1)S(1)}, bf16[64,2688]{1,0:T(8,128)(2,1)S(1)}, u32[]{:S(2)}, u32[]{:S(2)}) collective-permute-start(bf16[64,2688]{1,0:T(8,128)(2,1)S(1)} %pad_maximum_fusion.2), channel_id=1, source_target_pairs={{0,22},{2,0},{4,2},{6,4},{8,6},{10,8},{12,10},{14,12},{16,14},{18,... | collective-permute-start | bytes 1032200 | tf_op jit(solution)/shard_map/ppermute | solution.py:149
  201.1 6.8 %collective-permute-start.23 = (bf16[128,2688]{1,0:T(8,128)(2,1)S(1)}, bf16[128,2688]{1,0:T(8,128)(2,1)S(1)}, u32[]{:S(2)}, u32[]{:S(2)}) collective-permute-start(bf16[128,2688]{1,0:T(8,128)(2,1)S(1)} %convolution_convert_fusion), channel_id=1, source_target_pairs={{0,1},{1,0},{2,3},{3,2},{4,5},{5,4},{6,7},{7,6},{8,9},{9,8},{10,11... | collective-permute-start | bytes 2064392 | tf_op jit(solution)/shard_map/ppermute | solution.py:152
  (7 other events, 47.0 us)

commit v3 on v1

v3 whole, which is shorter than its diff:
```python
import jax
import jax.numpy as jnp
from jax import lax
from jax.experimental import pallas as pl
from jax.experimental.pallas import tpu as pltpu
from jax.sharding import Mesh
from jax.sharding import PartitionSpec as P

VOCAB = 262144
STEP = 100


BETA_ONE = 0.9
BETA_TWO = 0.999
LEARN_RATE = 0.01
EPSILON = 1e-08

X_SIZE, Y_SIZE, Z_SIZE, CORES = 4, 8, 12, 2
APART = 3
GROUP = Z_SIZE // APART
GROUPS = [[r + APART * k for k in range(GROUP)] for r in range(APART)]
BLOCK_COLS = 896

SWAP = [(0, 1), (1, 0)]


def shifted(steps):
    return [(i, (i + steps) % Z_SIZE) for i in range(Z_SIZE)]


def adam_rows(gradient, moment, second, master, alive_rows):
    corr_one = 1.0 - BETA_ONE**STEP
    corr_two = 1.0 - BETA_TWO**STEP
    moment_new = BETA_ONE * moment + (1.0 - BETA_ONE) * gradient
    second_new = BETA_TWO * second + (1.0 - BETA_TWO) * gradient * gradient
    master_new = master - LEARN_RATE * (moment_new / corr_one) / (
        jnp.sqrt(second_new / corr_two) + EPSILON
    )
    kept = alive_rows[:, None]
    return (
        jnp.where(kept, moment_new, moment),
        jnp.where(kept, second_new, second),
        jnp.where(kept, master_new, master),
    )


def matches(rows, columns):
    return (rows[:, None] == columns[None, :]).astype(jnp.bfloat16)


def dot32(a, b):
    return jnp.dot(a, b, preferred_element_type=jnp.float32)


def sum_kernel(rows_ref, own_slot_ref, other_slot_ref, own_ref, other_ref, *out_refs):
    rows = rows_ref[...]
    total = dot32((rows == own_slot_ref[...]).astype(jnp.bfloat16), own_ref[...])
    total += dot32((rows == other_slot_ref[...]).astype(jnp.bfloat16), other_ref[...])
    part = total.shape[0] // len(out_refs)
    for i, out_ref in enumerate(out_refs):
        out_ref[...] = total[i * part : (i + 1) * part].astype(out_ref.dtype)


def slot_sums(rows, own_slot, other_slot, own, other, parts):
    tokens, width = own.shape
    whole = lambda shape: pl.BlockSpec(shape, lambda i: (0, 0))
    columns = lambda height: pl.BlockSpec((height, BLOCK_COLS), lambda i: (0, i))
    part = rows.shape[0] // parts
    return pl.pallas_call(
        sum_kernel,
        grid=(width // BLOCK_COLS,),
        in_specs=[
            whole((rows.shape[0], 1)),
            whole((1, tokens)),
            whole((1, tokens)),
            columns(tokens),
            columns(tokens),
        ],
        out_specs=[columns(part)] * parts,
        out_shape=[jax.ShapeDtypeStruct((part, width), jnp.bfloat16)] * parts,
        cost_estimate=pl.CostEstimate(
            flops=4 * rows.shape[0] * tokens * width,
            bytes_accessed=2 * (2 * tokens + rows.shape[0]) * width,
            transcendentals=0,
        ),
        compiler_params=pltpu.CompilerParams(vmem_limit_bytes=16 * 2**20),
    )(rows[:, None], own_slot[None, :], other_slot[None, :], own, other)


def on_device(grads, token_slot, node_ids, touched_ids, owner_map, moment, second, master):
    slot_dev = node_ids.shape[1]
    width = grads.shape[1]
    node_count = X_SIZE * Y_SIZE
    capacity = owner_map.shape[2]
    touch_cap = touched_ids.shape[0]
    core = lax.axis_index("c")
    place = lax.axis_index("z")

    other_slot = lax.ppermute(token_slot, "c", SWAP)
    other_grads = lax.ppermute(grads, "c", SWAP)

    def rows_of(shift):
        row = lax.iota(jnp.int32, GROUP * slot_dev)
        z_of_row = lax.div(row, slot_dev) * APART + lax.rem(place + (shift + APART), APART)
        return (z_of_row * CORES + core) * slot_dev + lax.rem(row, slot_dev)

    listed = jnp.concatenate([rows_of(0), rows_of(-1), rows_of(1)])

    kept, for_down, for_up = slot_sums(listed, token_slot, other_slot, grads, other_grads, 3)
    from_down = lax.ppermute(for_up, "z", shifted(1))
    from_up = lax.ppermute(for_down, "z", shifted(-1))
    near = (
        kept.astype(jnp.float32) + from_down.astype(jnp.float32) + from_up.astype(jnp.float32)
    ).astype(jnp.bfloat16)
    blocks = lax.all_to_all(
        near.reshape(GROUP, slot_dev, width),
        "z",
        split_axis=0,
        concat_axis=0,
        tiled=True,
        axis_index_groups=GROUPS,
    )
    node_sum = jnp.sum(blocks.astype(jnp.float32), axis=0).astype(jnp.bfloat16)

    owner_node = node_ids[0] // (VOCAB // node_count)
    same_owner = owner_node[:, None] == owner_node[None, :]
    positions = lax.iota(jnp.int32, slot_dev)
    earlier = positions[None, :] < positions[:, None]
    rank_slot = jnp.sum((same_owner & earlier).astype(jnp.int32), axis=1)
    send_slot = owner_node * capacity + rank_slot
    send_places = lax.iota(jnp.int32, node_count * capacity)
    touched_places = lax.iota(jnp.int32, touch_cap)
    position_map = owner_map.reshape(-1)

    def exchange(rows):
        return lax.all_to_all(
            rows.astype(jnp.bfloat16).reshape(node_count, capacity, width),
            ("x", "y"),
            split_axis=0,
            concat_axis=0,
            tiled=True,
        ).reshape(node_count * capacity, width)

    incoming = exchange(dot32(matches(send_places, send_slot), node_sum))
    gradient = dot32(matches(touched_places, position_map), incoming)
    moment_out, second_out, master_out = adam_rows(
        gradient, moment, second, master, touched_ids >= 0
    )
    fresh_rows = master_out.astype(jnp.bfloat16)
    returned = exchange(dot32(matches(position_map, touched_places), fresh_rows))
    rows = dot32(matches(send_slot, send_places), returned).astype(jnp.bfloat16)

    here = lax.all_gather(rows, "z", axis=0, tiled=True, axis_index_groups=GROUPS)
    from_down = lax.ppermute(here, "z", shifted(1))
    from_up = lax.ppermute(here, "z", shifted(-1))
    gathered = jnp.concatenate([here, from_down, from_up])
    theirs = dot32(matches(other_slot, listed), gathered).astype(jnp.bfloat16)
    mine = dot32(matches(token_slot, listed), gathered).astype(jnp.bfloat16)
    token_rows = mine + lax.ppermute(theirs, "c", SWAP)
    return token_rows, moment_out, second_out, master_out


def solution(mesh):
    axes = ("x", "y", "z", "c")
    fine = Mesh(mesh.devices.reshape(X_SIZE, Y_SIZE, Z_SIZE, CORES), axes)
    rows = P(axes, None)
    return jax.shard_map(
        on_device,
        mesh=fine,
        in_specs=(
            rows,
            P(axes),
            P(("x", "y"), ("z", "c")),
            P(axes),
            P(axes, None, None),
            rows,
            rows,
            rows,
        ),
        out_specs=(rows, rows, rows, rows),
        check_vma=False,
    )
```

time: 208 us -> 187 us (0.90)
  starting transfers between devices: 59.1 us -> 77.9 us
  between operations: 15.8 us -> 0.95 us
  blocking collectives: 32.1 us -> 20.6 us
  matrix products: 11.4 us -> 4.41 us
  waiting for transfers between devices: 79.5 us -> 73 us
  Pallas kernels: 0 us -> 2.76 us
    all_to_all x5 -> x3, waiting for transfers between devices: 78.9 us -> 42.8 us  [the longest x2 27.2 us: exchange(): lax.all_to_all(rows.astype(jnp.bfloat16).reshape(node_count, capacity, wi...]
    ppermute x3 -> x6, starting transfers between devices: 26.3 us -> 56.1 us  [the longest x1 17.7 us: on_device(): from_up = lax.ppermute(here, 'z', shifted(-1))]
    ppermute x3 -> x6, waiting for transfers between devices: 0.14 us -> 29.3 us  [the longest x1 13.7 us: on_device(): from_down = lax.ppermute(for_up, 'z', shifted(1))]
    all_gather x1, blocking collectives: 32.1 us -> 20.6 us  [on_device(): lax.all_gather(rows, 'z', axis=0, tiled=True, axis_index_groups=GROUPS)]
    all_to_all x5 -> x3, starting transfers between devices: 30.9 us -> 19.9 us  [the longest x2 14.4 us: exchange(): lax.all_to_all(rows.astype(jnp.bfloat16).reshape(node_count, capacity, wi...]
    dot_general x11 -> x6, matrix products: 9.77 us -> 4.41 us  [dot32(): return jnp.dot(a, b, preferred_element_type=jnp.float32)]
    pallas_call x0 -> x1, Pallas kernels: none -> 2.76 us  [slot_sums(): pl.pallas_call(sum_kernel, grid=(width // BLOCK_COLS,), in_specs=[whole((...]
    concatenate x3 -> x1, other arithmetic: 2.81 us -> 0.08 us  [on_device(): listed = jnp.concatenate([rows_of(0), rows_of(-1), rows_of(1)])]
  transfers between devices with their start and end apart: 11 -> 10, of which waited for: 6 -> 8; matrix products, arithmetic and copies ran while one was open for 7% -> 0% of each run, Pallas kernels for 0% -> 0%
where the time goes in v3:
time: 187 us
  starting transfers between devices  77.9 us (42%)
  waiting for transfers between devices  73 us (39%)
  blocking collectives  20.6 us (11%)
  local copies, waits for them, and re-layouts  5.22 us (3%)
  matrix products  4.41 us (2%)
  Pallas kernels  2.76 us (1%)
    all_to_all x2, waiting for transfers between devices, exchange(): lax.all_to_all(rows.astype(jnp.bfloat16).reshape(node_count, capacity, wi...  27.2 us
    all_gather x1, blocking collectives, on_device(): lax.all_gather(rows, 'z', axis=0, tiled=True, axis_index_groups=GROUPS)  20.6 us
    ppermute x1, starting transfers between devices, on_device(): from_up = lax.ppermute(here, 'z', shifted(-1))  17.7 us
    all_to_all x1, waiting for transfers between devices, on_device(): lax.all_to_all(near.reshape(GROUP, slot_dev, width), 'z', split_axis=0, c...  15.5 us
    all_to_all x2, starting transfers between devices, exchange(): lax.all_to_all(rows.astype(jnp.bfloat16).reshape(node_count, capacity, wi...  14.4 us
    ppermute x1, waiting for transfers between devices, on_device(): from_down = lax.ppermute(for_up, 'z', shifted(1))  13.7 us
    ppermute x1, starting transfers between devices, on_device(): other_grads = lax.ppermute(grads, 'c', SWAP)  12.4 us
    ppermute x1, waiting for transfers between devices, on_device(): from_down = lax.ppermute(here, 'z', shifted(1))  12 us
  transfers between devices with their start and end apart: 10, of which 8 were waited for; matrix products, arithmetic and copies ran while one was open for 0% of the time, Pallas kernels for 0%

profile of v3, /device:TPU:1, one launch (start us, length us, event | category | flops | bytes accessed | tf_op | source)
XLA Modules:
  0.0 186.5 jit_solution(6132124248788986605)
XLA Ops:
  0.6 12.4 %collective-permute-start.1 = (bf16[128,5376]{1,0:T(8,128)(2,1)}, bf16[128,5376]{1,0:T(8,128)(2,1)S(1)}, u32[]{:S(2)}, u32[]{:S(2)}) collective-permute-start(bf16[128,5376]{1,0:T(8,128)(2,1)} %own_ref.1), channel_id=1, source_target_pairs={{0,1},{1,0},{2,3},{3,2},{4,5},{5,4},{6,7},{7,6},{8,9},{9,8},{10,11... | collective-permute-start | bytes 4128776 | tf_op jit(solution)/shard_map/ppermute | solution.py:100
  13.1 1.9 %collective-permute-start = (s32[128]{0:T(128)}, s32[128]{0:T(128)S(1)}, u32[]{:S(2)}, u32[]{:S(2)}) collective-permute-start(s32[128]{0:T(128)} %param.9), channel_id=1, source_target_pairs={{0,1},{1,0},{2,3},{3,2},{4,5},{5,4},{6,7},{7,6},{8,9},{9,8},{10,11... | collective-permute-start | bytes 1544 | tf_op jit(solution)/shard_map/ppermute | solution.py:99
  15.3 1.0 collective-permute-done
  16.2 1.3 copy-done
  17.6 0.7 copy-done.1
  18.2 2.8 %shard_map.111 = (bf16[64,5376]{1,0:T(8,128)(2,1)S(1)}, bf16[64,5376]{1,0:T(8,128)(2,1)S(1)}, bf16[64,5376]{1,0:T(8,128)(2,1)S(1)}) custom-call(s32[192,1]{1,0:T(8,128)S(1)} %copy.16.rows_ref, s32[1,128]{1,0:T(1,128)S(1)} %bitcast.27, s32[1,128]{1,0:T(1,128)S(1)} %bitcast.28, bf16[128,5376]{1,0:T(8,128)(2,1)S(1)} %copy-done, ...), custom_call_target="tpu_custom_call" | custom-call | flops 528482304 | bytes 4816896 | tf_op jit(solution)/shard_map/pallas_call | solution.py:69
  21.0 1.9 %collective-permute-start.2 = (bf16[64,5376]{1,0:T(8,128)(2,1)S(1)}, bf16[64,5376]{1,0:T(8,128)(2,1)S(1)}, u32[]{:S(2)}, u32[]{:S(2)}) collective-permute-start(bf16[64,5376]{1,0:T(8,128)(2,1)S(1)} %get-tuple-element.8), channel_id=1, source_target_pairs={{0,2},{2,4},{4,6},{6,8},{8,10},{10,12},{12,14},{14,16},{16,18},{18... | collective-permute-start | bytes 2064392 | tf_op jit(solution)/shard_map/ppermute | solution.py:110
  22.9 5.3 %collective-permute-start.3 = (bf16[64,5376]{1,0:T(8,128)(2,1)S(1)}, bf16[64,5376]{1,0:T(8,128)(2,1)S(1)}, u32[]{:S(2)}, u32[]{:S(2)}) collective-permute-start(bf16[64,5376]{1,0:T(8,128)(2,1)S(1)} %get-tuple-element.9), channel_id=1, source_target_pairs={{0,22},{2,0},{4,2},{6,4},{8,6},{10,8},{12,10},{14,12},{16,14},{18,... | collective-permute-start | bytes 2064392 | tf_op jit(solution)/shard_map/ppermute | solution.py:111
  28.2 13.7 %collective-permute-done.2 = bf16[64,5376]{1,0:T(8,128)(2,1)S(1)} collective-permute-done((bf16[64,5376]{1,0:T(8,128)(2,1)S(1)}, bf16[64,5376]{1,0:T(8,128)(2,1)S(1)}, u32[]{:S(2)}, u32[]{:S(2)}) %collective-permute-start.2) | collective-permute-done | bytes 688160 | tf_op jit(solution)/shard_map/ppermute | solution.py:110
  41.9 0.9 collective-permute-done.3
  42.8 1.1 add_convert_fusion
  43.9 5.5 %all-to-all-start = ((bf16[4,16,5376]{2,1,0:T(8,128)(2,1)}), bf16[4,16,5376]{2,1,0:T(8,128)(2,1)S(1)}, u32[]{:S(2)}, u32[]{:S(2)}) async-start(bf16[4,16,5376]{2,1,0:T(8,128)(2,1)} %bitcast.7), calls=%async_computation | async-start | bytes 1376256 | tf_op jit(solution)/shard_map/all_to_all | solution.py:115
  49.7 15.5 %all-to-all-done = bf16[4,16,5376]{2,1,0:T(8,128)(2,1)S(1)} async-done(((bf16[4,16,5376]{2,1,0:T(8,128)(2,1)}), bf16[4,16,5376]{2,1,0:T(8,128)(2,1)S(1)}, u32[]{:S(2)}, u32[]{:S(2)}) %all-to-all-start) | async-done | bytes 688160 | tf_op jit(solution)/shard_map/all_to_all | solution.py:115
  65.4 0.3 convolution_convert_fusion.3
  65.7 1.1 reshape.72
  66.8 9.5 %all-to-all-start.1 = ((bf16[32,2,5376]{2,1,0:T(2,128)(2,1)}), bf16[32,2,5376]{2,1,0:T(2,128)(2,1)S(1)}, u32[]{:S(2)}, u32[]{:S(2)}) async-start(bf16[32,2,5376]{2,1,0:T(2,128)(2,1)} %reshape.72), calls=%async_computation.1 | async-start | bytes 1376256 | tf_op jit(solution)/shard_map/all_to_all | solution.py:136
  76.5 13.5 %all-to-all-done.1 = bf16[32,2,5376]{2,1,0:T(2,128)(2,1)S(1)} async-done(((bf16[32,2,5376]{2,1,0:T(2,128)(2,1)}), bf16[32,2,5376]{2,1,0:T(2,128)(2,1)S(1)}, u32[]{:S(2)}, u32[]{:S(2)}) %all-to-all-start.1) | async-done | bytes 688160 | tf_op jit(solution)/shard_map/all_to_all | solution.py:136
  90.0 0.3 reshape.73
  90.3 1.2 fusion.3
  91.5 0.4 convolution_convert_fusion.2
  91.9 1.1 reshape.74
  93.0 4.9 %all-to-all-start.2 = ((bf16[32,2,5376]{2,1,0:T(2,128)(2,1)}), bf16[32,2,5376]{2,1,0:T(2,128)(2,1)S(1)}, u32[]{:S(2)}, u32[]{:S(2)}) async-start(bf16[32,2,5376]{2,1,0:T(2,128)(2,1)} %reshape.74), calls=%async_computation.2 | async-start | bytes 1376256 | tf_op jit(solution)/shard_map/all_to_all | solution.py:136
  98.0 13.8 %all-to-all-done.2 = bf16[32,2,5376]{2,1,0:T(2,128)(2,1)S(1)} async-done(((bf16[32,2,5376]{2,1,0:T(2,128)(2,1)}), bf16[32,2,5376]{2,1,0:T(2,128)(2,1)S(1)}, u32[]{:S(2)}, u32[]{:S(2)}) %all-to-all-start.2) | async-done | bytes 688160 | tf_op jit(solution)/shard_map/all_to_all | solution.py:136
  112.0 0.3 convolution_convert_fusion.4
  112.3 20.6 %all_gather.3 = bf16[64,5376]{1,0:T(8,128)(2,1)S(1)} all-gather(bf16[16,5376]{1,0:T(8,128)(2,1)S(1)} %convolution_convert_fusion.4), channel_id=1, replica_groups={{0,6,12,18},{2,8,14,20},{4,10,16,22},{1,7,13,19},{3,9,15,21},{5,11,17,2..., dimensions={0}, use_global_device_ids=true | all-gather | bytes 860160 | tf_op jit(solution)/shard_map/all_gather | solution.py:153
  132.9 17.7 %collective-permute-start.5 = (bf16[64,5376]{1,0:T(8,128)(2,1)S(1)}, bf16[64,5376]{1,0:T(8,128)(2,1)S(1)}, u32[]{:S(2)}, u32[]{:S(2)}) collective-permute-start(bf16[64,5376]{1,0:T(8,128)(2,1)S(1)} %all_gather.3), channel_id=1, source_target_pairs={{0,22},{2,0},{4,2},{6,4},{8,6},{10,8},{12,10},{14,12},{16,14},{18,... | collective-permute-start | bytes 2064392 | tf_op jit(solution)/shard_map/ppermute | solution.py:155
  150.6 11.0 %collective-permute-start.4 = (bf16[64,5376]{1,0:T(8,128)(2,1)S(1)}, bf16[64,5376]{1,0:T(8,128)(2,1)S(1)}, u32[]{:S(2)}, u32[]{:S(2)}) collective-permute-start(bf16[64,5376]{1,0:T(8,128)(2,1)S(1)} %all_gather.3), channel_id=1, source_target_pairs={{0,2},{2,4},{4,6},{6,8},{8,10},{10,12},{12,14},{14,16},{16,18},{18... | collective-permute-start | bytes 2064392 | tf_op jit(solution)/shard_map/ppermute | solution.py:154
  161.7 12.0 %collective-permute-done.4 = bf16[64,5376]{1,0:T(8,128)(2,1)S(1)} collective-permute-done((bf16[64,5376]{1,0:T(8,128)(2,1)S(1)}, bf16[64,5376]{1,0:T(8,128)(2,1)S(1)}, u32[]{:S(2)}, u32[]{:S(2)}) %collective-permute-start.4) | collective-permute-done | bytes 688160 | tf_op jit(solution)/shard_map/ppermute | solution.py:154
  173.8 0.6 convolution_convert_fusion
  174.4 7.8 %collective-permute-start.6 = (bf16[128,5376]{1,0:T(8,128)(2,1)S(1)}, bf16[128,5376]{1,0:T(8,128)(2,1)S(1)}, u32[]{:S(2)}, u32[]{:S(2)}) collective-permute-start(bf16[128,5376]{1,0:T(8,128)(2,1)S(1)} %convolution_convert_fusion), channel_id=1, source_target_pairs={{0,1},{1,0},{2,3},{3,2},{4,5},{5,4},{6,7},{7,6},{8,9},{9,8},{10,11... | collective-permute-start | bytes 4128776 | tf_op jit(solution)/shard_map/ppermute | solution.py:159
  182.1 2.7 %collective-permute-done.6 = bf16[128,5376]{1,0:T(8,128)(2,1)S(1)} collective-permute-done((bf16[128,5376]{1,0:T(8,128)(2,1)S(1)}, bf16[128,5376]{1,0:T(8,128)(2,1)S(1)}, u32[]{:S(2)}, u32[]{:S(2)}) %collective-permute-start.6) | collective-permute-done | bytes 1376288 | tf_op jit(solution)/shard_map/ppermute | solution.py:159
  184.9 1.7 fusion
  (37 shorter events, 1.2 us)
Async XLA Ops:
  0.6 15.6 %collective-permute-start.1 = (bf16[128,5376]{1,0:T(8,128)(2,1)}, bf16[128,5376]{1,0:T(8,128)(2,1)S(1)}, u32[]{:S(2)}, u32[]{:S(2)}) collective-permute-start(bf16[128,5376]{1,0:T(8,128)(2,1)} %own_ref.1), channel_id=1, source_target_pairs={{0,1},{1,0},{2,3},{3,2},{4,5},{5,4},{6,7},{7,6},{8,9},{9,8},{10,11... | collective-permute-start | bytes 4128776 | tf_op jit(solution)/shard_map/ppermute | solution.py:100
  13.1 3.2 %collective-permute-start = (s32[128]{0:T(128)}, s32[128]{0:T(128)S(1)}, u32[]{:S(2)}, u32[]{:S(2)}) collective-permute-start(s32[128]{0:T(128)} %param.9), channel_id=1, source_target_pairs={{0,1},{1,0},{2,3},{3,2},{4,5},{5,4},{6,7},{7,6},{8,9},{9,8},{10,11... | collective-permute-start | bytes 1544 | tf_op jit(solution)/shard_map/ppermute | solution.py:99
  16.2 1.3 copy-start
  17.6 0.7 copy-start.1
  21.0 21.0 %collective-permute-start.2 = (bf16[64,5376]{1,0:T(8,128)(2,1)S(1)}, bf16[64,5376]{1,0:T(8,128)(2,1)S(1)}, u32[]{:S(2)}, u32[]{:S(2)}) collective-permute-start(bf16[64,5376]{1,0:T(8,128)(2,1)S(1)} %get-tuple-element.8), channel_id=1, source_target_pairs={{0,2},{2,4},{4,6},{6,8},{8,10},{10,12},{12,14},{14,16},{16,18},{18... | collective-permute-start | bytes 2064392 | tf_op jit(solution)/shard_map/ppermute | solution.py:110
  22.9 19.9 %collective-permute-start.3 = (bf16[64,5376]{1,0:T(8,128)(2,1)S(1)}, bf16[64,5376]{1,0:T(8,128)(2,1)S(1)}, u32[]{:S(2)}, u32[]{:S(2)}) collective-permute-start(bf16[64,5376]{1,0:T(8,128)(2,1)S(1)} %get-tuple-element.9), channel_id=1, source_target_pairs={{0,22},{2,0},{4,2},{6,4},{8,6},{10,8},{12,10},{14,12},{16,14},{18,... | collective-permute-start | bytes 2064392 | tf_op jit(solution)/shard_map/ppermute | solution.py:111
  42.8 6.7 %copy-start.9 = (s32[1,16]{1,0:T(1,128)S(1)}, s32[1,16]{1,0:T(1,128)}, u32[]{:S(2)}) copy-start(s32[1,16]{1,0:T(1,128)} %param.10) | copy-start | bytes 196
  43.9 21.3 %all-to-all-start = ((bf16[4,16,5376]{2,1,0:T(8,128)(2,1)}), bf16[4,16,5376]{2,1,0:T(8,128)(2,1)S(1)}, u32[]{:S(2)}, u32[]{:S(2)}) async-start(bf16[4,16,5376]{2,1,0:T(8,128)(2,1)} %bitcast.7), calls=%async_computation | async-start | bytes 1376256 | tf_op jit(solution)/shard_map/all_to_all | solution.py:115
  49.7 26.6 %copy-start.4 = (s32[1,32,2]{1,2,0:T(2,128)S(1)}, s32[1,32,2]{1,2,0:T(2,128)}, u32[]{:S(2)}) copy-start(s32[1,32,2]{1,2,0:T(2,128)} %param.12) | copy-start | bytes 772
  49.7 26.8 %copy-start.8 = (s32[16]{0:T(128)S(1)}, s32[16]{0:T(128)}, u32[]{:S(2)}) copy-start(s32[16]{0:T(128)} %param.11) | copy-start | bytes 196
  65.7 24.6 %copy-start.5 = (f32[16,5376]{1,0:T(8,128)S(1)}, f32[16,5376]{1,0:T(8,128)}, u32[]{:S(2)}) copy-start(f32[16,5376]{1,0:T(8,128)} %param.14) | copy-start | bytes 1032196
  65.7 24.6 %copy-start.6 = (f32[16,5376]{1,0:T(8,128)S(1)}, f32[16,5376]{1,0:T(8,128)}, u32[]{:S(2)}) copy-start(f32[16,5376]{1,0:T(8,128)} %param.15) | copy-start | bytes 1032196
  65.7 24.6 %copy-start.7 = (f32[16,5376]{1,0:T(8,128)S(1)}, f32[16,5376]{1,0:T(8,128)}, u32[]{:S(2)}) copy-start(f32[16,5376]{1,0:T(8,128)} %param.13) | copy-start | bytes 1032196
  66.8 23.2 %all-to-all-start.1 = ((bf16[32,2,5376]{2,1,0:T(2,128)(2,1)}), bf16[32,2,5376]{2,1,0:T(2,128)(2,1)S(1)}, u32[]{:S(2)}, u32[]{:S(2)}) async-start(bf16[32,2,5376]{2,1,0:T(2,128)(2,1)} %reshape.72), calls=%async_computation.1 | async-start | bytes 1376256 | tf_op jit(solution)/shard_map/all_to_all | solution.py:136
  91.5 20.5 %copy-start.3 = (f32[16,5376]{1,0:T(8,128)}, f32[16,5376]{1,0:T(8,128)S(1)}, u32[]{:S(2)}) copy-start(f32[16,5376]{1,0:T(8,128)S(1)} %get-tuple-element.11) | copy-start | bytes 1032196
  93.0 18.7 %all-to-all-start.2 = ((bf16[32,2,5376]{2,1,0:T(2,128)(2,1)}), bf16[32,2,5376]{2,1,0:T(2,128)(2,1)S(1)}, u32[]{:S(2)}, u32[]{:S(2)}) async-start(bf16[32,2,5376]{2,1,0:T(2,128)(2,1)} %reshape.74), calls=%async_computation.2 | async-start | bytes 1376256 | tf_op jit(solution)/shard_map/all_to_all | solution.py:136
  132.9 40.8 %collective-permute-start.5 = (bf16[64,5376]{1,0:T(8,128)(2,1)S(1)}, bf16[64,5376]{1,0:T(8,128)(2,1)S(1)}, u32[]{:S(2)}, u32[]{:S(2)}) collective-permute-start(bf16[64,5376]{1,0:T(8,128)(2,1)S(1)} %all_gather.3), channel_id=1, source_target_pairs={{0,22},{2,0},{4,2},{6,4},{8,6},{10,8},{12,10},{14,12},{16,14},{18,... | collective-permute-start | bytes 2064392 | tf_op jit(solution)/shard_map/ppermute | solution.py:155
  150.6 23.0 %collective-permute-start.4 = (bf16[64,5376]{1,0:T(8,128)(2,1)S(1)}, bf16[64,5376]{1,0:T(8,128)(2,1)S(1)}, u32[]{:S(2)}, u32[]{:S(2)}) collective-permute-start(bf16[64,5376]{1,0:T(8,128)(2,1)S(1)} %all_gather.3), channel_id=1, source_target_pairs={{0,2},{2,4},{4,6},{6,8},{8,10},{10,12},{12,14},{14,16},{16,18},{18... | collective-permute-start | bytes 2064392 | tf_op jit(solution)/shard_map/ppermute | solution.py:154
  173.8 11.1 %copy-start.2 = (s32[128]{0:T(128)S(1)}, s32[128]{0:T(128)}, u32[]{:S(2)}) copy-start(s32[128]{0:T(128)} %param.9) | copy-start | bytes 1540
  174.4 10.5 %collective-permute-start.6 = (bf16[128,5376]{1,0:T(8,128)(2,1)S(1)}, bf16[128,5376]{1,0:T(8,128)(2,1)S(1)}, u32[]{:S(2)}, u32[]{:S(2)}) collective-permute-start(bf16[128,5376]{1,0:T(8,128)(2,1)S(1)} %convolution_convert_fusion), channel_id=1, source_target_pairs={{0,1},{1,0},{2,3},{3,2},{4,5},{5,4},{6,7},{7,6},{8,9},{9,8},{10,11... | collective-permute-start | bytes 4128776 | tf_op jit(solution)/shard_map/ppermute | solution.py:159

commit v4 on v3

--- a/solution.py
+++ b/solution.py
@@ -24,8 +24,12 @@
 SWAP = [(0, 1), (1, 0)]
 
 
-def shifted(steps):
-    return [(i, (i + steps) % Z_SIZE) for i in range(Z_SIZE)]
+def neighbour(steps):
+    pairs = []
+    for z in range(Z_SIZE):
+        pairs.append((z * CORES, (z + steps) % Z_SIZE * CORES))
+        pairs.append((z * CORES + 1, (z - steps) % Z_SIZE * CORES + 1))
+    return pairs
 
 
 def adam_rows(gradient, moment, second, master, alive_rows):
@@ -52,39 +56,53 @@
     return jnp.dot(a, b, preferred_element_type=jnp.float32)
 
 
-def sum_kernel(rows_ref, own_slot_ref, other_slot_ref, own_ref, other_ref, *out_refs):
-    rows = rows_ref[...]
-    total = dot32((rows == own_slot_ref[...]).astype(jnp.bfloat16), own_ref[...])
-    total += dot32((rows == other_slot_ref[...]).astype(jnp.bfloat16), other_ref[...])
+def whole(shape):
+    return pl.BlockSpec(shape, lambda i: (0, 0))
+
+
+def columns(height):
+    return pl.BlockSpec((height, BLOCK_COLS), lambda i: (0, i))
+
+
+def own_kernel(rows_ref, slot_ref, tokens_ref, out_ref):
+    chosen = (rows_ref[...] == slot_ref[...]).astype(jnp.bfloat16)
+    out_ref[...] = dot32(chosen, tokens_ref[...])
+
+
+def both_kernel(rows_ref, slot_ref, tokens_ref, own_ref, *out_refs):
+    chosen = (rows_ref[...] == slot_ref[...]).astype(jnp.bfloat16)
+    total = own_ref[...] + dot32(chosen, tokens_ref[...])
     part = total.shape[0] // len(out_refs)
     for i, out_ref in enumerate(out_refs):
         out_ref[...] = total[i * part : (i + 1) * part].astype(out_ref.dtype)
 
 
-def slot_sums(rows, own_slot, other_slot, own, other, parts):
-    tokens, width = own.shape
-    whole = lambda shape: pl.BlockSpec(shape, lambda i: (0, 0))
-    columns = lambda height: pl.BlockSpec((height, BLOCK_COLS), lambda i: (0, i))
-    part = rows.shape[0] // parts
-    return pl.pallas_call(
-        sum_kernel,
+def slot_sums(rows, slots, tokens, own, parts):
+    height, count, width = rows.shape[0], tokens.shape[0], tokens.shape[1]
+    inputs = [rows[:, None], slots[None, :], tokens]
+    in_specs = [whole((height, 1)), whole((1, count)), columns(count)]
+    if own is None:
+        kernel, out = own_kernel, [jax.ShapeDtypeStruct((height, width), jnp.float32)]
+    else:
+        kernel, out = both_kernel, [
+            jax.ShapeDtypeStruct((height // parts, width), jnp.bfloat16) for _ in range(parts)
+        ]
+        inputs.append(own)
+        in_specs.append(columns(height))
+    results = pl.pallas_call(
+        kernel,
         grid=(width // BLOCK_COLS,),
-        in_specs=[
-            whole((rows.shape[0], 1)),
-            whole((1, tokens)),
-            whole((1, tokens)),
-            columns(tokens),
-            columns(tokens),
-        ],
-        out_specs=[columns(part)] * parts,
-        out_shape=[jax.ShapeDtypeStruct((part, width), jnp.bfloat16)] * parts,
+        in_specs=in_specs,
+        out_specs=[columns(shape.shape[0]) for shape in out],
+        out_shape=out,
         cost_estimate=pl.CostEstimate(
-            flops=4 * rows.shape[0] * tokens * width,
-            bytes_accessed=2 * (2 * tokens + rows.shape[0]) * width,
+            flops=2 * height * count * width,
+            bytes_accessed=(2 * count + 4 * height) * width,
             transcendentals=0,
         ),
         compiler_params=pltpu.CompilerParams(vmem_limit_bytes=16 * 2**20),
-    )(rows[:, None], own_slot[None, :], other_slot[None, :], own, other)
+    )(*inputs)
+    return results[0] if own is None else results
 
 
 def on_device(grads, token_slot, node_ids, touched_ids, owner_map, moment, second, master):
@@ -96,21 +114,25 @@
     core = lax.axis_index("c")
     place = lax.axis_index("z")
 
+    other_grads = lax.ppermute(grads, "c", SWAP)
     other_slot = lax.ppermute(token_slot, "c", SWAP)
-    other_grads = lax.ppermute(grads, "c", SWAP)
 
     def rows_of(shift):
         row = lax.iota(jnp.int32, GROUP * slot_dev)
         z_of_row = lax.div(row, slot_dev) * APART + lax.rem(place + (shift + APART), APART)
         return (z_of_row * CORES + core) * slot_dev + lax.rem(row, slot_dev)
 
-    listed = jnp.concatenate([rows_of(0), rows_of(-1), rows_of(1)])
-
-    kept, for_down, for_up = slot_sums(listed, token_slot, other_slot, grads, other_grads, 3)
-    from_down = lax.ppermute(for_up, "z", shifted(1))
-    from_up = lax.ppermute(for_down, "z", shifted(-1))
+    ahead = 1 - 2 * core
+    listed = jnp.concatenate([rows_of(0), rows_of(ahead), rows_of(-ahead)])
+
+    own_sums = slot_sums(listed, token_slot, grads, None, 1)
+    kept, for_ahead, for_behind = slot_sums(listed, other_slot, other_grads, own_sums, 3)
+    from_behind = lax.ppermute(for_ahead, ("z", "c"), neighbour(1))
+    from_ahead = lax.ppermute(for_behind, ("z", "c"), neighbour(-1))
     near = (
-        kept.astype(jnp.float32) + from_down.astype(jnp.float32) + from_up.astype(jnp.float32)
+        kept.astype(jnp.float32)
+        + from_behind.astype(jnp.float32)
+        + from_ahead.astype(jnp.float32)
     ).astype(jnp.bfloat16)
     blocks = lax.all_to_all(
         near.reshape(GROUP, slot_dev, width),
@@ -151,12 +173,12 @@
     rows = dot32(matches(send_slot, send_places), returned).astype(jnp.bfloat16)
 
     here = lax.all_gather(rows, "z", axis=0, tiled=True, axis_index_groups=GROUPS)
-    from_down = lax.ppermute(here, "z", shifted(1))
-    from_up = lax.ppermute(here, "z", shifted(-1))
-    gathered = jnp.concatenate([here, from_down, from_up])
+    from_behind = lax.ppermute(here, ("z", "c"), neighbour(1))
+    from_ahead = lax.ppermute(here, ("z", "c"), neighbour(-1))
+    gathered = jnp.concatenate([here, from_ahead, from_behind])
     theirs = dot32(matches(other_slot, listed), gathered).astype(jnp.bfloat16)
     mine = dot32(matches(token_slot, listed), gathered).astype(jnp.bfloat16)
-    token_rows = mine + lax.ppermute(theirs, "c", SWAP)
+    token_rows = lax.optimization_barrier(mine) + lax.ppermute(theirs, "c", SWAP)
     return token_rows, moment_out, second_out, master_out
 
 

time: 187 us -> 187 us (level)
  waiting for transfers between devices: 73 us -> 79.6 us
  starting transfers between devices: 77.9 us -> 72.1 us
  blocking collectives: 20.6 us -> 17 us
    ppermute x5, waiting for transfers between devices: 29.3 us -> 34.7 us  [the longest x1 11.1 us: on_device(): from_behind = lax.ppermute(here, ('z', 'c'), neighbour(1))]
    ppermute x5, starting transfers between devices: 43.7 us -> 39.6 us  [the longest x1 23.7 us: on_device(): from_ahead = lax.ppermute(here, ('z', 'c'), neighbour(-1))]
    all_gather x1, blocking collectives: 20.6 us -> 17 us  [on_device(): lax.all_gather(rows, 'z', axis=0, tiled=True, axis_index_groups=GROUPS)]
    all_to_all x1, starting transfers between devices: 5.54 us -> 3.56 us  [on_device(): lax.all_to_all(near.reshape(GROUP, slot_dev, width), 'z', split_axis=0, c...]
    pallas_call x1 -> x2, Pallas kernels: 2.76 us -> 4.61 us  [slot_sums(): pl.pallas_call(kernel, grid=(width // BLOCK_COLS,), in_specs=in_specs, ou...]
  transfers between devices with their start and end apart: 10 -> 10, of which waited for: 8 -> 8; matrix products, arithmetic and copies ran while one was open for 0% -> 1% of each run, Pallas kernels for 0% -> 1%
where the time goes in v4:
time: 187 us; the launch traced here: 186 us
  waiting for transfers between devices  79.6 us (43%)
  starting transfers between devices  72.1 us (39%)
  blocking collectives  17 us (9%)
  local copies, waits for them, and re-layouts  5.22 us (3%)
  Pallas kernels  4.61 us (2%)
  matrix products  3.33 us (2%)
  other arithmetic  2.95 us (2%)
    all_to_all x2, waiting for transfers between devices, exchange(): lax.all_to_all(rows.astype(jnp.bfloat16).reshape(node_count, capacity, wi...  28.9 us
    ppermute x1, starting transfers between devices, on_device(): from_ahead = lax.ppermute(here, ('z', 'c'), neighbour(-1))  23.7 us
    all_gather x1, blocking collectives, on_device(): lax.all_gather(rows, 'z', axis=0, tiled=True, axis_index_groups=GROUPS)  17 us
    all_to_all x1, waiting for transfers between devices, on_device(): lax.all_to_all(near.reshape(GROUP, slot_dev, width), 'z', split_axis=0, c...  15.9 us
    all_to_all x2, starting transfers between devices, exchange(): lax.all_to_all(rows.astype(jnp.bfloat16).reshape(node_count, capacity, wi...  14.6 us
    ppermute x1, starting transfers between devices, on_device(): other_grads = lax.ppermute(grads, 'c', SWAP)  12.4 us
    ppermute x1, waiting for transfers between devices, on_device(): from_behind = lax.ppermute(here, ('z', 'c'), neighbour(1))  11.1 us
    ppermute x1, waiting for transfers between devices, on_device(): from_behind = lax.ppermute(for_ahead, ('z', 'c'), neighbour(1))  10.4 us
  transfers between devices with their start and end apart: 10, of which 8 were waited for; matrix products, arithmetic and copies ran while one was open for 1% of the time, Pallas kernels for 1%

profile of v4, /device:TPU:1, one launch (start us, length us, event | category | flops | bytes accessed | tf_op | source)
XLA Modules:
  0.0 185.8 jit_solution(2302372560893676117)
XLA Ops:
  0.6 12.4 %collective-permute-start.1 = (bf16[128,5376]{1,0:T(8,128)(2,1)}, bf16[128,5376]{1,0:T(8,128)(2,1)S(1)}, u32[]{:S(2)}, u32[]{:S(2)}) collective-permute-start(bf16[128,5376]{1,0:T(8,128)(2,1)} %tokens_ref.1), channel_id=1, source_target_pairs={{0,1},{1,0},{2,3},{3,2},{4,5},{5,4},{6,7},{7,6},{8,9},{9,8},{10,11... | collective-permute-start | bytes 4128776 | tf_op jit(solution)/shard_map/ppermute | solution.py:117
  13.1 1.9 %collective-permute-start = (s32[128]{0:T(128)}, s32[128]{0:T(128)S(1)}, u32[]{:S(2)}, u32[]{:S(2)}) collective-permute-start(s32[128]{0:T(128)} %param.9), channel_id=1, source_target_pairs={{0,1},{1,0},{2,3},{3,2},{4,5},{5,4},{6,7},{7,6},{8,9},{9,8},{10,11... | collective-permute-start | bytes 1544 | tf_op jit(solution)/shard_map/ppermute | solution.py:118
  15.3 1.3 copy-done
  16.6 0.7 copy-done.1
  17.3 2.2 %shard_map.111.own_ref = f32[192,5376]{1,0:T(8,128)S(1)} custom-call(s32[192,1]{1,0:T(8,128)S(1)} %copy.18.rows_ref, s32[1,128]{1,0:T(1,128)S(1)} %bitcast.27, bf16[128,5376]{1,0:T(8,128)(2,1)S(1)} %copy-done), custom_call_target="tpu_custom_call" | custom-call | flops 264241152 | bytes 5505024 | tf_op jit(solution)/shard_map/pallas_call | solution.py:92
  19.5 2.4 %shard_map.112 = (bf16[64,5376]{1,0:T(8,128)(2,1)S(1)}, bf16[64,5376]{1,0:T(8,128)(2,1)S(1)}, bf16[64,5376]{1,0:T(8,128)(2,1)S(1)}) custom-call(s32[192,1]{1,0:T(8,128)S(1)} %copy.18.rows_ref, s32[1,128]{1,0:T(1,128)S(1)} %bitcast.28, bf16[128,5376]{1,0:T(8,128)(2,1)S(1)} %collective-permute-done.1.tokens_ref, f32[192,5376]{1,0:T(8,128)S(1)} %shard_map.111.own_ref), custom_call_target="tpu_custom_call" | custom-call | flops 264241152 | bytes 5505024 | tf_op jit(solution)/shard_map/pallas_call | solution.py:92
  21.9 5.3 %collective-permute-start.2 = (bf16[64,5376]{1,0:T(8,128)(2,1)S(1)}, bf16[64,5376]{1,0:T(8,128)(2,1)S(1)}, u32[]{:S(2)}, u32[]{:S(2)}) collective-permute-start(bf16[64,5376]{1,0:T(8,128)(2,1)S(1)} %get-tuple-element.8), channel_id=1, source_target_pairs={{0,2},{1,23},{2,4},{3,1},{4,6},{5,3},{6,8},{7,5},{8,10},{9,7},{10,... | collective-permute-start | bytes 2064392 | tf_op jit(solution)/shard_map/ppermute | solution.py:130
  27.2 1.9 %collective-permute-start.3 = (bf16[64,5376]{1,0:T(8,128)(2,1)S(1)}, bf16[64,5376]{1,0:T(8,128)(2,1)S(1)}, u32[]{:S(2)}, u32[]{:S(2)}) collective-permute-start(bf16[64,5376]{1,0:T(8,128)(2,1)S(1)} %get-tuple-element.9), channel_id=1, source_target_pairs={{0,22},{1,3},{2,0},{3,5},{4,2},{5,7},{6,4},{7,9},{8,6},{9,11},{10,... | collective-permute-start | bytes 2064392 | tf_op jit(solution)/shard_map/ppermute | solution.py:131
  29.1 10.4 %collective-permute-done.2 = bf16[64,5376]{1,0:T(8,128)(2,1)S(1)} collective-permute-done((bf16[64,5376]{1,0:T(8,128)(2,1)S(1)}, bf16[64,5376]{1,0:T(8,128)(2,1)S(1)}, u32[]{:S(2)}, u32[]{:S(2)}) %collective-permute-start.2) | collective-permute-done | bytes 688160 | tf_op jit(solution)/shard_map/ppermute | solution.py:130
  39.5 4.1 %collective-permute-done.3 = bf16[64,5376]{1,0:T(8,128)(2,1)S(1)} collective-permute-done((bf16[64,5376]{1,0:T(8,128)(2,1)S(1)}, bf16[64,5376]{1,0:T(8,128)(2,1)S(1)}, u32[]{:S(2)}, u32[]{:S(2)}) %collective-permute-start.3) | collective-permute-done | bytes 688160 | tf_op jit(solution)/shard_map/ppermute | solution.py:131
  43.6 1.1 add_convert_fusion
  44.7 3.6 %all-to-all-start = ((bf16[4,16,5376]{2,1,0:T(8,128)(2,1)}), bf16[4,16,5376]{2,1,0:T(8,128)(2,1)S(1)}, u32[]{:S(2)}, u32[]{:S(2)}) async-start(bf16[4,16,5376]{2,1,0:T(8,128)(2,1)} %bitcast.7), calls=%async_computation | async-start | bytes 1376256 | tf_op jit(solution)/shard_map/all_to_all | solution.py:137
  48.5 15.9 %all-to-all-done = bf16[4,16,5376]{2,1,0:T(8,128)(2,1)S(1)} async-done(((bf16[4,16,5376]{2,1,0:T(8,128)(2,1)}), bf16[4,16,5376]{2,1,0:T(8,128)(2,1)S(1)}, u32[]{:S(2)}, u32[]{:S(2)}) %all-to-all-start) | async-done | bytes 688160 | tf_op jit(solution)/shard_map/all_to_all | solution.py:137
  64.6 0.3 convolution_convert_fusion.3
  64.9 1.1 reshape.72
  66.0 9.7 %all-to-all-start.1 = ((bf16[32,2,5376]{2,1,0:T(2,128)(2,1)}), bf16[32,2,5376]{2,1,0:T(2,128)(2,1)S(1)}, u32[]{:S(2)}, u32[]{:S(2)}) async-start(bf16[32,2,5376]{2,1,0:T(2,128)(2,1)} %reshape.72), calls=%async_computation.1 | async-start | bytes 1376256 | tf_op jit(solution)/shard_map/all_to_all | solution.py:158
  75.9 13.5 %all-to-all-done.1 = bf16[32,2,5376]{2,1,0:T(2,128)(2,1)S(1)} async-done(((bf16[32,2,5376]{2,1,0:T(2,128)(2,1)}), bf16[32,2,5376]{2,1,0:T(2,128)(2,1)S(1)}, u32[]{:S(2)}, u32[]{:S(2)}) %all-to-all-start.1) | async-done | bytes 688160 | tf_op jit(solution)/shard_map/all_to_all | solution.py:158
  89.7 1.2 fusion.2
  90.9 0.4 convolution_convert_fusion.2
  91.3 1.1 reshape.74
  92.4 4.9 %all-to-all-start.2 = ((bf16[32,2,5376]{2,1,0:T(2,128)(2,1)}), bf16[32,2,5376]{2,1,0:T(2,128)(2,1)S(1)}, u32[]{:S(2)}, u32[]{:S(2)}) async-start(bf16[32,2,5376]{2,1,0:T(2,128)(2,1)} %reshape.74), calls=%async_computation.2 | async-start | bytes 1376256 | tf_op jit(solution)/shard_map/all_to_all | solution.py:158
  97.4 15.5 %all-to-all-done.2 = bf16[32,2,5376]{2,1,0:T(2,128)(2,1)S(1)} async-done(((bf16[32,2,5376]{2,1,0:T(2,128)(2,1)}), bf16[32,2,5376]{2,1,0:T(2,128)(2,1)S(1)}, u32[]{:S(2)}, u32[]{:S(2)}) %all-to-all-start.2) | async-done | bytes 688160 | tf_op jit(solution)/shard_map/all_to_all | solution.py:158
  113.4 17.0 %all_gather.3 = bf16[64,5376]{1,0:T(8,128)(2,1)S(1)} all-gather(bf16[16,5376]{1,0:T(8,128)(2,1)S(1)} %convolution_convert_fusion.4), channel_id=1, replica_groups={{0,6,12,18},{2,8,14,20},{4,10,16,22},{1,7,13,19},{3,9,15,21},{5,11,17,2..., dimensions={0}, use_global_device_ids=true | all-gather | bytes 860160 | tf_op jit(solution)/shard_map/all_gather | solution.py:175
  130.4 23.7 %collective-permute-start.4 = (bf16[64,5376]{1,0:T(8,128)(2,1)S(1)}, bf16[64,5376]{1,0:T(8,128)(2,1)S(1)}, u32[]{:S(2)}, u32[]{:S(2)}) collective-permute-start(bf16[64,5376]{1,0:T(8,128)(2,1)S(1)} %all_gather.3), channel_id=1, source_target_pairs={{0,22},{1,3},{2,0},{3,5},{4,2},{5,7},{6,4},{7,9},{8,6},{9,11},{10,... | collective-permute-start | bytes 2064392 | tf_op jit(solution)/shard_map/ppermute | solution.py:177
  154.1 4.9 %collective-permute-start.5 = (bf16[64,5376]{1,0:T(8,128)(2,1)S(1)}, bf16[64,5376]{1,0:T(8,128)(2,1)S(1)}, u32[]{:S(2)}, u32[]{:S(2)}) collective-permute-start(bf16[64,5376]{1,0:T(8,128)(2,1)S(1)} %all_gather.3), channel_id=1, source_target_pairs={{0,2},{1,23},{2,4},{3,1},{4,6},{5,3},{6,8},{7,5},{8,10},{9,7},{10,... | collective-permute-start | bytes 2064392 | tf_op jit(solution)/shard_map/ppermute | solution.py:176
  159.1 7.0 %collective-permute-done.4 = bf16[64,5376]{1,0:T(8,128)(2,1)S(1)} collective-permute-done((bf16[64,5376]{1,0:T(8,128)(2,1)S(1)}, bf16[64,5376]{1,0:T(8,128)(2,1)S(1)}, u32[]{:S(2)}, u32[]{:S(2)}) %collective-permute-start.4) | collective-permute-done | bytes 688160 | tf_op jit(solution)/shard_map/ppermute | solution.py:177
  166.2 11.1 %collective-permute-done.5 = bf16[64,5376]{1,0:T(8,128)(2,1)S(1)} collective-permute-done((bf16[64,5376]{1,0:T(8,128)(2,1)S(1)}, bf16[64,5376]{1,0:T(8,128)(2,1)S(1)}, u32[]{:S(2)}, u32[]{:S(2)}) %collective-permute-start.5) | collective-permute-done | bytes 688160 | tf_op jit(solution)/shard_map/ppermute | solution.py:176
  177.3 0.6 convolution_convert_fusion
  177.9 3.7 %collective-permute-start.6 = (bf16[128,5376]{1,0:T(8,128)(2,1)S(1)}, bf16[128,5376]{1,0:T(8,128)(2,1)S(1)}, u32[]{:S(2)}, u32[]{:S(2)}) collective-permute-start(bf16[128,5376]{1,0:T(8,128)(2,1)S(1)} %convolution_convert_fusion), channel_id=1, source_target_pairs={{0,1},{1,0},{2,3},{3,2},{4,5},{5,4},{6,7},{7,6},{8,9},{9,8},{10,11... | collective-permute-start | bytes 4128776 | tf_op jit(solution)/shard_map/ppermute | solution.py:181
  181.7 0.6 convolution_convert_fusion.1
  182.2 2.1 %collective-permute-done.6 = bf16[128,5376]{1,0:T(8,128)(2,1)S(1)} collective-permute-done((bf16[128,5376]{1,0:T(8,128)(2,1)S(1)}, bf16[128,5376]{1,0:T(8,128)(2,1)S(1)}, u32[]{:S(2)}, u32[]{:S(2)}) %collective-permute-start.6) | collective-permute-done | bytes 1376288 | tf_op jit(solution)/shard_map/ppermute | solution.py:181
  184.4 1.4 add.124
  (39 shorter events, 1.7 us)
Async XLA Ops:
  0.6 18.8 %collective-permute-start.1 = (bf16[128,5376]{1,0:T(8,128)(2,1)}, bf16[128,5376]{1,0:T(8,128)(2,1)S(1)}, u32[]{:S(2)}, u32[]{:S(2)}) collective-permute-start(bf16[128,5376]{1,0:T(8,128)(2,1)} %tokens_ref.1), channel_id=1, source_target_pairs={{0,1},{1,0},{2,3},{3,2},{4,5},{5,4},{6,7},{7,6},{8,9},{9,8},{10,11... | collective-permute-start | bytes 4128776 | tf_op jit(solution)/shard_map/ppermute | solution.py:117
  13.1 6.4 %collective-permute-start = (s32[128]{0:T(128)}, s32[128]{0:T(128)S(1)}, u32[]{:S(2)}, u32[]{:S(2)}) collective-permute-start(s32[128]{0:T(128)} %param.9), channel_id=1, source_target_pairs={{0,1},{1,0},{2,3},{3,2},{4,5},{5,4},{6,7},{7,6},{8,9},{9,8},{10,11... | collective-permute-start | bytes 1544 | tf_op jit(solution)/shard_map/ppermute | solution.py:118
  15.3 1.3 copy-start
  16.6 0.7 copy-start.1
  21.9 17.6 %collective-permute-start.2 = (bf16[64,5376]{1,0:T(8,128)(2,1)S(1)}, bf16[64,5376]{1,0:T(8,128)(2,1)S(1)}, u32[]{:S(2)}, u32[]{:S(2)}) collective-permute-start(bf16[64,5376]{1,0:T(8,128)(2,1)S(1)} %get-tuple-element.8), channel_id=1, source_target_pairs={{0,2},{1,23},{2,4},{3,1},{4,6},{5,3},{6,8},{7,5},{8,10},{9,7},{10,... | collective-permute-start | bytes 2064392 | tf_op jit(solution)/shard_map/ppermute | solution.py:130
  27.2 16.4 %collective-permute-start.3 = (bf16[64,5376]{1,0:T(8,128)(2,1)S(1)}, bf16[64,5376]{1,0:T(8,128)(2,1)S(1)}, u32[]{:S(2)}, u32[]{:S(2)}) collective-permute-start(bf16[64,5376]{1,0:T(8,128)(2,1)S(1)} %get-tuple-element.9), channel_id=1, source_target_pairs={{0,22},{1,3},{2,0},{3,5},{4,2},{5,7},{6,4},{7,9},{8,6},{9,11},{10,... | collective-permute-start | bytes 2064392 | tf_op jit(solution)/shard_map/ppermute | solution.py:131
  43.6 4.7 %copy-start.9 = (s32[1,16]{1,0:T(1,128)S(1)}, s32[1,16]{1,0:T(1,128)}, u32[]{:S(2)}) copy-start(s32[1,16]{1,0:T(1,128)} %param.10) | copy-start | bytes 196
  44.7 19.8 %all-to-all-start = ((bf16[4,16,5376]{2,1,0:T(8,128)(2,1)}), bf16[4,16,5376]{2,1,0:T(8,128)(2,1)S(1)}, u32[]{:S(2)}, u32[]{:S(2)}) async-start(bf16[4,16,5376]{2,1,0:T(8,128)(2,1)} %bitcast.7), calls=%async_computation | async-start | bytes 1376256 | tf_op jit(solution)/shard_map/all_to_all | solution.py:137
  48.5 27.3 %copy-start.4 = (s32[1,32,2]{1,2,0:T(2,128)S(1)}, s32[1,32,2]{1,2,0:T(2,128)}, u32[]{:S(2)}) copy-start(s32[1,32,2]{1,2,0:T(2,128)} %param.12) | copy-start | bytes 772
  48.5 27.5 %copy-start.8 = (s32[16]{0:T(128)S(1)}, s32[16]{0:T(128)}, u32[]{:S(2)}) copy-start(s32[16]{0:T(128)} %param.11) | copy-start | bytes 196
  64.9 24.8 %copy-start.5 = (f32[16,5376]{1,0:T(8,128)S(1)}, f32[16,5376]{1,0:T(8,128)}, u32[]{:S(2)}) copy-start(f32[16,5376]{1,0:T(8,128)} %param.14) | copy-start | bytes 1032196
  64.9 24.8 %copy-start.6 = (f32[16,5376]{1,0:T(8,128)S(1)}, f32[16,5376]{1,0:T(8,128)}, u32[]{:S(2)}) copy-start(f32[16,5376]{1,0:T(8,128)} %param.15) | copy-start | bytes 1032196
  64.9 24.8 %copy-start.7 = (f32[16,5376]{1,0:T(8,128)S(1)}, f32[16,5376]{1,0:T(8,128)}, u32[]{:S(2)}) copy-start(f32[16,5376]{1,0:T(8,128)} %param.13) | copy-start | bytes 1032196
  66.0 23.4 %all-to-all-start.1 = ((bf16[32,2,5376]{2,1,0:T(2,128)(2,1)}), bf16[32,2,5376]{2,1,0:T(2,128)(2,1)S(1)}, u32[]{:S(2)}, u32[]{:S(2)}) async-start(bf16[32,2,5376]{2,1,0:T(2,128)(2,1)} %reshape.72), calls=%async_computation.1 | async-start | bytes 1376256 | tf_op jit(solution)/shard_map/all_to_all | solution.py:158
  90.9 22.2 %copy-start.3 = (f32[16,5376]{1,0:T(8,128)}, f32[16,5376]{1,0:T(8,128)S(1)}, u32[]{:S(2)}) copy-start(f32[16,5376]{1,0:T(8,128)S(1)} %get-tuple-element.11) | copy-start | bytes 1032196
  92.4 20.4 %all-to-all-start.2 = ((bf16[32,2,5376]{2,1,0:T(2,128)(2,1)}), bf16[32,2,5376]{2,1,0:T(2,128)(2,1)S(1)}, u32[]{:S(2)}, u32[]{:S(2)}) async-start(bf16[32,2,5376]{2,1,0:T(2,128)(2,1)} %reshape.74), calls=%async_computation.2 | async-start | bytes 1376256 | tf_op jit(solution)/shard_map/all_to_all | solution.py:158
  130.4 35.8 %collective-permute-start.4 = (bf16[64,5376]{1,0:T(8,128)(2,1)S(1)}, bf16[64,5376]{1,0:T(8,128)(2,1)S(1)}, u32[]{:S(2)}, u32[]{:S(2)}) collective-permute-start(bf16[64,5376]{1,0:T(8,128)(2,1)S(1)} %all_gather.3), channel_id=1, source_target_pairs={{0,22},{1,3},{2,0},{3,5},{4,2},{5,7},{6,4},{7,9},{8,6},{9,11},{10,... | collective-permute-start | bytes 2064392 | tf_op jit(solution)/shard_map/ppermute | solution.py:177
  154.1 23.2 %collective-permute-start.5 = (bf16[64,5376]{1,0:T(8,128)(2,1)S(1)}, bf16[64,5376]{1,0:T(8,128)(2,1)S(1)}, u32[]{:S(2)}, u32[]{:S(2)}) collective-permute-start(bf16[64,5376]{1,0:T(8,128)(2,1)S(1)} %all_gather.3), channel_id=1, source_target_pairs={{0,2},{1,23},{2,4},{3,1},{4,6},{5,3},{6,8},{7,5},{8,10},{9,7},{10,... | collective-permute-start | bytes 2064392 | tf_op jit(solution)/shard_map/ppermute | solution.py:176
  177.3 4.3 %copy-start.2 = (s32[128]{0:T(128)S(1)}, s32[128]{0:T(128)}, u32[]{:S(2)}) copy-start(s32[128]{0:T(128)} %param.9) | copy-start | bytes 1540
  177.9 6.5 %collective-permute-start.6 = (bf16[128,5376]{1,0:T(8,128)(2,1)S(1)}, bf16[128,5376]{1,0:T(8,128)(2,1)S(1)}, u32[]{:S(2)}, u32[]{:S(2)}) collective-permute-start(bf16[128,5376]{1,0:T(8,128)(2,1)S(1)} %convolution_convert_fusion), channel_id=1, source_target_pairs={{0,1},{1,0},{2,3},{3,2},{4,5},{5,4},{6,7},{7,6},{8,9},{9,8},{10,11... | collective-permute-start | bytes 4128776 | tf_op jit(solution)/shard_map/ppermute | solution.py:181

commit v5 on v4

--- a/solution.py
+++ b/solution.py
@@ -20,6 +20,7 @@
 GROUP = Z_SIZE // APART
 GROUPS = [[r + APART * k for k in range(GROUP)] for r in range(APART)]
 BLOCK_COLS = 896
+KERNEL_VMEM = 56 * 2**20
 
 SWAP = [(0, 1), (1, 0)]
 
@@ -64,45 +65,37 @@
     return pl.BlockSpec((height, BLOCK_COLS), lambda i: (0, i))
 
 
-def own_kernel(rows_ref, slot_ref, tokens_ref, out_ref):
-    chosen = (rows_ref[...] == slot_ref[...]).astype(jnp.bfloat16)
-    out_ref[...] = dot32(chosen, tokens_ref[...])
-
-
-def both_kernel(rows_ref, slot_ref, tokens_ref, own_ref, *out_refs):
-    chosen = (rows_ref[...] == slot_ref[...]).astype(jnp.bfloat16)
-    total = own_ref[...] + dot32(chosen, tokens_ref[...])
+def sum_kernel(rows_ref, own_slot_ref, other_slot_ref, own_ref, other_ref, *out_refs):
+    rows = rows_ref[...]
+    total = dot32((rows == own_slot_ref[...]).astype(jnp.bfloat16), own_ref[...])
+    total += dot32((rows == other_slot_ref[...]).astype(jnp.bfloat16), other_ref[...])
     part = total.shape[0] // len(out_refs)
     for i, out_ref in enumerate(out_refs):
         out_ref[...] = total[i * part : (i + 1) * part].astype(out_ref.dtype)
 
 
-def slot_sums(rows, slots, tokens, own, parts):
-    height, count, width = rows.shape[0], tokens.shape[0], tokens.shape[1]
-    inputs = [rows[:, None], slots[None, :], tokens]
-    in_specs = [whole((height, 1)), whole((1, count)), columns(count)]
-    if own is None:
-        kernel, out = own_kernel, [jax.ShapeDtypeStruct((height, width), jnp.float32)]
-    else:
-        kernel, out = both_kernel, [
-            jax.ShapeDtypeStruct((height // parts, width), jnp.bfloat16) for _ in range(parts)
-        ]
-        inputs.append(own)
-        in_specs.append(columns(height))
-    results = pl.pallas_call(
-        kernel,
+def slot_sums(rows, own_slot, other_slot, own, other, parts):
+    height, count, width = rows.shape[0], own.shape[0], own.shape[1]
+    part = height // parts
+    return pl.pallas_call(
+        sum_kernel,
         grid=(width // BLOCK_COLS,),
-        in_specs=in_specs,
-        out_specs=[columns(shape.shape[0]) for shape in out],
-        out_shape=out,
+        in_specs=[
+            whole((height, 1)),
+            whole((1, count)),
+            whole((1, count)),
+            columns(count),
+            columns(count),
+        ],
+        out_specs=[columns(part)] * parts,
+        out_shape=[jax.ShapeDtypeStruct((part, width), jnp.bfloat16)] * parts,
         cost_estimate=pl.CostEstimate(
-            flops=2 * height * count * width,
-            bytes_accessed=(2 * count + 4 * height) * width,
+            flops=4 * height * count * width,
+            bytes_accessed=2 * (2 * count + height) * width,
             transcendentals=0,
         ),
-        compiler_params=pltpu.CompilerParams(vmem_limit_bytes=16 * 2**20),
-    )(*inputs)
-    return results[0] if own is None else results
+        compiler_params=pltpu.CompilerParams(vmem_limit_bytes=KERNEL_VMEM),
+    )(rows[:, None], own_slot[None, :], other_slot[None, :], own, other)
 
 
 def on_device(grads, token_slot, node_ids, touched_ids, owner_map, moment, second, master):
@@ -117,16 +110,21 @@
     other_grads = lax.ppermute(grads, "c", SWAP)
     other_slot = lax.ppermute(token_slot, "c", SWAP)
 
-    def rows_of(shift):
+    ahead = 1 - 2 * core
+
+    def rows_of(shift, first_here):
         row = lax.iota(jnp.int32, GROUP * slot_dev)
-        z_of_row = lax.div(row, slot_dev) * APART + lax.rem(place + (shift + APART), APART)
+        member = lax.div(row, slot_dev) * APART
+        if first_here:
+            z_of_row = lax.rem(place + shift + ahead * member + 2 * Z_SIZE, Z_SIZE)
+        else:
+            z_of_row = lax.rem(place + shift + APART, APART) + member
         return (z_of_row * CORES + core) * slot_dev + lax.rem(row, slot_dev)
 
-    ahead = 1 - 2 * core
-    listed = jnp.concatenate([rows_of(0), rows_of(ahead), rows_of(-ahead)])
-
-    own_sums = slot_sums(listed, token_slot, grads, None, 1)
-    kept, for_ahead, for_behind = slot_sums(listed, other_slot, other_grads, own_sums, 3)
+    summed = jnp.concatenate([rows_of(shift, True) for shift in (0, ahead, -ahead)])
+    kept, for_ahead, for_behind = slot_sums(
+        summed, token_slot, other_slot, grads, other_grads, 3
+    )
     from_behind = lax.ppermute(for_ahead, ("z", "c"), neighbour(1))
     from_ahead = lax.ppermute(for_behind, ("z", "c"), neighbour(-1))
     near = (
@@ -134,15 +132,11 @@
         + from_behind.astype(jnp.float32)
         + from_ahead.astype(jnp.float32)
     ).astype(jnp.bfloat16)
-    blocks = lax.all_to_all(
-        near.reshape(GROUP, slot_dev, width),
-        "z",
-        split_axis=0,
-        concat_axis=0,
-        tiled=True,
-        axis_index_groups=GROUPS,
-    )
-    node_sum = jnp.sum(blocks.astype(jnp.float32), axis=0).astype(jnp.bfloat16)
+    blocks = [near[i * slot_dev : (i + 1) * slot_dev] for i in range(GROUP)]
+    total = blocks[0].astype(jnp.float32)
+    for i in range(1, GROUP):
+        total += lax.ppermute(blocks[i], ("z", "c"), neighbour(i * APART)).astype(jnp.float32)
+    node_sum = total.astype(jnp.bfloat16)
 
     owner_node = node_ids[0] // (VOCAB // node_count)
     same_owner = owner_node[:, None] == owner_node[None, :]
@@ -172,6 +166,8 @@
     returned = exchange(dot32(matches(position_map, touched_places), fresh_rows))
     rows = dot32(matches(send_slot, send_places), returned).astype(jnp.bfloat16)
 
+    listed = jnp.concatenate([rows_of(shift, False) for shift in (0, ahead, -ahead)])
+
     here = lax.all_gather(rows, "z", axis=0, tiled=True, axis_index_groups=GROUPS)
     from_behind = lax.ppermute(here, ("z", "c"), neighbour(1))
     from_ahead = lax.ppermute(here, ("z", "c"), neighbour(-1))

time: 187 us -> 187 us (level)
  blocking collectives: 17 us -> 31.5 us
  starting transfers between devices: 72.1 us -> 62.2 us
  waiting for transfers between devices: 79.6 us -> 73.4 us
    ppermute x1, starting transfers between devices: 23.7 us -> 1.95 us  [on_device(): from_ahead = lax.ppermute(here, ('z', 'c'), neighbour(-1))]
    all_to_all x1 -> x0, waiting for transfers between devices: 15.9 us -> none  [on_device(): lax.all_to_all(near.reshape(GROUP, slot_dev, width), 'z', split_axis=0, c...]
    all_gather x1, blocking collectives: 17 us -> 31.5 us  [on_device(): lax.all_gather(rows, 'z', axis=0, tiled=True, axis_index_groups=GROUPS)]
    ppermute x0 -> x3, waiting for transfers between devices: none -> 13.6 us  [on_device(): lax.ppermute(blocks[i], ('z', 'c'), neighbour(i * APART))]
    ppermute x0 -> x3, starting transfers between devices: none -> 12.5 us  [on_device(): lax.ppermute(blocks[i], ('z', 'c'), neighbour(i * APART))]
    ppermute x1, waiting for transfers between devices: 11.1 us -> 0.01 us  [on_device(): from_behind = lax.ppermute(here, ('z', 'c'), neighbour(1))]
    ppermute x1, waiting for transfers between devices: 7.04 us -> 16.2 us  [on_device(): from_ahead = lax.ppermute(here, ('z', 'c'), neighbour(-1))]
    all_to_all x1 -> x0, starting transfers between devices: 3.56 us -> none  [on_device(): lax.all_to_all(near.reshape(GROUP, slot_dev, width), 'z', split_axis=0, c...]
  transfers between devices with their start and end apart: 10 -> 12, of which waited for: 8 -> 10; matrix products, arithmetic and copies ran while one was open for 1% -> 1% of each run, Pallas kernels for 1% -> 0%
where the time goes in v5:
time: 187 us; the launch traced here: 186 us
  waiting for transfers between devices  73.4 us (39%)
  starting transfers between devices  62.2 us (33%)
  blocking collectives  31.5 us (17%)
  Pallas kernels  6.11 us (3%)
  local copies, waits for them, and re-layouts  5 us (3%)
  matrix products  3.34 us (2%)
  other arithmetic  3.2 us (2%)
    all_gather x1, blocking collectives, on_device(): lax.all_gather(rows, 'z', axis=0, tiled=True, axis_index_groups=GROUPS)  31.5 us
    all_to_all x2, waiting for transfers between devices, exchange(): lax.all_to_all(rows.astype(jnp.bfloat16).reshape(node_count, capacity, wi...  27 us
    all_to_all x2, starting transfers between devices, exchange(): lax.all_to_all(rows.astype(jnp.bfloat16).reshape(node_count, capacity, wi...  16.7 us
    ppermute x1, waiting for transfers between devices, on_device(): from_ahead = lax.ppermute(here, ('z', 'c'), neighbour(-1))  16.2 us
    ppermute x3, waiting for transfers between devices, on_device(): lax.ppermute(blocks[i], ('z', 'c'), neighbour(i * APART))  13.6 us
    ppermute x3, starting transfers between devices, on_device(): lax.ppermute(blocks[i], ('z', 'c'), neighbour(i * APART))  12.5 us
    ppermute x1, starting transfers between devices, on_device(): other_grads = lax.ppermute(grads, 'c', SWAP)  12.4 us
    ppermute x1, waiting for transfers between devices, on_device(): from_behind = lax.ppermute(for_ahead, ('z', 'c'), neighbour(1))  10.7 us
  transfers between devices with their start and end apart: 12, of which 10 were waited for; matrix products, arithmetic and copies ran while one was open for 1% of the time, Pallas kernels for 0%

profile of v5, /device:TPU:1, one launch (start us, length us, event | category | flops | bytes accessed | tf_op | source)
XLA Modules:
  0.0 185.7 jit_solution(1598904572788271609)
XLA Ops:
  0.6 12.4 %collective-permute-start.1 = (bf16[128,5376]{1,0:T(8,128)(2,1)}, bf16[128,5376]{1,0:T(8,128)(2,1)S(1)}, u32[]{:S(2)}, u32[]{:S(2)}) collective-permute-start(bf16[128,5376]{1,0:T(8,128)(2,1)} %own_ref.1), channel_id=1, source_target_pairs={{0,1},{1,0},{2,3},{3,2},{4,5},{5,4},{6,7},{7,6},{8,9},{9,8},{10,11... | collective-permute-start | bytes 4128776 | tf_op jit(solution)/shard_map/ppermute | solution.py:110
  13.1 1.9 %collective-permute-start = (s32[128]{0:T(128)}, s32[128]{0:T(128)S(1)}, u32[]{:S(2)}, u32[]{:S(2)}) collective-permute-start(s32[128]{0:T(128)} %param.9), channel_id=1, source_target_pairs={{0,1},{1,0},{2,3},{3,2},{4,5},{5,4},{6,7},{7,6},{8,9},{9,8},{10,11... | collective-permute-start | bytes 1544 | tf_op jit(solution)/shard_map/ppermute | solution.py:111
  15.1 0.8 copy.16.rows_ref
  16.8 0.5 copy-done
  17.3 6.1 %shard_map.111 = (bf16[64,5376]{1,0:T(8,128)(2,1)}, bf16[64,5376]{1,0:T(8,128)(2,1)}, bf16[64,5376]{1,0:T(8,128)(2,1)}) custom-call(s32[192,1]{1,0:T(8,128)} %copy.16.rows_ref, s32[1,128]{1,0:T(1,128)} %bitcast.26, s32[1,128]{1,0:T(1,128)} %bitcast.27, bf16[128,5376]{1,0:T(8,128)(2,1)} %own_ref.1, bf16[128,5376]{1,0:T(8,128)(2,1)} %copy-done), custom_call_target="tpu_custom_call" | custom-call | flops 528482304 | bytes 4816896 | tf_op jit(solution)/shard_map/pallas_call | solution.py:80
  23.4 5.3 %collective-permute-start.2 = (bf16[64,5376]{1,0:T(8,128)(2,1)}, bf16[64,5376]{1,0:T(8,128)(2,1)S(1)}, u32[]{:S(2)}, u32[]{:S(2)}) collective-permute-start(bf16[64,5376]{1,0:T(8,128)(2,1)} %get-tuple-element.8), channel_id=1, source_target_pairs={{0,2},{1,23},{2,4},{3,1},{4,6},{5,3},{6,8},{7,5},{8,10},{9,7},{10,... | collective-permute-start | bytes 2064392 | tf_op jit(solution)/shard_map/ppermute | solution.py:128
  28.7 1.9 %collective-permute-start.3 = (bf16[64,5376]{1,0:T(8,128)(2,1)}, bf16[64,5376]{1,0:T(8,128)(2,1)S(1)}, u32[]{:S(2)}, u32[]{:S(2)}) collective-permute-start(bf16[64,5376]{1,0:T(8,128)(2,1)} %get-tuple-element.9), channel_id=1, source_target_pairs={{0,22},{1,3},{2,0},{3,5},{4,2},{5,7},{6,4},{7,9},{8,6},{9,11},{10,... | collective-permute-start | bytes 2064392 | tf_op jit(solution)/shard_map/ppermute | solution.py:129
  30.9 10.7 %collective-permute-done.2 = bf16[64,5376]{1,0:T(8,128)(2,1)S(1)} collective-permute-done((bf16[64,5376]{1,0:T(8,128)(2,1)}, bf16[64,5376]{1,0:T(8,128)(2,1)S(1)}, u32[]{:S(2)}, u32[]{:S(2)}) %collective-permute-start.2) | collective-permute-done | bytes 688160 | tf_op jit(solution)/shard_map/ppermute | solution.py:128
  41.6 3.4 %collective-permute-done.3 = bf16[64,5376]{1,0:T(8,128)(2,1)S(1)} collective-permute-done((bf16[64,5376]{1,0:T(8,128)(2,1)}, bf16[64,5376]{1,0:T(8,128)(2,1)S(1)}, u32[]{:S(2)}, u32[]{:S(2)}) %collective-permute-start.3) | collective-permute-done | bytes 688160 | tf_op jit(solution)/shard_map/ppermute | solution.py:129
  45.0 1.4 add_convert_fusion
  46.4 3.6 %collective-permute-start.4 = (bf16[16,5376]{1,0:T(8,128)(2,1)S(1)}, bf16[16,5376]{1,0:T(8,128)(2,1)S(1)}, u32[]{:S(2)}, u32[]{:S(2)}) collective-permute-start(bf16[16,5376]{1,0:T(8,128)(2,1)S(1)} %get-tuple-element.13), channel_id=1, source_target_pairs={{0,6},{1,19},{2,8},{3,21},{4,10},{5,23},{6,12},{7,1},{8,14},{9,3},... | collective-permute-start | bytes 516104 | tf_op jit(solution)/shard_map/ppermute | solution.py:138
  50.0 3.5 %collective-permute-start.6 = (bf16[16,5376]{1,0:T(8,128)(2,1)S(1)}, bf16[16,5376]{1,0:T(8,128)(2,1)S(1)}, u32[]{:S(2)}, u32[]{:S(2)}) collective-permute-start(bf16[16,5376]{1,0:T(8,128)(2,1)S(1)} %get-tuple-element.14), channel_id=1, source_target_pairs={{0,18},{1,7},{2,20},{3,9},{4,22},{5,11},{6,0},{7,13},{8,2},{9,15},... | collective-permute-start | bytes 516104 | tf_op jit(solution)/shard_map/ppermute | solution.py:138
  53.5 5.4 %collective-permute-start.5 = (bf16[16,5376]{1,0:T(8,128)(2,1)S(1)}, bf16[16,5376]{1,0:T(8,128)(2,1)S(1)}, u32[]{:S(2)}, u32[]{:S(2)}) collective-permute-start(bf16[16,5376]{1,0:T(8,128)(2,1)S(1)} %get-tuple-element.15), channel_id=1, source_target_pairs={{0,12},{1,13},{2,14},{3,15},{4,16},{5,17},{6,18},{7,19},{8,20},{9,... | collective-permute-start | bytes 516104 | tf_op jit(solution)/shard_map/ppermute | solution.py:138
  58.9 2.6 %collective-permute-done.4 = bf16[16,5376]{1,0:T(8,128)(2,1)S(1)} collective-permute-done((bf16[16,5376]{1,0:T(8,128)(2,1)S(1)}, bf16[16,5376]{1,0:T(8,128)(2,1)S(1)}, u32[]{:S(2)}, u32[]{:S(2)}) %collective-permute-start.4) | collective-permute-done | bytes 172064 | tf_op jit(solution)/shard_map/ppermute | solution.py:138
  61.5 0.9 collective-permute-done.6
  62.5 10.1 %collective-permute-done.5 = bf16[16,5376]{1,0:T(8,128)(2,1)S(1)} collective-permute-done((bf16[16,5376]{1,0:T(8,128)(2,1)S(1)}, bf16[16,5376]{1,0:T(8,128)(2,1)S(1)}, u32[]{:S(2)}, u32[]{:S(2)}) %collective-permute-start.5) | collective-permute-done | bytes 172064 | tf_op jit(solution)/shard_map/ppermute | solution.py:138
  72.9 1.1 reshape.68
  74.0 9.6 %all-to-all-start = ((bf16[32,2,5376]{2,1,0:T(2,128)(2,1)}), bf16[32,2,5376]{2,1,0:T(2,128)(2,1)S(1)}, u32[]{:S(2)}, u32[]{:S(2)}) async-start(bf16[32,2,5376]{2,1,0:T(2,128)(2,1)} %reshape.68), calls=%async_computation | async-start | bytes 1376256 | tf_op jit(solution)/shard_map/all_to_all | solution.py:152
  83.9 13.5 %all-to-all-done = bf16[32,2,5376]{2,1,0:T(2,128)(2,1)S(1)} async-done(((bf16[32,2,5376]{2,1,0:T(2,128)(2,1)}), bf16[32,2,5376]{2,1,0:T(2,128)(2,1)S(1)}, u32[]{:S(2)}, u32[]{:S(2)}) %all-to-all-start) | async-done | bytes 688160 | tf_op jit(solution)/shard_map/all_to_all | solution.py:152
  97.7 1.2 fusion.2
  99.3 1.1 reshape.70
  100.4 7.1 %all-to-all-start.1 = ((bf16[32,2,5376]{2,1,0:T(2,128)(2,1)}), bf16[32,2,5376]{2,1,0:T(2,128)(2,1)S(1)}, u32[]{:S(2)}, u32[]{:S(2)}) async-start(bf16[32,2,5376]{2,1,0:T(2,128)(2,1)} %reshape.70), calls=%async_computation.1 | async-start | bytes 1376256 | tf_op jit(solution)/shard_map/all_to_all | solution.py:152
  107.6 13.5 %all-to-all-done.1 = bf16[32,2,5376]{2,1,0:T(2,128)(2,1)S(1)} async-done(((bf16[32,2,5376]{2,1,0:T(2,128)(2,1)}), bf16[32,2,5376]{2,1,0:T(2,128)(2,1)S(1)}, u32[]{:S(2)}, u32[]{:S(2)}) %all-to-all-start.1) | async-done | bytes 688160 | tf_op jit(solution)/shard_map/all_to_all | solution.py:152
  121.7 31.5 %all_gather.3 = bf16[64,5376]{1,0:T(8,128)(2,1)S(1)} all-gather(bf16[16,5376]{1,0:T(8,128)(2,1)S(1)} %convolution_convert_fusion.4), channel_id=1, replica_groups={{0,6,12,18},{2,8,14,20},{4,10,16,22},{1,7,13,19},{3,9,15,21},{5,11,17,2..., dimensions={0}, use_global_device_ids=true | all-gather | bytes 860160 | tf_op jit(solution)/shard_map/all_gather | solution.py:171
  153.1 4.9 %collective-permute-start.8 = (bf16[64,5376]{1,0:T(8,128)(2,1)S(1)}, bf16[64,5376]{1,0:T(8,128)(2,1)S(1)}, u32[]{:S(2)}, u32[]{:S(2)}) collective-permute-start(bf16[64,5376]{1,0:T(8,128)(2,1)S(1)} %all_gather.3), channel_id=1, source_target_pairs={{0,2},{1,23},{2,4},{3,1},{4,6},{5,3},{6,8},{7,5},{8,10},{9,7},{10,... | collective-permute-start | bytes 2064392 | tf_op jit(solution)/shard_map/ppermute | solution.py:172
  158.1 1.9 %collective-permute-start.7 = (bf16[64,5376]{1,0:T(8,128)(2,1)S(1)}, bf16[64,5376]{1,0:T(8,128)(2,1)S(1)}, u32[]{:S(2)}, u32[]{:S(2)}) collective-permute-start(bf16[64,5376]{1,0:T(8,128)(2,1)S(1)} %all_gather.3), channel_id=1, source_target_pairs={{0,22},{1,3},{2,0},{3,5},{4,2},{5,7},{6,4},{7,9},{8,6},{9,11},{10,... | collective-permute-start | bytes 2064392 | tf_op jit(solution)/shard_map/ppermute | solution.py:173
  160.1 16.2 %collective-permute-done.7 = bf16[64,5376]{1,0:T(8,128)(2,1)S(1)} collective-permute-done((bf16[64,5376]{1,0:T(8,128)(2,1)S(1)}, bf16[64,5376]{1,0:T(8,128)(2,1)S(1)}, u32[]{:S(2)}, u32[]{:S(2)}) %collective-permute-start.7) | collective-permute-done | bytes 688160 | tf_op jit(solution)/shard_map/ppermute | solution.py:173
  176.4 0.6 convolution_convert_fusion
  177.0 4.6 %collective-permute-start.9 = (bf16[128,5376]{1,0:T(8,128)(2,1)S(1)}, bf16[128,5376]{1,0:T(8,128)(2,1)S(1)}, u32[]{:S(2)}, u32[]{:S(2)}) collective-permute-start(bf16[128,5376]{1,0:T(8,128)(2,1)S(1)} %convolution_convert_fusion), channel_id=1, source_target_pairs={{0,1},{1,0},{2,3},{3,2},{4,5},{5,4},{6,7},{7,6},{8,9},{9,8},{10,11... | collective-permute-start | bytes 4128776 | tf_op jit(solution)/shard_map/ppermute | solution.py:177
  181.6 0.6 convolution_convert_fusion.1
  182.2 2.1 %collective-permute-done.9 = bf16[128,5376]{1,0:T(8,128)(2,1)S(1)} collective-permute-done((bf16[128,5376]{1,0:T(8,128)(2,1)S(1)}, bf16[128,5376]{1,0:T(8,128)(2,1)S(1)}, u32[]{:S(2)}, u32[]{:S(2)}) %collective-permute-start.9) | collective-permute-done | bytes 1376288 | tf_op jit(solution)/shard_map/ppermute | solution.py:177
  184.3 1.4 add.200
  (47 shorter events, 3.2 us)
Async XLA Ops:
  0.6 30.0 %copy-start.10 = (s32[1,16]{1,0:T(1,128)S(1)}, s32[1,16]{1,0:T(1,128)}, u32[]{:S(2)}) copy-start(s32[1,16]{1,0:T(1,128)} %param.10) | copy-start | bytes 196
  0.6 15.6 %collective-permute-start.1 = (bf16[128,5376]{1,0:T(8,128)(2,1)}, bf16[128,5376]{1,0:T(8,128)(2,1)S(1)}, u32[]{:S(2)}, u32[]{:S(2)}) collective-permute-start(bf16[128,5376]{1,0:T(8,128)(2,1)} %own_ref.1), channel_id=1, source_target_pairs={{0,1},{1,0},{2,3},{3,2},{4,5},{5,4},{6,7},{7,6},{8,9},{9,8},{10,11... | collective-permute-start | bytes 4128776 | tf_op jit(solution)/shard_map/ppermute | solution.py:110
  13.1 3.2 %collective-permute-start = (s32[128]{0:T(128)}, s32[128]{0:T(128)S(1)}, u32[]{:S(2)}, u32[]{:S(2)}) collective-permute-start(s32[128]{0:T(128)} %param.9), channel_id=1, source_target_pairs={{0,1},{1,0},{2,3},{3,2},{4,5},{5,4},{6,7},{7,6},{8,9},{9,8},{10,11... | collective-permute-start | bytes 1544 | tf_op jit(solution)/shard_map/ppermute | solution.py:111
  16.2 0.5 copy-start.3
  16.2 1.1 copy-start
  23.4 18.2 %collective-permute-start.2 = (bf16[64,5376]{1,0:T(8,128)(2,1)}, bf16[64,5376]{1,0:T(8,128)(2,1)S(1)}, u32[]{:S(2)}, u32[]{:S(2)}) collective-permute-start(bf16[64,5376]{1,0:T(8,128)(2,1)} %get-tuple-element.8), channel_id=1, source_target_pairs={{0,2},{1,23},{2,4},{3,1},{4,6},{5,3},{6,8},{7,5},{8,10},{9,7},{10,... | collective-permute-start | bytes 2064392 | tf_op jit(solution)/shard_map/ppermute | solution.py:128
  28.7 16.3 %collective-permute-start.3 = (bf16[64,5376]{1,0:T(8,128)(2,1)}, bf16[64,5376]{1,0:T(8,128)(2,1)S(1)}, u32[]{:S(2)}, u32[]{:S(2)}) collective-permute-start(bf16[64,5376]{1,0:T(8,128)(2,1)} %get-tuple-element.9), channel_id=1, source_target_pairs={{0,22},{1,3},{2,0},{3,5},{4,2},{5,7},{6,4},{7,9},{8,6},{9,11},{10,... | collective-permute-start | bytes 2064392 | tf_op jit(solution)/shard_map/ppermute | solution.py:129
  46.4 15.2 %collective-permute-start.4 = (bf16[16,5376]{1,0:T(8,128)(2,1)S(1)}, bf16[16,5376]{1,0:T(8,128)(2,1)S(1)}, u32[]{:S(2)}, u32[]{:S(2)}) collective-permute-start(bf16[16,5376]{1,0:T(8,128)(2,1)S(1)} %get-tuple-element.13), channel_id=1, source_target_pairs={{0,6},{1,19},{2,8},{3,21},{4,10},{5,23},{6,12},{7,1},{8,14},{9,3},... | collective-permute-start | bytes 516104 | tf_op jit(solution)/shard_map/ppermute | solution.py:138
  50.0 12.4 %collective-permute-start.6 = (bf16[16,5376]{1,0:T(8,128)(2,1)S(1)}, bf16[16,5376]{1,0:T(8,128)(2,1)S(1)}, u32[]{:S(2)}, u32[]{:S(2)}) collective-permute-start(bf16[16,5376]{1,0:T(8,128)(2,1)S(1)} %get-tuple-element.14), channel_id=1, source_target_pairs={{0,18},{1,7},{2,20},{3,9},{4,22},{5,11},{6,0},{7,13},{8,2},{9,15},... | collective-permute-start | bytes 516104 | tf_op jit(solution)/shard_map/ppermute | solution.py:138
  53.5 19.1 %collective-permute-start.5 = (bf16[16,5376]{1,0:T(8,128)(2,1)S(1)}, bf16[16,5376]{1,0:T(8,128)(2,1)S(1)}, u32[]{:S(2)}, u32[]{:S(2)}) collective-permute-start(bf16[16,5376]{1,0:T(8,128)(2,1)S(1)} %get-tuple-element.15), channel_id=1, source_target_pairs={{0,12},{1,13},{2,14},{3,15},{4,16},{5,17},{6,18},{7,19},{8,20},{9,... | collective-permute-start | bytes 516104 | tf_op jit(solution)/shard_map/ppermute | solution.py:138
  58.9 24.7 %copy-start.5 = (s32[1,32,2]{1,2,0:T(2,128)S(1)}, s32[1,32,2]{1,2,0:T(2,128)}, u32[]{:S(2)}) copy-start(s32[1,32,2]{1,2,0:T(2,128)} %param.12) | copy-start | bytes 772
  58.9 24.9 %copy-start.9 = (s32[16]{0:T(128)S(1)}, s32[16]{0:T(128)}, u32[]{:S(2)}) copy-start(s32[16]{0:T(128)} %param.11) | copy-start | bytes 196
  72.9 24.7 %copy-start.6 = (f32[16,5376]{1,0:T(8,128)S(1)}, f32[16,5376]{1,0:T(8,128)}, u32[]{:S(2)}) copy-start(f32[16,5376]{1,0:T(8,128)} %param.14) | copy-start | bytes 1032196
  72.9 24.7 %copy-start.7 = (f32[16,5376]{1,0:T(8,128)S(1)}, f32[16,5376]{1,0:T(8,128)}, u32[]{:S(2)}) copy-start(f32[16,5376]{1,0:T(8,128)} %param.15) | copy-start | bytes 1032196
  72.9 24.7 %copy-start.8 = (f32[16,5376]{1,0:T(8,128)S(1)}, f32[16,5376]{1,0:T(8,128)}, u32[]{:S(2)}) copy-start(f32[16,5376]{1,0:T(8,128)} %param.13) | copy-start | bytes 1032196
  74.0 23.3 %all-to-all-start = ((bf16[32,2,5376]{2,1,0:T(2,128)(2,1)}), bf16[32,2,5376]{2,1,0:T(2,128)(2,1)S(1)}, u32[]{:S(2)}, u32[]{:S(2)}) async-start(bf16[32,2,5376]{2,1,0:T(2,128)(2,1)} %reshape.68), calls=%async_computation | async-start | bytes 1376256 | tf_op jit(solution)/shard_map/all_to_all | solution.py:152
  98.9 22.5 %copy-start.1 = (f32[16,5376]{1,0:T(8,128)}, f32[16,5376]{1,0:T(8,128)S(1)}, u32[]{:S(2)}) copy-start(f32[16,5376]{1,0:T(8,128)S(1)} %get-tuple-element.11) | copy-start | bytes 1032196
  100.4 20.8 %all-to-all-start.1 = ((bf16[32,2,5376]{2,1,0:T(2,128)(2,1)}), bf16[32,2,5376]{2,1,0:T(2,128)(2,1)S(1)}, u32[]{:S(2)}, u32[]{:S(2)}) async-start(bf16[32,2,5376]{2,1,0:T(2,128)(2,1)} %reshape.70), calls=%async_computation.1 | async-start | bytes 1376256 | tf_op jit(solution)/shard_map/all_to_all | solution.py:152
  153.1 23.2 %copy-start.4 = (s32[128]{0:T(128)S(1)}, s32[128]{0:T(128)}, u32[]{:S(2)}) copy-start(s32[128]{0:T(128)} %copy-done.3) | copy-start | bytes 1540
  153.1 23.2 %collective-permute-start.8 = (bf16[64,5376]{1,0:T(8,128)(2,1)S(1)}, bf16[64,5376]{1,0:T(8,128)(2,1)S(1)}, u32[]{:S(2)}, u32[]{:S(2)}) collective-permute-start(bf16[64,5376]{1,0:T(8,128)(2,1)S(1)} %all_gather.3), channel_id=1, source_target_pairs={{0,2},{1,23},{2,4},{3,1},{4,6},{5,3},{6,8},{7,5},{8,10},{9,7},{10,... | collective-permute-start | bytes 2064392 | tf_op jit(solution)/shard_map/ppermute | solution.py:172
  158.1 18.2 %collective-permute-start.7 = (bf16[64,5376]{1,0:T(8,128)(2,1)S(1)}, bf16[64,5376]{1,0:T(8,128)(2,1)S(1)}, u32[]{:S(2)}, u32[]{:S(2)}) collective-permute-start(bf16[64,5376]{1,0:T(8,128)(2,1)S(1)} %all_gather.3), channel_id=1, source_target_pairs={{0,22},{1,3},{2,0},{3,5},{4,2},{5,7},{6,4},{7,9},{8,6},{9,11},{10,... | collective-permute-start | bytes 2064392 | tf_op jit(solution)/shard_map/ppermute | solution.py:173
  176.4 5.2 %copy-start.2 = (s32[128]{0:T(128)S(1)}, s32[128]{0:T(128)}, u32[]{:S(2)}) copy-start(s32[128]{0:T(128)} %param.9) | copy-start | bytes 1540
  177.0 7.4 %collective-permute-start.9 = (bf16[128,5376]{1,0:T(8,128)(2,1)S(1)}, bf16[128,5376]{1,0:T(8,128)(2,1)S(1)}, u32[]{:S(2)}, u32[]{:S(2)}) collective-permute-start(bf16[128,5376]{1,0:T(8,128)(2,1)S(1)} %convolution_convert_fusion), channel_id=1, source_target_pairs={{0,1},{1,0},{2,3},{3,2},{4,5},{5,4},{6,7},{7,6},{8,9},{9,8},{10,11... | collective-permute-start | bytes 4128776 | tf_op jit(solution)/shard_map/ppermute | solution.py:177

commit v6 on v5

--- a/solution.py
+++ b/solution.py
@@ -20,7 +20,7 @@
 GROUP = Z_SIZE // APART
 GROUPS = [[r + APART * k for k in range(GROUP)] for r in range(APART)]
 BLOCK_COLS = 896
-KERNEL_VMEM = 56 * 2**20
+LAST_PARTS = 2
 
 SWAP = [(0, 1), (1, 0)]
 
@@ -57,44 +57,32 @@
     return jnp.dot(a, b, preferred_element_type=jnp.float32)
 
 
-def whole(shape):
-    return pl.BlockSpec(shape, lambda i: (0, 0))
-
-
-def columns(height):
-    return pl.BlockSpec((height, BLOCK_COLS), lambda i: (0, i))
-
-
 def sum_kernel(rows_ref, own_slot_ref, other_slot_ref, own_ref, other_ref, *out_refs):
     rows = rows_ref[...]
-    total = dot32((rows == own_slot_ref[...]).astype(jnp.bfloat16), own_ref[...])
-    total += dot32((rows == other_slot_ref[...]).astype(jnp.bfloat16), other_ref[...])
-    part = total.shape[0] // len(out_refs)
-    for i, out_ref in enumerate(out_refs):
-        out_ref[...] = total[i * part : (i + 1) * part].astype(out_ref.dtype)
+    own = (rows == own_slot_ref[...]).astype(jnp.bfloat16)
+    other = (rows == other_slot_ref[...]).astype(jnp.bfloat16)
+    part = rows.shape[0] // len(out_refs)
+    for start in range(0, own_ref.shape[1], BLOCK_COLS):
+        at = pl.ds(start, BLOCK_COLS)
+        total = dot32(own, own_ref[:, at]) + dot32(other, other_ref[:, at])
+        for i, out_ref in enumerate(out_refs):
+            out_ref[:, at] = total[i * part : (i + 1) * part].astype(out_ref.dtype)
 
 
 def slot_sums(rows, own_slot, other_slot, own, other, parts):
     height, count, width = rows.shape[0], own.shape[0], own.shape[1]
-    part = height // parts
+    in_vmem = pl.BlockSpec(memory_space=pltpu.VMEM)
     return pl.pallas_call(
         sum_kernel,
-        grid=(width // BLOCK_COLS,),
-        in_specs=[
-            whole((height, 1)),
-            whole((1, count)),
-            whole((1, count)),
-            columns(count),
-            columns(count),
-        ],
-        out_specs=[columns(part)] * parts,
-        out_shape=[jax.ShapeDtypeStruct((part, width), jnp.bfloat16)] * parts,
+        in_specs=[in_vmem] * 5,
+        out_specs=[in_vmem] * parts,
+        out_shape=[jax.ShapeDtypeStruct((height // parts, width), jnp.bfloat16)] * parts,
         cost_estimate=pl.CostEstimate(
             flops=4 * height * count * width,
             bytes_accessed=2 * (2 * count + height) * width,
             transcendentals=0,
         ),
-        compiler_params=pltpu.CompilerParams(vmem_limit_bytes=KERNEL_VMEM),
+        compiler_params=pltpu.CompilerParams(vmem_limit_bytes=16 * 2**20),
     )(rows[:, None], own_slot[None, :], other_slot[None, :], own, other)
 
 
@@ -169,12 +157,23 @@
     listed = jnp.concatenate([rows_of(shift, False) for shift in (0, ahead, -ahead)])
 
     here = lax.all_gather(rows, "z", axis=0, tiled=True, axis_index_groups=GROUPS)
-    from_behind = lax.ppermute(here, ("z", "c"), neighbour(1))
-    from_ahead = lax.ppermute(here, ("z", "c"), neighbour(-1))
-    gathered = jnp.concatenate([here, from_ahead, from_behind])
-    theirs = dot32(matches(other_slot, listed), gathered).astype(jnp.bfloat16)
-    mine = dot32(matches(token_slot, listed), gathered).astype(jnp.bfloat16)
-    token_rows = lax.optimization_barrier(mine) + lax.ppermute(theirs, "c", SWAP)
+    own_choice, other_choice = matches(token_slot, listed), matches(other_slot, listed)
+    step = width // LAST_PARTS
+    halves = [here[:, i * step : (i + 1) * step] for i in range(LAST_PARTS)]
+    arrived = [
+        (
+            half,
+            lax.ppermute(half, ("z", "c"), neighbour(-1)),
+            lax.ppermute(half, ("z", "c"), neighbour(1)),
+        )
+        for half in halves
+    ]
+    tokens = []
+    for gathered in map(jnp.concatenate, arrived):
+        theirs = dot32(other_choice, gathered).astype(jnp.bfloat16)
+        mine = dot32(own_choice, gathered).astype(jnp.bfloat16)
+        tokens.append(lax.optimization_barrier(mine) + lax.ppermute(theirs, "c", SWAP))
+    token_rows = jnp.concatenate(tokens, axis=1)
     return token_rows, moment_out, second_out, master_out
 
 

time: 187 us -> 181 us (0.968)
  waiting for transfers between devices: 73.4 us -> 59.7 us
  starting transfers between devices: 62.2 us -> 71.3 us
  Pallas kernels: 6.11 us -> 1.27 us
  blocking collectives: 31.5 us -> 35.9 us
    ppermute x2 -> x4, waiting for transfers between devices: 16.2 us -> 4.08 us  [the longest x2 4.08 us: on_device(): lax.ppermute(half, ('z', 'c'), neighbour(-1))]
    ppermute x2 -> x4, starting transfers between devices: 6.87 us -> 12.2 us  [the longest x2 6.27 us: on_device(): lax.ppermute(half, ('z', 'c'), neighbour(-1))]
    ppermute x1, waiting for transfers between devices: 10.7 us -> 5.52 us  [on_device(): from_behind = lax.ppermute(for_ahead, ('z', 'c'), neighbour(1))]
    pallas_call x1, Pallas kernels: 6.11 us -> 1.27 us  [slot_sums(): pl.pallas_call(sum_kernel, in_specs=[in_vmem] * 5, out_specs=[in_vmem] *...]
    ppermute x1, waiting for transfers between devices: 3.4 us -> 8.23 us  [on_device(): from_ahead = lax.ppermute(for_behind, ('z', 'c'), neighbour(-1))]
    all_gather x1, blocking collectives: 31.5 us -> 35.9 us  [on_device(): lax.all_gather(rows, 'z', axis=0, tiled=True, axis_index_groups=GROUPS)]
    ppermute x1 -> x2, starting transfers between devices: 4.63 us -> 8.97 us  [on_device(): lax.ppermute(theirs, 'c', SWAP)]
    dot_general x6 -> x8, matrix products: 3.34 us -> 3.8 us  [dot32(): return jnp.dot(a, b, preferred_element_type=jnp.float32)]
  transfers between devices with their start and end apart: 12 -> 15, of which waited for: 10 -> 10; matrix products, arithmetic and copies ran while one was open for 1% -> 1% of each run, Pallas kernels for 0% -> 0%
where the time goes in v6:
time: 181 us; the launch traced here: 180 us
  starting transfers between devices  71.3 us (39%)
  waiting for transfers between devices  59.7 us (33%)
  blocking collectives  35.9 us (20%)
  local copies, waits for them, and re-layouts  5.16 us (3%)
  matrix products  3.8 us (2%)
  other arithmetic  2.19 us (1%)
    all_gather x1, blocking collectives, on_device(): lax.all_gather(rows, 'z', axis=0, tiled=True, axis_index_groups=GROUPS)  35.9 us
    all_to_all x2, waiting for transfers between devices, exchange(): lax.all_to_all(rows.astype(jnp.bfloat16).reshape(node_count, capacity, wi...  28.3 us
    all_to_all x2, starting transfers between devices, exchange(): lax.all_to_all(rows.astype(jnp.bfloat16).reshape(node_count, capacity, wi...  16.3 us
    ppermute x1, starting transfers between devices, on_device(): other_grads = lax.ppermute(grads, 'c', SWAP)  12.4 us
    ppermute x3, starting transfers between devices, on_device(): lax.ppermute(blocks[i], ('z', 'c'), neighbour(i * APART))  12.1 us
    ppermute x3, waiting for transfers between devices, on_device(): lax.ppermute(blocks[i], ('z', 'c'), neighbour(i * APART))  11.9 us
    ppermute x2, starting transfers between devices, on_device(): lax.ppermute(theirs, 'c', SWAP)  8.97 us
    ppermute x1, waiting for transfers between devices, on_device(): from_ahead = lax.ppermute(for_behind, ('z', 'c'), neighbour(-1))  8.23 us
  transfers between devices with their start and end apart: 15, of which 10 were waited for; matrix products, arithmetic and copies ran while one was open for 1% of the time, Pallas kernels for 0%

profile of v6, /device:TPU:1, one launch (start us, length us, event | category | flops | bytes accessed | tf_op | source)
XLA Modules:
  0.0 180.4 jit_solution(11777863270238158347)
XLA Ops:
  0.6 12.4 %collective-permute-start.1 = (bf16[128,5376]{1,0:T(8,128)(2,1)}, bf16[128,5376]{1,0:T(8,128)(2,1)S(1)}, u32[]{:S(2)}, u32[]{:S(2)}) collective-permute-start(bf16[128,5376]{1,0:T(8,128)(2,1)} %own_ref.1), channel_id=1, source_target_pairs={{0,1},{1,0},{2,3},{3,2},{4,5},{5,4},{6,7},{7,6},{8,9},{9,8},{10,11... | collective-permute-start | bytes 4128776 | tf_op jit(solution)/shard_map/ppermute | solution.py:98
  13.1 1.9 %collective-permute-start = (s32[128]{0:T(128)}, s32[128]{0:T(128)S(1)}, u32[]{:S(2)}, u32[]{:S(2)}) collective-permute-start(s32[128]{0:T(128)} %param.9), channel_id=1, source_target_pairs={{0,1},{1,0},{2,3},{3,2},{4,5},{5,4},{6,7},{7,6},{8,9},{9,8},{10,11... | collective-permute-start | bytes 1544 | tf_op jit(solution)/shard_map/ppermute | solution.py:99
  15.3 1.0 collective-permute-done
  16.2 1.3 copy-done
  18.2 1.3 shard_map.111
  19.5 1.9 %collective-permute-start.3 = (bf16[64,5376]{1,0:T(8,128)(2,1)S(1)}, bf16[64,5376]{1,0:T(8,128)(2,1)S(1)}, u32[]{:S(2)}, u32[]{:S(2)}) collective-permute-start(bf16[64,5376]{1,0:T(8,128)(2,1)S(1)} %get-tuple-element.9), channel_id=1, source_target_pairs={{0,22},{1,3},{2,0},{3,5},{4,2},{5,7},{6,4},{7,9},{8,6},{9,11},{10,... | collective-permute-start | bytes 2064392 | tf_op jit(solution)/shard_map/ppermute | solution.py:117
  21.4 5.3 %collective-permute-start.2 = (bf16[64,5376]{1,0:T(8,128)(2,1)S(1)}, bf16[64,5376]{1,0:T(8,128)(2,1)S(1)}, u32[]{:S(2)}, u32[]{:S(2)}) collective-permute-start(bf16[64,5376]{1,0:T(8,128)(2,1)S(1)} %get-tuple-element.8), channel_id=1, source_target_pairs={{0,2},{1,23},{2,4},{3,1},{4,6},{5,3},{6,8},{7,5},{8,10},{9,7},{10,... | collective-permute-start | bytes 2064392 | tf_op jit(solution)/shard_map/ppermute | solution.py:116
  26.9 8.2 %collective-permute-done.3 = bf16[64,5376]{1,0:T(8,128)(2,1)S(1)} collective-permute-done((bf16[64,5376]{1,0:T(8,128)(2,1)S(1)}, bf16[64,5376]{1,0:T(8,128)(2,1)S(1)}, u32[]{:S(2)}, u32[]{:S(2)}) %collective-permute-start.3) | collective-permute-done | bytes 688160 | tf_op jit(solution)/shard_map/ppermute | solution.py:117
  35.2 5.5 %collective-permute-done.2 = bf16[64,5376]{1,0:T(8,128)(2,1)S(1)} collective-permute-done((bf16[64,5376]{1,0:T(8,128)(2,1)S(1)}, bf16[64,5376]{1,0:T(8,128)(2,1)S(1)}, u32[]{:S(2)}, u32[]{:S(2)}) %collective-permute-start.2) | collective-permute-done | bytes 688160 | tf_op jit(solution)/shard_map/ppermute | solution.py:116
  41.0 1.9 %collective-permute-start.6 = (bf16[16,5376]{1,0:T(8,128)(2,1)S(1)}, bf16[16,5376]{1,0:T(8,128)(2,1)S(1)}, u32[]{:S(2)}, u32[]{:S(2)}) collective-permute-start(bf16[16,5376]{1,0:T(8,128)(2,1)S(1)} %get-tuple-element.16), channel_id=1, source_target_pairs={{0,18},{1,7},{2,20},{3,9},{4,22},{5,11},{6,0},{7,13},{8,2},{9,15},... | collective-permute-start | bytes 516104 | tf_op jit(solution)/shard_map/ppermute | solution.py:126
  42.9 8.0 %collective-permute-start.5 = (bf16[16,5376]{1,0:T(8,128)(2,1)S(1)}, bf16[16,5376]{1,0:T(8,128)(2,1)S(1)}, u32[]{:S(2)}, u32[]{:S(2)}) collective-permute-start(bf16[16,5376]{1,0:T(8,128)(2,1)S(1)} %get-tuple-element.17), channel_id=1, source_target_pairs={{0,12},{1,13},{2,14},{3,15},{4,16},{5,17},{6,18},{7,19},{8,20},{9,... | collective-permute-start | bytes 516104 | tf_op jit(solution)/shard_map/ppermute | solution.py:126
  50.9 2.2 %collective-permute-start.4 = (bf16[16,5376]{1,0:T(8,128)(2,1)S(1)}, bf16[16,5376]{1,0:T(8,128)(2,1)S(1)}, u32[]{:S(2)}, u32[]{:S(2)}) collective-permute-start(bf16[16,5376]{1,0:T(8,128)(2,1)S(1)} %get-tuple-element.15), channel_id=1, source_target_pairs={{0,6},{1,19},{2,8},{3,21},{4,10},{5,23},{6,12},{7,1},{8,14},{9,3},... | collective-permute-start | bytes 516104 | tf_op jit(solution)/shard_map/ppermute | solution.py:126
  53.2 6.5 %collective-permute-done.5 = bf16[16,5376]{1,0:T(8,128)(2,1)S(1)} collective-permute-done((bf16[16,5376]{1,0:T(8,128)(2,1)S(1)}, bf16[16,5376]{1,0:T(8,128)(2,1)S(1)}, u32[]{:S(2)}, u32[]{:S(2)}) %collective-permute-start.5) | collective-permute-done | bytes 172064 | tf_op jit(solution)/shard_map/ppermute | solution.py:126
  59.6 5.4 %collective-permute-done.4 = bf16[16,5376]{1,0:T(8,128)(2,1)S(1)} collective-permute-done((bf16[16,5376]{1,0:T(8,128)(2,1)S(1)}, bf16[16,5376]{1,0:T(8,128)(2,1)S(1)}, u32[]{:S(2)}, u32[]{:S(2)}) %collective-permute-start.4) | collective-permute-done | bytes 172064 | tf_op jit(solution)/shard_map/ppermute | solution.py:126
  65.4 1.1 reshape.68
  66.5 9.7 %all-to-all-start = ((bf16[32,2,5376]{2,1,0:T(2,128)(2,1)}), bf16[32,2,5376]{2,1,0:T(2,128)(2,1)S(1)}, u32[]{:S(2)}, u32[]{:S(2)}) async-start(bf16[32,2,5376]{2,1,0:T(2,128)(2,1)} %reshape.68), calls=%async_computation | async-start | bytes 1376256 | tf_op jit(solution)/shard_map/all_to_all | solution.py:140
  76.5 14.4 %all-to-all-done = bf16[32,2,5376]{2,1,0:T(2,128)(2,1)S(1)} async-done(((bf16[32,2,5376]{2,1,0:T(2,128)(2,1)}), bf16[32,2,5376]{2,1,0:T(2,128)(2,1)S(1)}, u32[]{:S(2)}, u32[]{:S(2)}) %all-to-all-start) | async-done | bytes 688160 | tf_op jit(solution)/shard_map/all_to_all | solution.py:140
  91.2 1.2 fusion.2
  92.8 1.1 reshape.70
  93.9 6.6 %all-to-all-start.1 = ((bf16[32,2,5376]{2,1,0:T(2,128)(2,1)}), bf16[32,2,5376]{2,1,0:T(2,128)(2,1)S(1)}, u32[]{:S(2)}, u32[]{:S(2)}) async-start(bf16[32,2,5376]{2,1,0:T(2,128)(2,1)} %reshape.70), calls=%async_computation.1 | async-start | bytes 1376256 | tf_op jit(solution)/shard_map/all_to_all | solution.py:140
  100.6 13.9 %all-to-all-done.1 = bf16[32,2,5376]{2,1,0:T(2,128)(2,1)S(1)} async-done(((bf16[32,2,5376]{2,1,0:T(2,128)(2,1)}), bf16[32,2,5376]{2,1,0:T(2,128)(2,1)S(1)}, u32[]{:S(2)}, u32[]{:S(2)}) %all-to-all-start.1) | async-done | bytes 688160 | tf_op jit(solution)/shard_map/all_to_all | solution.py:140
  115.0 35.9 %all_gather.3 = bf16[64,5376]{1,0:T(8,128)(2,1)S(1)} all-gather(bf16[16,5376]{1,0:T(8,128)(2,1)S(1)} %convolution_convert_fusion.2), channel_id=1, replica_groups={{0,6,12,18},{2,8,14,20},{4,10,16,22},{1,7,13,19},{3,9,15,21},{5,11,17,2..., dimensions={0}, use_global_device_ids=true | all-gather | bytes 860160 | tf_op jit(solution)/shard_map/all_gather | solution.py:159
  150.9 2.1 %collective-permute-start.11 = (bf16[64,2688]{1,0:T(8,128)(2,1)S(1)}, bf16[64,2688]{1,0:T(8,128)(2,1)S(1)}, u32[]{:S(2)}, u32[]{:S(2)}) collective-permute-start(bf16[64,2688]{1,0:T(8,128)(2,1)S(1)} %get-tuple-element.14), channel_id=1, source_target_pairs={{0,2},{1,23},{2,4},{3,1},{4,6},{5,3},{6,8},{7,5},{8,10},{9,7},{10,... | collective-permute-start | bytes 1032200 | tf_op jit(solution)/shard_map/ppermute | solution.py:167
  153.1 4.4 %collective-permute-start.10 = (bf16[64,2688]{1,0:T(8,128)(2,1)S(1)}, bf16[64,2688]{1,0:T(8,128)(2,1)S(1)}, u32[]{:S(2)}, u32[]{:S(2)}) collective-permute-start(bf16[64,2688]{1,0:T(8,128)(2,1)S(1)} %get-tuple-element.14), channel_id=1, source_target_pairs={{0,22},{1,3},{2,0},{3,5},{4,2},{5,7},{6,4},{7,9},{8,6},{9,11},{10,... | collective-permute-start | bytes 1032200 | tf_op jit(solution)/shard_map/ppermute | solution.py:166
  157.5 3.9 %collective-permute-start.8 = (bf16[64,2688]{1,0:T(8,128)(2,1)S(1)}, bf16[64,2688]{1,0:T(8,128)(2,1)S(1)}, u32[]{:S(2)}, u32[]{:S(2)}) collective-permute-start(bf16[64,2688]{1,0:T(8,128)(2,1)S(1)} %get-tuple-element.13), channel_id=1, source_target_pairs={{0,2},{1,23},{2,4},{3,1},{4,6},{5,3},{6,8},{7,5},{8,10},{9,7},{10,... | collective-permute-start | bytes 1032200 | tf_op jit(solution)/shard_map/ppermute | solution.py:167
  161.4 1.9 %collective-permute-start.7 = (bf16[64,2688]{1,0:T(8,128)(2,1)S(1)}, bf16[64,2688]{1,0:T(8,128)(2,1)S(1)}, u32[]{:S(2)}, u32[]{:S(2)}) collective-permute-start(bf16[64,2688]{1,0:T(8,128)(2,1)S(1)} %get-tuple-element.13), channel_id=1, source_target_pairs={{0,22},{1,3},{2,0},{3,5},{4,2},{5,7},{6,4},{7,9},{8,6},{9,11},{10,... | collective-permute-start | bytes 1032200 | tf_op jit(solution)/shard_map/ppermute | solution.py:166
  163.4 2.3 %collective-permute-done.10 = bf16[64,2688]{1,0:T(8,128)(2,1)S(1)} collective-permute-done((bf16[64,2688]{1,0:T(8,128)(2,1)S(1)}, bf16[64,2688]{1,0:T(8,128)(2,1)S(1)}, u32[]{:S(2)}, u32[]{:S(2)}) %collective-permute-start.10) | collective-permute-done | bytes 344096 | tf_op jit(solution)/shard_map/ppermute | solution.py:166
  166.1 6.1 %collective-permute-start.12 = (bf16[128,2688]{1,0:T(8,128)(2,1)S(1)}, bf16[128,2688]{1,0:T(8,128)(2,1)S(1)}, u32[]{:S(2)}, u32[]{:S(2)}) collective-permute-start(bf16[128,2688]{1,0:T(8,128)(2,1)S(1)} %convolution_convert_fusion.3), channel_id=1, source_target_pairs={{0,1},{1,0},{2,3},{3,2},{4,5},{5,4},{6,7},{7,6},{8,9},{9,8},{10,11... | collective-permute-start | bytes 2064392 | tf_op jit(solution)/shard_map/ppermute | solution.py:175
  172.2 1.8 collective-permute-done.7
  174.4 2.9 %collective-permute-start.9 = (bf16[128,2688]{1,0:T(8,128)(2,1)S(1)}, bf16[128,2688]{1,0:T(8,128)(2,1)S(1)}, u32[]{:S(2)}, u32[]{:S(2)}) collective-permute-start(bf16[128,2688]{1,0:T(8,128)(2,1)S(1)} %convolution_convert_fusion.5), channel_id=1, source_target_pairs={{0,1},{1,0},{2,3},{3,2},{4,5},{5,4},{6,7},{7,6},{8,9},{9,8},{10,11... | collective-permute-start | bytes 2064392 | tf_op jit(solution)/shard_map/ppermute | solution.py:175
  178.3 0.7 collective-permute-done.9
  179.2 1.2 pad_maximum_fusion
  (53 shorter events, 5.2 us)
Async XLA Ops:
  0.6 15.6 %collective-permute-start.1 = (bf16[128,5376]{1,0:T(8,128)(2,1)}, bf16[128,5376]{1,0:T(8,128)(2,1)S(1)}, u32[]{:S(2)}, u32[]{:S(2)}) collective-permute-start(bf16[128,5376]{1,0:T(8,128)(2,1)} %own_ref.1), channel_id=1, source_target_pairs={{0,1},{1,0},{2,3},{3,2},{4,5},{5,4},{6,7},{7,6},{8,9},{9,8},{10,11... | collective-permute-start | bytes 4128776 | tf_op jit(solution)/shard_map/ppermute | solution.py:98
  13.1 3.2 %collective-permute-start = (s32[128]{0:T(128)}, s32[128]{0:T(128)S(1)}, u32[]{:S(2)}, u32[]{:S(2)}) collective-permute-start(s32[128]{0:T(128)} %param.9), channel_id=1, source_target_pairs={{0,1},{1,0},{2,3},{3,2},{4,5},{5,4},{6,7},{7,6},{8,9},{9,8},{10,11... | collective-permute-start | bytes 1544 | tf_op jit(solution)/shard_map/ppermute | solution.py:99
  16.2 1.3 copy-start
  17.6 0.7 copy-start.1
  18.2 8.5 %copy-start.9 = (s32[1,16]{1,0:T(1,128)S(1)}, s32[1,16]{1,0:T(1,128)}, u32[]{:S(2)}) copy-start(s32[1,16]{1,0:T(1,128)} %param.10) | copy-start | bytes 196
  19.5 15.7 %collective-permute-start.3 = (bf16[64,5376]{1,0:T(8,128)(2,1)S(1)}, bf16[64,5376]{1,0:T(8,128)(2,1)S(1)}, u32[]{:S(2)}, u32[]{:S(2)}) collective-permute-start(bf16[64,5376]{1,0:T(8,128)(2,1)S(1)} %get-tuple-element.9), channel_id=1, source_target_pairs={{0,22},{1,3},{2,0},{3,5},{4,2},{5,7},{6,4},{7,9},{8,6},{9,11},{10,... | collective-permute-start | bytes 2064392 | tf_op jit(solution)/shard_map/ppermute | solution.py:117
  21.4 19.3 %collective-permute-start.2 = (bf16[64,5376]{1,0:T(8,128)(2,1)S(1)}, bf16[64,5376]{1,0:T(8,128)(2,1)S(1)}, u32[]{:S(2)}, u32[]{:S(2)}) collective-permute-start(bf16[64,5376]{1,0:T(8,128)(2,1)S(1)} %get-tuple-element.8), channel_id=1, source_target_pairs={{0,2},{1,23},{2,4},{3,1},{4,6},{5,3},{6,8},{7,5},{8,10},{9,7},{10,... | collective-permute-start | bytes 2064392 | tf_op jit(solution)/shard_map/ppermute | solution.py:116
  41.0 12.2 %collective-permute-start.6 = (bf16[16,5376]{1,0:T(8,128)(2,1)S(1)}, bf16[16,5376]{1,0:T(8,128)(2,1)S(1)}, u32[]{:S(2)}, u32[]{:S(2)}) collective-permute-start(bf16[16,5376]{1,0:T(8,128)(2,1)S(1)} %get-tuple-element.16), channel_id=1, source_target_pairs={{0,18},{1,7},{2,20},{3,9},{4,22},{5,11},{6,0},{7,13},{8,2},{9,15},... | collective-permute-start | bytes 516104 | tf_op jit(solution)/shard_map/ppermute | solution.py:126
  42.9 16.7 %collective-permute-start.5 = (bf16[16,5376]{1,0:T(8,128)(2,1)S(1)}, bf16[16,5376]{1,0:T(8,128)(2,1)S(1)}, u32[]{:S(2)}, u32[]{:S(2)}) collective-permute-start(bf16[16,5376]{1,0:T(8,128)(2,1)S(1)} %get-tuple-element.17), channel_id=1, source_target_pairs={{0,12},{1,13},{2,14},{3,15},{4,16},{5,17},{6,18},{7,19},{8,20},{9,... | collective-permute-start | bytes 516104 | tf_op jit(solution)/shard_map/ppermute | solution.py:126
  50.9 14.2 %collective-permute-start.4 = (bf16[16,5376]{1,0:T(8,128)(2,1)S(1)}, bf16[16,5376]{1,0:T(8,128)(2,1)S(1)}, u32[]{:S(2)}, u32[]{:S(2)}) collective-permute-start(bf16[16,5376]{1,0:T(8,128)(2,1)S(1)} %get-tuple-element.15), channel_id=1, source_target_pairs={{0,6},{1,19},{2,8},{3,21},{4,10},{5,23},{6,12},{7,1},{8,14},{9,3},... | collective-permute-start | bytes 516104 | tf_op jit(solution)/shard_map/ppermute | solution.py:126
  65.4 10.9 %copy-start.4 = (s32[1,32,2]{1,2,0:T(2,128)S(1)}, s32[1,32,2]{1,2,0:T(2,128)}, u32[]{:S(2)}) copy-start(s32[1,32,2]{1,2,0:T(2,128)} %param.12) | copy-start | bytes 772
  65.4 11.1 %copy-start.8 = (s32[16]{0:T(128)S(1)}, s32[16]{0:T(128)}, u32[]{:S(2)}) copy-start(s32[16]{0:T(128)} %param.11) | copy-start | bytes 196
  66.5 24.6 %copy-start.5 = (f32[16,5376]{1,0:T(8,128)S(1)}, f32[16,5376]{1,0:T(8,128)}, u32[]{:S(2)}) copy-start(f32[16,5376]{1,0:T(8,128)} %param.14) | copy-start | bytes 1032196
  66.5 24.6 %copy-start.6 = (f32[16,5376]{1,0:T(8,128)S(1)}, f32[16,5376]{1,0:T(8,128)}, u32[]{:S(2)}) copy-start(f32[16,5376]{1,0:T(8,128)} %param.15) | copy-start | bytes 1032196
  66.5 24.7 %copy-start.7 = (f32[16,5376]{1,0:T(8,128)S(1)}, f32[16,5376]{1,0:T(8,128)}, u32[]{:S(2)}) copy-start(f32[16,5376]{1,0:T(8,128)} %param.13) | copy-start | bytes 1032196
  66.5 24.4 %all-to-all-start = ((bf16[32,2,5376]{2,1,0:T(2,128)(2,1)}), bf16[32,2,5376]{2,1,0:T(2,128)(2,1)S(1)}, u32[]{:S(2)}, u32[]{:S(2)}) async-start(bf16[32,2,5376]{2,1,0:T(2,128)(2,1)} %reshape.68), calls=%async_computation | async-start | bytes 1376256 | tf_op jit(solution)/shard_map/all_to_all | solution.py:140
  92.4 1.5 copy-start.3
  93.9 20.5 %all-to-all-start.1 = ((bf16[32,2,5376]{2,1,0:T(2,128)(2,1)}), bf16[32,2,5376]{2,1,0:T(2,128)(2,1)S(1)}, u32[]{:S(2)}, u32[]{:S(2)}) async-start(bf16[32,2,5376]{2,1,0:T(2,128)(2,1)} %reshape.70), calls=%async_computation.1 | async-start | bytes 1376256 | tf_op jit(solution)/shard_map/all_to_all | solution.py:140
  150.9 12.4 %collective-permute-start.11 = (bf16[64,2688]{1,0:T(8,128)(2,1)S(1)}, bf16[64,2688]{1,0:T(8,128)(2,1)S(1)}, u32[]{:S(2)}, u32[]{:S(2)}) collective-permute-start(bf16[64,2688]{1,0:T(8,128)(2,1)S(1)} %get-tuple-element.14), channel_id=1, source_target_pairs={{0,2},{1,23},{2,4},{3,1},{4,6},{5,3},{6,8},{7,5},{8,10},{9,7},{10,... | collective-permute-start | bytes 1032200 | tf_op jit(solution)/shard_map/ppermute | solution.py:167
  153.1 12.6 %collective-permute-start.10 = (bf16[64,2688]{1,0:T(8,128)(2,1)S(1)}, bf16[64,2688]{1,0:T(8,128)(2,1)S(1)}, u32[]{:S(2)}, u32[]{:S(2)}) collective-permute-start(bf16[64,2688]{1,0:T(8,128)(2,1)S(1)} %get-tuple-element.14), channel_id=1, source_target_pairs={{0,22},{1,3},{2,0},{3,5},{4,2},{5,7},{6,4},{7,9},{8,6},{9,11},{10,... | collective-permute-start | bytes 1032200 | tf_op jit(solution)/shard_map/ppermute | solution.py:166
  157.5 14.7 %collective-permute-start.8 = (bf16[64,2688]{1,0:T(8,128)(2,1)S(1)}, bf16[64,2688]{1,0:T(8,128)(2,1)S(1)}, u32[]{:S(2)}, u32[]{:S(2)}) collective-permute-start(bf16[64,2688]{1,0:T(8,128)(2,1)S(1)} %get-tuple-element.13), channel_id=1, source_target_pairs={{0,2},{1,23},{2,4},{3,1},{4,6},{5,3},{6,8},{7,5},{8,10},{9,7},{10,... | collective-permute-start | bytes 1032200 | tf_op jit(solution)/shard_map/ppermute | solution.py:167
  161.4 12.6 %collective-permute-start.7 = (bf16[64,2688]{1,0:T(8,128)(2,1)S(1)}, bf16[64,2688]{1,0:T(8,128)(2,1)S(1)}, u32[]{:S(2)}, u32[]{:S(2)}) collective-permute-start(bf16[64,2688]{1,0:T(8,128)(2,1)S(1)} %get-tuple-element.13), channel_id=1, source_target_pairs={{0,22},{1,3},{2,0},{3,5},{4,2},{5,7},{6,4},{7,9},{8,6},{9,11},{10,... | collective-permute-start | bytes 1032200 | tf_op jit(solution)/shard_map/ppermute | solution.py:166
  166.1 11.2 %copy-start.2 = (s32[128]{0:T(128)S(1)}, s32[128]{0:T(128)}, u32[]{:S(2)}) copy-start(s32[128]{0:T(128)} %param.9) | copy-start | bytes 1540
  166.1 12.0 %collective-permute-start.12 = (bf16[128,2688]{1,0:T(8,128)(2,1)S(1)}, bf16[128,2688]{1,0:T(8,128)(2,1)S(1)}, u32[]{:S(2)}, u32[]{:S(2)}) collective-permute-start(bf16[128,2688]{1,0:T(8,128)(2,1)S(1)} %convolution_convert_fusion.3), channel_id=1, source_target_pairs={{0,1},{1,0},{2,3},{3,2},{4,5},{5,4},{6,7},{7,6},{8,9},{9,8},{10,11... | collective-permute-start | bytes 2064392 | tf_op jit(solution)/shard_map/ppermute | solution.py:175
  174.4 4.6 %collective-permute-start.9 = (bf16[128,2688]{1,0:T(8,128)(2,1)S(1)}, bf16[128,2688]{1,0:T(8,128)(2,1)S(1)}, u32[]{:S(2)}, u32[]{:S(2)}) collective-permute-start(bf16[128,2688]{1,0:T(8,128)(2,1)S(1)} %convolution_convert_fusion.5), channel_id=1, source_target_pairs={{0,1},{1,0},{2,3},{3,2},{4,5},{5,4},{6,7},{7,6},{8,9},{9,8},{10,11... | collective-permute-start | bytes 2064392 | tf_op jit(solution)/shard_map/ppermute | solution.py:175

commit v7 on v6

--- a/solution.py
+++ b/solution.py
@@ -16,6 +16,7 @@
 EPSILON = 1e-08
 
 X_SIZE, Y_SIZE, Z_SIZE, CORES = 4, 8, 12, 2
+SUM_APART = 4
 APART = 3
 GROUP = Z_SIZE // APART
 GROUPS = [[r + APART * k for k in range(GROUP)] for r in range(APART)]
@@ -61,25 +62,27 @@
     rows = rows_ref[...]
     own = (rows == own_slot_ref[...]).astype(jnp.bfloat16)
     other = (rows == other_slot_ref[...]).astype(jnp.bfloat16)
-    part = rows.shape[0] // len(out_refs)
     for start in range(0, own_ref.shape[1], BLOCK_COLS):
         at = pl.ds(start, BLOCK_COLS)
         total = dot32(own, own_ref[:, at]) + dot32(other, other_ref[:, at])
-        for i, out_ref in enumerate(out_refs):
-            out_ref[:, at] = total[i * part : (i + 1) * part].astype(out_ref.dtype)
-
-
-def slot_sums(rows, own_slot, other_slot, own, other, parts):
-    height, count, width = rows.shape[0], own.shape[0], own.shape[1]
+        first = 0
+        for out_ref in out_refs:
+            height = out_ref.shape[0]
+            out_ref[:, at] = total[first : first + height].astype(out_ref.dtype)
+            first += height
+
+
+def slot_sums(rows, own_slot, other_slot, own, other, heights):
+    count, width = own.shape
     in_vmem = pl.BlockSpec(memory_space=pltpu.VMEM)
     return pl.pallas_call(
         sum_kernel,
         in_specs=[in_vmem] * 5,
-        out_specs=[in_vmem] * parts,
-        out_shape=[jax.ShapeDtypeStruct((height // parts, width), jnp.bfloat16)] * parts,
+        out_specs=[in_vmem] * len(heights),
+        out_shape=[jax.ShapeDtypeStruct((height, width), jnp.bfloat16) for height in heights],
         cost_estimate=pl.CostEstimate(
-            flops=4 * height * count * width,
-            bytes_accessed=2 * (2 * count + height) * width,
+            flops=4 * rows.shape[0] * count * width,
+            bytes_accessed=2 * (2 * count + rows.shape[0]) * width,
             transcendentals=0,
         ),
         compiler_params=pltpu.CompilerParams(vmem_limit_bytes=16 * 2**20),
@@ -100,31 +103,42 @@
 
     ahead = 1 - 2 * core
 
-    def rows_of(shift, first_here):
-        row = lax.iota(jnp.int32, GROUP * slot_dev)
-        member = lax.div(row, slot_dev) * APART
-        if first_here:
-            z_of_row = lax.rem(place + shift + ahead * member + 2 * Z_SIZE, Z_SIZE)
-        else:
-            z_of_row = lax.rem(place + shift + APART, APART) + member
-        return (z_of_row * CORES + core) * slot_dev + lax.rem(row, slot_dev)
-
-    summed = jnp.concatenate([rows_of(shift, True) for shift in (0, ahead, -ahead)])
-    kept, for_ahead, for_behind = slot_sums(
-        summed, token_slot, other_slot, grads, other_grads, 3
-    )
-    from_behind = lax.ppermute(for_ahead, ("z", "c"), neighbour(1))
-    from_ahead = lax.ppermute(for_behind, ("z", "c"), neighbour(-1))
-    near = (
-        kept.astype(jnp.float32)
-        + from_behind.astype(jnp.float32)
-        + from_ahead.astype(jnp.float32)
-    ).astype(jnp.bfloat16)
-    blocks = [near[i * slot_dev : (i + 1) * slot_dev] for i in range(GROUP)]
-    total = blocks[0].astype(jnp.float32)
-    for i in range(1, GROUP):
-        total += lax.ppermute(blocks[i], ("z", "c"), neighbour(i * APART)).astype(jnp.float32)
-    node_sum = total.astype(jnp.bfloat16)
+    def rows_at(z_of_row):
+        k = lax.rem(lax.iota(jnp.int32, z_of_row.shape[0]), slot_dev)
+        return (z_of_row * CORES + core) * slot_dev + k
+
+    def hub_rows(shift):
+        block = lax.div(lax.iota(jnp.int32, Z_SIZE // SUM_APART * slot_dev), slot_dev)
+        steps = shift + SUM_APART * block
+        return rows_at(lax.rem(place + ahead * steps + 2 * Z_SIZE, Z_SIZE))
+
+    def group_rows(shift):
+        block = lax.div(lax.iota(jnp.int32, GROUP * slot_dev), slot_dev)
+        return rows_at(lax.rem(place + ahead * shift + APART, APART) + APART * block)
+
+    def send(rows, steps):
+        return lax.ppermute(rows, ("z", "c"), neighbour(steps))
+
+    def add(*terms):
+        return sum(term.astype(jnp.float32) for term in terms)
+
+    summed = jnp.concatenate([hub_rows(shift) for shift in (0, 1, -1, 2)])
+    stay, move = slot_dev, (Z_SIZE // SUM_APART - 1) * slot_dev
+    parts = slot_sums(summed, token_slot, other_slot, grads, other_grads, [stay, move] * 4)
+    here, next_hub, last_hub, far_hub = zip(parts[::2], parts[1::2])
+
+    def at_hub(part):
+        relayed = send(far_hub[part], 1)
+        from_ahead = send(last_hub[part], -1)
+        from_behind = send(add(next_hub[part], relayed).astype(jnp.bfloat16), 1)
+        return add(here[part], from_ahead, from_behind)
+
+    moving = at_hub(1).astype(jnp.bfloat16)
+    arrived = [
+        send(moving[i * slot_dev : (i + 1) * slot_dev], (i + 1) * SUM_APART)
+        for i in range(move // slot_dev)
+    ]
+    node_sum = add(at_hub(0), *arrived).astype(jnp.bfloat16)
 
     owner_node = node_ids[0] // (VOCAB // node_count)
     same_owner = owner_node[:, None] == owner_node[None, :]
@@ -147,14 +161,14 @@
 
     incoming = exchange(dot32(matches(send_places, send_slot), node_sum))
     gradient = dot32(matches(touched_places, position_map), incoming)
-    moment_out, second_out, master_out = adam_rows(
-        gradient, moment, second, master, touched_ids >= 0
-    )
-    fresh_rows = master_out.astype(jnp.bfloat16)
+    alive = touched_ids >= 0
+    fresh_rows = adam_rows(gradient, moment, second, master, alive)[2].astype(jnp.bfloat16)
+    states = adam_rows(lax.optimization_barrier(gradient), moment, second, master, alive)
     returned = exchange(dot32(matches(position_map, touched_places), fresh_rows))
+    returned, moment_out, second_out, master_out = lax.optimization_barrier((returned, *states))
     rows = dot32(matches(send_slot, send_places), returned).astype(jnp.bfloat16)
 
-    listed = jnp.concatenate([rows_of(shift, False) for shift in (0, ahead, -ahead)])
+    listed = jnp.concatenate([group_rows(shift) for shift in (0, 1, -1)])
 
     here = lax.all_gather(rows, "z", axis=0, tiled=True, axis_index_groups=GROUPS)
     own_choice, other_choice = matches(token_slot, listed), matches(other_slot, listed)
@@ -163,8 +177,8 @@
     arrived = [
         (
             half,
-            lax.ppermute(half, ("z", "c"), neighbour(-1)),
-            lax.ppermute(half, ("z", "c"), neighbour(1)),
+            send(half, -1),
+            send(half, 1),
         )
         for half in halves
     ]

time: 181 us -> 174 us (0.961)
  waiting for transfers between devices: 59.7 us -> 51.8 us
  starting transfers between devices: 71.3 us -> 78.6 us
  blocking collectives: 35.9 us -> 28.9 us
    ppermute x9 -> x12, waiting for transfers between devices: 29.7 us -> 21.4 us  [send(): return lax.ppermute(rows, ('z', 'c'), neighbour(steps))]
    ppermute x9 -> x12, starting transfers between devices: 31.6 us -> 39.9 us  [send(): return lax.ppermute(rows, ('z', 'c'), neighbour(steps))]
    all_gather x1, blocking collectives: 35.9 us -> 28.9 us  [on_device(): lax.all_gather(rows, 'z', axis=0, tiled=True, axis_index_groups=GROUPS)]
    ppermute x2, starting transfers between devices: 8.97 us -> 6.84 us  [on_device(): lax.ppermute(theirs, 'c', SWAP)]
  transfers between devices with their start and end apart: 15 -> 18, of which waited for: 10 -> 9; matrix products, arithmetic and copies ran while one was open for 1% -> 2% of each run, Pallas kernels for 0% -> 0%
where the time goes in v7:
time: 174 us; the launch traced here: 173 us
  starting transfers between devices  78.6 us (45%)
  waiting for transfers between devices  51.8 us (30%)
  blocking collectives  28.9 us (17%)
  local copies, waits for them, and re-layouts  5.15 us (3%)
  other arithmetic  3.36 us (2%)
  matrix products  2.87 us (2%)
    ppermute x12, starting transfers between devices, send(): return lax.ppermute(rows, ('z', 'c'), neighbour(steps))  39.9 us
    all_gather x1, blocking collectives, on_device(): lax.all_gather(rows, 'z', axis=0, tiled=True, axis_index_groups=GROUPS)  28.9 us
    all_to_all x2, waiting for transfers between devices, exchange(): lax.all_to_all(rows.astype(jnp.bfloat16).reshape(node_count, capacity, wi...  28.7 us
    ppermute x12, waiting for transfers between devices, send(): return lax.ppermute(rows, ('z', 'c'), neighbour(steps))  21.4 us
    all_to_all x2, starting transfers between devices, exchange(): lax.all_to_all(rows.astype(jnp.bfloat16).reshape(node_count, capacity, wi...  17.5 us
    ppermute x1, starting transfers between devices, on_device(): other_grads = lax.ppermute(grads, 'c', SWAP)  12.4 us
    ppermute x2, starting transfers between devices, on_device(): lax.ppermute(theirs, 'c', SWAP)  6.84 us
  transfers between devices with their start and end apart: 18, of which 9 were waited for; matrix products, arithmetic and copies ran while one was open for 2% of the time, Pallas kernels for 0%

profile of v7, /device:TPU:1, one launch (start us, length us, event | category | flops | bytes accessed | tf_op | source)
XLA Modules:
  0.0 173.1 jit_solution(13297997041289073151)
XLA Ops:
  0.6 12.4 %collective-permute-start.1 = (bf16[128,5376]{1,0:T(8,128)(2,1)}, bf16[128,5376]{1,0:T(8,128)(2,1)S(1)}, u32[]{:S(2)}, u32[]{:S(2)}) collective-permute-start(bf16[128,5376]{1,0:T(8,128)(2,1)} %own_ref.1), channel_id=1, source_target_pairs={{0,1},{1,0},{2,3},{3,2},{4,5},{5,4},{6,7},{7,6},{8,9},{9,8},{10,11... | collective-permute-start | bytes 4128776 | tf_op jit(solution)/shard_map/ppermute | solution.py:101
  13.1 1.9 %collective-permute-start = (s32[128]{0:T(128)}, s32[128]{0:T(128)S(1)}, u32[]{:S(2)}, u32[]{:S(2)}) collective-permute-start(s32[128]{0:T(128)} %param.9), channel_id=1, source_target_pairs={{0,1},{1,0},{2,3},{3,2},{4,5},{5,4},{6,7},{7,6},{8,9},{9,8},{10,11... | collective-permute-start | bytes 1544 | tf_op jit(solution)/shard_map/ppermute | solution.py:102
  16.2 1.3 copy-done
  18.2 1.3 shard_map.111
  19.5 5.3 %collective-permute-start.6 = (bf16[32,5376]{1,0:T(8,128)(2,1)S(1)}, bf16[32,5376]{1,0:T(8,128)(2,1)S(1)}, u32[]{:S(2)}, u32[]{:S(2)}) collective-permute-start(bf16[32,5376]{1,0:T(8,128)(2,1)S(1)} %get-tuple-element.23), channel_id=1, source_target_pairs={{0,2},{1,23},{2,4},{3,1},{4,6},{5,3},{6,8},{7,5},{8,10},{9,7},{10,... | collective-permute-start | bytes 1032200 | tf_op jit(solution)/shard_map/ppermute | solution.py:120
  25.0 1.9 %collective-permute-start.5 = (bf16[32,5376]{1,0:T(8,128)(2,1)S(1)}, bf16[32,5376]{1,0:T(8,128)(2,1)S(1)}, u32[]{:S(2)}, u32[]{:S(2)}) collective-permute-start(bf16[32,5376]{1,0:T(8,128)(2,1)S(1)} %get-tuple-element.21), channel_id=1, source_target_pairs={{0,22},{1,3},{2,0},{3,5},{4,2},{5,7},{6,4},{7,9},{8,6},{9,11},{10,... | collective-permute-start | bytes 1032200 | tf_op jit(solution)/shard_map/ppermute | solution.py:120
  26.9 4.6 %collective-permute-start.3 = (bf16[16,5376]{1,0:T(8,128)(2,1)S(1)}, bf16[16,5376]{1,0:T(8,128)(2,1)S(1)}, u32[]{:S(2)}, u32[]{:S(2)}) collective-permute-start(bf16[16,5376]{1,0:T(8,128)(2,1)S(1)} %get-tuple-element.19), channel_id=1, source_target_pairs={{0,2},{1,23},{2,4},{3,1},{4,6},{5,3},{6,8},{7,5},{8,10},{9,7},{10,... | collective-permute-start | bytes 516104 | tf_op jit(solution)/shard_map/ppermute | solution.py:120
  31.5 1.9 %collective-permute-start.2 = (bf16[16,5376]{1,0:T(8,128)(2,1)S(1)}, bf16[16,5376]{1,0:T(8,128)(2,1)S(1)}, u32[]{:S(2)}, u32[]{:S(2)}) collective-permute-start(bf16[16,5376]{1,0:T(8,128)(2,1)S(1)} %get-tuple-element.17), channel_id=1, source_target_pairs={{0,22},{1,3},{2,0},{3,5},{4,2},{5,7},{6,4},{7,9},{8,6},{9,11},{10,... | collective-permute-start | bytes 516104 | tf_op jit(solution)/shard_map/ppermute | solution.py:120
  33.6 4.6 %collective-permute-start.7 = (bf16[32,5376]{1,0:T(8,128)(2,1)S(1)}, bf16[32,5376]{1,0:T(8,128)(2,1)S(1)}, u32[]{:S(2)}, u32[]{:S(2)}) collective-permute-start(bf16[32,5376]{1,0:T(8,128)(2,1)S(1)} %add_convert_fusion.1), channel_id=1, source_target_pairs={{0,2},{1,23},{2,4},{3,1},{4,6},{5,3},{6,8},{7,5},{8,10},{9,7},{10,... | collective-permute-start | bytes 1032200 | tf_op jit(solution)/shard_map/ppermute | solution.py:120
  38.2 1.9 %collective-permute-start.4 = (bf16[16,5376]{1,0:T(8,128)(2,1)S(1)}, bf16[16,5376]{1,0:T(8,128)(2,1)S(1)}, u32[]{:S(2)}, u32[]{:S(2)}) collective-permute-start(bf16[16,5376]{1,0:T(8,128)(2,1)S(1)} %add_convert_fusion.3), channel_id=1, source_target_pairs={{0,2},{1,23},{2,4},{3,1},{4,6},{5,3},{6,8},{7,5},{8,10},{9,7},{10,... | collective-permute-start | bytes 516104 | tf_op jit(solution)/shard_map/ppermute | solution.py:120
  40.1 2.2 %collective-permute-done.7 = bf16[32,5376]{1,0:T(8,128)(2,1)S(1)} collective-permute-done((bf16[32,5376]{1,0:T(8,128)(2,1)S(1)}, bf16[32,5376]{1,0:T(8,128)(2,1)S(1)}, u32[]{:S(2)}, u32[]{:S(2)}) %collective-permute-start.7) | collective-permute-done | bytes 344096 | tf_op jit(solution)/shard_map/ppermute | solution.py:120
  42.5 1.9 %collective-permute-start.9 = (bf16[16,5376]{1,0:T(8,128)(2,1)S(1)}, bf16[16,5376]{1,0:T(8,128)(2,1)S(1)}, u32[]{:S(2)}, u32[]{:S(2)}) collective-permute-start(bf16[16,5376]{1,0:T(8,128)(2,1)S(1)} %get-tuple-element.34), channel_id=1, source_target_pairs={{0,16},{1,9},{2,18},{3,11},{4,20},{5,13},{6,22},{7,15},{8,0},{9,17... | collective-permute-start | bytes 516104 | tf_op jit(solution)/shard_map/ppermute | solution.py:120
  44.4 7.3 %collective-permute-start.8 = (bf16[16,5376]{1,0:T(8,128)(2,1)S(1)}, bf16[16,5376]{1,0:T(8,128)(2,1)S(1)}, u32[]{:S(2)}, u32[]{:S(2)}) collective-permute-start(bf16[16,5376]{1,0:T(8,128)(2,1)S(1)} %get-tuple-element.33), channel_id=1, source_target_pairs={{0,8},{1,17},{2,10},{3,19},{4,12},{5,21},{6,14},{7,23},{8,16},{9,1... | collective-permute-start | bytes 516104 | tf_op jit(solution)/shard_map/ppermute | solution.py:120
  51.7 2.6 %collective-permute-done.9 = bf16[16,5376]{1,0:T(8,128)(2,1)S(1)} collective-permute-done((bf16[16,5376]{1,0:T(8,128)(2,1)S(1)}, bf16[16,5376]{1,0:T(8,128)(2,1)S(1)}, u32[]{:S(2)}, u32[]{:S(2)}) %collective-permute-start.9) | collective-permute-done | bytes 172064 | tf_op jit(solution)/shard_map/ppermute | solution.py:120
  54.3 10.1 %collective-permute-done.8 = bf16[16,5376]{1,0:T(8,128)(2,1)S(1)} collective-permute-done((bf16[16,5376]{1,0:T(8,128)(2,1)S(1)}, bf16[16,5376]{1,0:T(8,128)(2,1)S(1)}, u32[]{:S(2)}, u32[]{:S(2)}) %collective-permute-start.8) | collective-permute-done | bytes 172064 | tf_op jit(solution)/shard_map/ppermute | solution.py:120
  64.8 1.1 reshape.68
  65.9 9.7 %all-to-all-start = ((bf16[32,2,5376]{2,1,0:T(2,128)(2,1)}), bf16[32,2,5376]{2,1,0:T(2,128)(2,1)S(1)}, u32[]{:S(2)}, u32[]{:S(2)}) async-start(bf16[32,2,5376]{2,1,0:T(2,128)(2,1)} %reshape.68), calls=%async_computation | async-start | bytes 1376256 | tf_op jit(solution)/shard_map/all_to_all | solution.py:154
  75.8 15.5 %all-to-all-done = bf16[32,2,5376]{2,1,0:T(2,128)(2,1)S(1)} async-done(((bf16[32,2,5376]{2,1,0:T(2,128)(2,1)}), bf16[32,2,5376]{2,1,0:T(2,128)(2,1)S(1)}, u32[]{:S(2)}, u32[]{:S(2)}) %all-to-all-start) | async-done | bytes 688160 | tf_op jit(solution)/shard_map/all_to_all | solution.py:154
  92.3 1.1 reshape.70
  93.4 7.8 %all-to-all-start.1 = ((bf16[32,2,5376]{2,1,0:T(2,128)(2,1)}), bf16[32,2,5376]{2,1,0:T(2,128)(2,1)S(1)}, u32[]{:S(2)}, u32[]{:S(2)}) async-start(bf16[32,2,5376]{2,1,0:T(2,128)(2,1)} %reshape.70), calls=%async_computation.1 | async-start | bytes 1376256 | tf_op jit(solution)/shard_map/all_to_all | solution.py:154
  101.2 1.1 subtract_select_fusion
  102.3 13.3 %all-to-all-done.1 = bf16[32,2,5376]{2,1,0:T(2,128)(2,1)S(1)} async-done(((bf16[32,2,5376]{2,1,0:T(2,128)(2,1)}), bf16[32,2,5376]{2,1,0:T(2,128)(2,1)S(1)}, u32[]{:S(2)}, u32[]{:S(2)}) %all-to-all-start.1) | async-done | bytes 688160 | tf_op jit(solution)/shard_map/all_to_all | solution.py:154
  116.1 28.9 %all_gather.3 = bf16[64,5376]{1,0:T(8,128)(2,1)S(1)} all-gather(bf16[16,5376]{1,0:T(8,128)(2,1)S(1)} %convolution_convert_fusion.2), channel_id=1, replica_groups={{0,6,12,18},{2,8,14,20},{4,10,16,22},{1,7,13,19},{3,9,15,21},{5,11,17,2..., dimensions={0}, use_global_device_ids=true | all-gather | bytes 860160 | tf_op jit(solution)/shard_map/all_gather | solution.py:173
  145.1 1.9 %collective-permute-start.14 = (bf16[64,2688]{1,0:T(8,128)(2,1)S(1)}, bf16[64,2688]{1,0:T(8,128)(2,1)S(1)}, u32[]{:S(2)}, u32[]{:S(2)}) collective-permute-start(bf16[64,2688]{1,0:T(8,128)(2,1)S(1)} %get-tuple-element.32), channel_id=1, source_target_pairs={{0,2},{1,23},{2,4},{3,1},{4,6},{5,3},{6,8},{7,5},{8,10},{9,7},{10,... | collective-permute-start | bytes 1032200 | tf_op jit(solution)/shard_map/ppermute | solution.py:120
  147.0 3.4 %collective-permute-start.13 = (bf16[64,2688]{1,0:T(8,128)(2,1)S(1)}, bf16[64,2688]{1,0:T(8,128)(2,1)S(1)}, u32[]{:S(2)}, u32[]{:S(2)}) collective-permute-start(bf16[64,2688]{1,0:T(8,128)(2,1)S(1)} %get-tuple-element.32), channel_id=1, source_target_pairs={{0,22},{1,3},{2,0},{3,5},{4,2},{5,7},{6,4},{7,9},{8,6},{9,11},{10,... | collective-permute-start | bytes 1032200 | tf_op jit(solution)/shard_map/ppermute | solution.py:120
  150.4 3.1 %collective-permute-start.11 = (bf16[64,2688]{1,0:T(8,128)(2,1)S(1)}, bf16[64,2688]{1,0:T(8,128)(2,1)S(1)}, u32[]{:S(2)}, u32[]{:S(2)}) collective-permute-start(bf16[64,2688]{1,0:T(8,128)(2,1)S(1)} %get-tuple-element.31), channel_id=1, source_target_pairs={{0,2},{1,23},{2,4},{3,1},{4,6},{5,3},{6,8},{7,5},{8,10},{9,7},{10,... | collective-permute-start | bytes 1032200 | tf_op jit(solution)/shard_map/ppermute | solution.py:120
  153.6 2.2 %collective-permute-start.10 = (bf16[64,2688]{1,0:T(8,128)(2,1)S(1)}, bf16[64,2688]{1,0:T(8,128)(2,1)S(1)}, u32[]{:S(2)}, u32[]{:S(2)}) collective-permute-start(bf16[64,2688]{1,0:T(8,128)(2,1)S(1)} %get-tuple-element.31), channel_id=1, source_target_pairs={{0,22},{1,3},{2,0},{3,5},{4,2},{5,7},{6,4},{7,9},{8,6},{9,11},{10,... | collective-permute-start | bytes 1032200 | tf_op jit(solution)/shard_map/ppermute | solution.py:120
  155.8 4.4 %collective-permute-done.13 = bf16[64,2688]{1,0:T(8,128)(2,1)S(1)} collective-permute-done((bf16[64,2688]{1,0:T(8,128)(2,1)S(1)}, bf16[64,2688]{1,0:T(8,128)(2,1)S(1)}, u32[]{:S(2)}, u32[]{:S(2)}) %collective-permute-start.13) | collective-permute-done | bytes 344096 | tf_op jit(solution)/shard_map/ppermute | solution.py:120
  160.6 4.5 %collective-permute-start.15 = (bf16[128,2688]{1,0:T(8,128)(2,1)S(1)}, bf16[128,2688]{1,0:T(8,128)(2,1)S(1)}, u32[]{:S(2)}, u32[]{:S(2)}) collective-permute-start(bf16[128,2688]{1,0:T(8,128)(2,1)S(1)} %convolution_convert_fusion.3), channel_id=1, source_target_pairs={{0,1},{1,0},{2,3},{3,2},{4,5},{5,4},{6,7},{7,6},{8,9},{9,8},{10,11... | collective-permute-start | bytes 2064392 | tf_op jit(solution)/shard_map/ppermute | solution.py:189
  165.1 2.1 %collective-permute-done.10 = bf16[64,2688]{1,0:T(8,128)(2,1)S(1)} collective-permute-done((bf16[64,2688]{1,0:T(8,128)(2,1)S(1)}, bf16[64,2688]{1,0:T(8,128)(2,1)S(1)}, u32[]{:S(2)}, u32[]{:S(2)}) %collective-permute-start.10) | collective-permute-done | bytes 344096 | tf_op jit(solution)/shard_map/ppermute | solution.py:120
  167.7 2.3 %collective-permute-start.12 = (bf16[128,2688]{1,0:T(8,128)(2,1)S(1)}, bf16[128,2688]{1,0:T(8,128)(2,1)S(1)}, u32[]{:S(2)}, u32[]{:S(2)}) collective-permute-start(bf16[128,2688]{1,0:T(8,128)(2,1)S(1)} %convolution_convert_fusion.5), channel_id=1, source_target_pairs={{0,1},{1,0},{2,3},{3,2},{4,5},{5,4},{6,7},{7,6},{8,9},{9,8},{10,11... | collective-permute-start | bytes 2064392 | tf_op jit(solution)/shard_map/ppermute | solution.py:189
  171.9 1.2 pad_maximum_fusion
  (60 shorter events, 7.2 us)
Async XLA Ops:
  0.6 15.6 %collective-permute-start.1 = (bf16[128,5376]{1,0:T(8,128)(2,1)}, bf16[128,5376]{1,0:T(8,128)(2,1)S(1)}, u32[]{:S(2)}, u32[]{:S(2)}) collective-permute-start(bf16[128,5376]{1,0:T(8,128)(2,1)} %own_ref.1), channel_id=1, source_target_pairs={{0,1},{1,0},{2,3},{3,2},{4,5},{5,4},{6,7},{7,6},{8,9},{9,8},{10,11... | collective-permute-start | bytes 4128776 | tf_op jit(solution)/shard_map/ppermute | solution.py:101
  13.1 3.2 %collective-permute-start = (s32[128]{0:T(128)}, s32[128]{0:T(128)S(1)}, u32[]{:S(2)}, u32[]{:S(2)}) collective-permute-start(s32[128]{0:T(128)} %param.9), channel_id=1, source_target_pairs={{0,1},{1,0},{2,3},{3,2},{4,5},{5,4},{6,7},{7,6},{8,9},{9,8},{10,11... | collective-permute-start | bytes 1544 | tf_op jit(solution)/shard_map/ppermute | solution.py:102
  16.2 1.3 copy-start
  17.6 0.7 copy-start.1
  18.2 6.6 %copy-start.8 = (s32[1,16]{1,0:T(1,128)S(1)}, s32[1,16]{1,0:T(1,128)}, u32[]{:S(2)}) copy-start(s32[1,16]{1,0:T(1,128)} %param.10) | copy-start | bytes 196
  19.5 14.0 %collective-permute-start.6 = (bf16[32,5376]{1,0:T(8,128)(2,1)S(1)}, bf16[32,5376]{1,0:T(8,128)(2,1)S(1)}, u32[]{:S(2)}, u32[]{:S(2)}) collective-permute-start(bf16[32,5376]{1,0:T(8,128)(2,1)S(1)} %get-tuple-element.23), channel_id=1, source_target_pairs={{0,2},{1,23},{2,4},{3,1},{4,6},{5,3},{6,8},{7,5},{8,10},{9,7},{10,... | collective-permute-start | bytes 1032200 | tf_op jit(solution)/shard_map/ppermute | solution.py:120
  25.0 15.1 %collective-permute-start.5 = (bf16[32,5376]{1,0:T(8,128)(2,1)S(1)}, bf16[32,5376]{1,0:T(8,128)(2,1)S(1)}, u32[]{:S(2)}, u32[]{:S(2)}) collective-permute-start(bf16[32,5376]{1,0:T(8,128)(2,1)S(1)} %get-tuple-element.21), channel_id=1, source_target_pairs={{0,22},{1,3},{2,0},{3,5},{4,2},{5,7},{6,4},{7,9},{8,6},{9,11},{10,... | collective-permute-start | bytes 1032200 | tf_op jit(solution)/shard_map/ppermute | solution.py:120
  26.9 11.2 %collective-permute-start.3 = (bf16[16,5376]{1,0:T(8,128)(2,1)S(1)}, bf16[16,5376]{1,0:T(8,128)(2,1)S(1)}, u32[]{:S(2)}, u32[]{:S(2)}) collective-permute-start(bf16[16,5376]{1,0:T(8,128)(2,1)S(1)} %get-tuple-element.19), channel_id=1, source_target_pairs={{0,2},{1,23},{2,4},{3,1},{4,6},{5,3},{6,8},{7,5},{8,10},{9,7},{10,... | collective-permute-start | bytes 516104 | tf_op jit(solution)/shard_map/ppermute | solution.py:120
  31.5 20.2 %collective-permute-start.2 = (bf16[16,5376]{1,0:T(8,128)(2,1)S(1)}, bf16[16,5376]{1,0:T(8,128)(2,1)S(1)}, u32[]{:S(2)}, u32[]{:S(2)}) collective-permute-start(bf16[16,5376]{1,0:T(8,128)(2,1)S(1)} %get-tuple-element.17), channel_id=1, source_target_pairs={{0,22},{1,3},{2,0},{3,5},{4,2},{5,7},{6,4},{7,9},{8,6},{9,11},{10,... | collective-permute-start | bytes 516104 | tf_op jit(solution)/shard_map/ppermute | solution.py:120
  33.6 8.8 %collective-permute-start.7 = (bf16[32,5376]{1,0:T(8,128)(2,1)S(1)}, bf16[32,5376]{1,0:T(8,128)(2,1)S(1)}, u32[]{:S(2)}, u32[]{:S(2)}) collective-permute-start(bf16[32,5376]{1,0:T(8,128)(2,1)S(1)} %add_convert_fusion.1), channel_id=1, source_target_pairs={{0,2},{1,23},{2,4},{3,1},{4,6},{5,3},{6,8},{7,5},{8,10},{9,7},{10,... | collective-permute-start | bytes 1032200 | tf_op jit(solution)/shard_map/ppermute | solution.py:120
  38.2 13.5 %collective-permute-start.4 = (bf16[16,5376]{1,0:T(8,128)(2,1)S(1)}, bf16[16,5376]{1,0:T(8,128)(2,1)S(1)}, u32[]{:S(2)}, u32[]{:S(2)}) collective-permute-start(bf16[16,5376]{1,0:T(8,128)(2,1)S(1)} %add_convert_fusion.3), channel_id=1, source_target_pairs={{0,2},{1,23},{2,4},{3,1},{4,6},{5,3},{6,8},{7,5},{8,10},{9,7},{10,... | collective-permute-start | bytes 516104 | tf_op jit(solution)/shard_map/ppermute | solution.py:120
  42.5 11.9 %collective-permute-start.9 = (bf16[16,5376]{1,0:T(8,128)(2,1)S(1)}, bf16[16,5376]{1,0:T(8,128)(2,1)S(1)}, u32[]{:S(2)}, u32[]{:S(2)}) collective-permute-start(bf16[16,5376]{1,0:T(8,128)(2,1)S(1)} %get-tuple-element.34), channel_id=1, source_target_pairs={{0,16},{1,9},{2,18},{3,11},{4,20},{5,13},{6,22},{7,15},{8,0},{9,17... | collective-permute-start | bytes 516104 | tf_op jit(solution)/shard_map/ppermute | solution.py:120
  44.4 20.0 %collective-permute-start.8 = (bf16[16,5376]{1,0:T(8,128)(2,1)S(1)}, bf16[16,5376]{1,0:T(8,128)(2,1)S(1)}, u32[]{:S(2)}, u32[]{:S(2)}) collective-permute-start(bf16[16,5376]{1,0:T(8,128)(2,1)S(1)} %get-tuple-element.33), channel_id=1, source_target_pairs={{0,8},{1,17},{2,10},{3,19},{4,12},{5,21},{6,14},{7,23},{8,16},{9,1... | collective-permute-start | bytes 516104 | tf_op jit(solution)/shard_map/ppermute | solution.py:120
  64.8 10.8 %copy-start.6 = (s32[1,32,2]{1,2,0:T(2,128)S(1)}, s32[1,32,2]{1,2,0:T(2,128)}, u32[]{:S(2)}) copy-start(s32[1,32,2]{1,2,0:T(2,128)} %param.12) | copy-start | bytes 772
  64.8 11.0 %copy-start.7 = (s32[16]{0:T(128)S(1)}, s32[16]{0:T(128)}, u32[]{:S(2)}) copy-start(s32[16]{0:T(128)} %param.11) | copy-start | bytes 196
  65.9 25.4 %all-to-all-start = ((bf16[32,2,5376]{2,1,0:T(2,128)(2,1)}), bf16[32,2,5376]{2,1,0:T(2,128)(2,1)S(1)}, u32[]{:S(2)}, u32[]{:S(2)}) async-start(bf16[32,2,5376]{2,1,0:T(2,128)(2,1)} %reshape.68), calls=%async_computation | async-start | bytes 1376256 | tf_op jit(solution)/shard_map/all_to_all | solution.py:154
  75.6 16.2 %copy-start.3 = (f32[16,5376]{1,0:T(8,128)S(1)}, f32[16,5376]{1,0:T(8,128)}, u32[]{:S(2)}) copy-start(f32[16,5376]{1,0:T(8,128)} %param.15) | copy-start | bytes 1032196
  75.6 16.2 %copy-start.4 = (f32[16,5376]{1,0:T(8,128)S(1)}, f32[16,5376]{1,0:T(8,128)}, u32[]{:S(2)}) copy-start(f32[16,5376]{1,0:T(8,128)} %param.14) | copy-start | bytes 1032196
  75.6 16.2 %copy-start.5 = (f32[16,5376]{1,0:T(8,128)S(1)}, f32[16,5376]{1,0:T(8,128)}, u32[]{:S(2)}) copy-start(f32[16,5376]{1,0:T(8,128)} %param.13) | copy-start | bytes 1032196
  93.4 22.2 %all-to-all-start.1 = ((bf16[32,2,5376]{2,1,0:T(2,128)(2,1)}), bf16[32,2,5376]{2,1,0:T(2,128)(2,1)S(1)}, u32[]{:S(2)}, u32[]{:S(2)}) async-start(bf16[32,2,5376]{2,1,0:T(2,128)(2,1)} %reshape.70), calls=%async_computation.1 | async-start | bytes 1376256 | tf_op jit(solution)/shard_map/all_to_all | solution.py:154
  145.1 10.7 %collective-permute-start.14 = (bf16[64,2688]{1,0:T(8,128)(2,1)S(1)}, bf16[64,2688]{1,0:T(8,128)(2,1)S(1)}, u32[]{:S(2)}, u32[]{:S(2)}) collective-permute-start(bf16[64,2688]{1,0:T(8,128)(2,1)S(1)} %get-tuple-element.32), channel_id=1, source_target_pairs={{0,2},{1,23},{2,4},{3,1},{4,6},{5,3},{6,8},{7,5},{8,10},{9,7},{10,... | collective-permute-start | bytes 1032200 | tf_op jit(solution)/shard_map/ppermute | solution.py:120
  147.0 13.2 %collective-permute-start.13 = (bf16[64,2688]{1,0:T(8,128)(2,1)S(1)}, bf16[64,2688]{1,0:T(8,128)(2,1)S(1)}, u32[]{:S(2)}, u32[]{:S(2)}) collective-permute-start(bf16[64,2688]{1,0:T(8,128)(2,1)S(1)} %get-tuple-element.32), channel_id=1, source_target_pairs={{0,22},{1,3},{2,0},{3,5},{4,2},{5,7},{6,4},{7,9},{8,6},{9,11},{10,... | collective-permute-start | bytes 1032200 | tf_op jit(solution)/shard_map/ppermute | solution.py:120
  150.4 14.7 %collective-permute-start.11 = (bf16[64,2688]{1,0:T(8,128)(2,1)S(1)}, bf16[64,2688]{1,0:T(8,128)(2,1)S(1)}, u32[]{:S(2)}, u32[]{:S(2)}) collective-permute-start(bf16[64,2688]{1,0:T(8,128)(2,1)S(1)} %get-tuple-element.31), channel_id=1, source_target_pairs={{0,2},{1,23},{2,4},{3,1},{4,6},{5,3},{6,8},{7,5},{8,10},{9,7},{10,... | collective-permute-start | bytes 1032200 | tf_op jit(solution)/shard_map/ppermute | solution.py:120
  153.6 13.7 %collective-permute-start.10 = (bf16[64,2688]{1,0:T(8,128)(2,1)S(1)}, bf16[64,2688]{1,0:T(8,128)(2,1)S(1)}, u32[]{:S(2)}, u32[]{:S(2)}) collective-permute-start(bf16[64,2688]{1,0:T(8,128)(2,1)S(1)} %get-tuple-element.31), channel_id=1, source_target_pairs={{0,22},{1,3},{2,0},{3,5},{4,2},{5,7},{6,4},{7,9},{8,6},{9,11},{10,... | collective-permute-start | bytes 1032200 | tf_op jit(solution)/shard_map/ppermute | solution.py:120
  160.6 9.4 %copy-start.2 = (s32[128]{0:T(128)S(1)}, s32[128]{0:T(128)}, u32[]{:S(2)}) copy-start(s32[128]{0:T(128)} %param.9) | copy-start | bytes 1540
  160.6 10.2 %collective-permute-start.15 = (bf16[128,2688]{1,0:T(8,128)(2,1)S(1)}, bf16[128,2688]{1,0:T(8,128)(2,1)S(1)}, u32[]{:S(2)}, u32[]{:S(2)}) collective-permute-start(bf16[128,2688]{1,0:T(8,128)(2,1)S(1)} %convolution_convert_fusion.3), channel_id=1, source_target_pairs={{0,1},{1,0},{2,3},{3,2},{4,5},{5,4},{6,7},{7,6},{8,9},{9,8},{10,11... | collective-permute-start | bytes 2064392 | tf_op jit(solution)/shard_map/ppermute | solution.py:189
  167.7 4.1 %collective-permute-start.12 = (bf16[128,2688]{1,0:T(8,128)(2,1)S(1)}, bf16[128,2688]{1,0:T(8,128)(2,1)S(1)}, u32[]{:S(2)}, u32[]{:S(2)}) collective-permute-start(bf16[128,2688]{1,0:T(8,128)(2,1)S(1)} %convolution_convert_fusion.5), channel_id=1, source_target_pairs={{0,1},{1,0},{2,3},{3,2},{4,5},{5,4},{6,7},{7,6},{8,9},{9,8},{10,11... | collective-permute-start | bytes 2064392 | tf_op jit(solution)/shard_map/ppermute | solution.py:189

commit v8 on v7

--- a/solution.py
+++ b/solution.py
@@ -127,18 +127,19 @@
     parts = slot_sums(summed, token_slot, other_slot, grads, other_grads, [stay, move] * 4)
     here, next_hub, last_hub, far_hub = zip(parts[::2], parts[1::2])
 
-    def at_hub(part):
-        relayed = send(far_hub[part], 1)
-        from_ahead = send(last_hub[part], -1)
-        from_behind = send(add(next_hub[part], relayed).astype(jnp.bfloat16), 1)
-        return add(here[part], from_ahead, from_behind)
-
-    moving = at_hub(1).astype(jnp.bfloat16)
-    arrived = [
-        send(moving[i * slot_dev : (i + 1) * slot_dev], (i + 1) * SUM_APART)
-        for i in range(move // slot_dev)
-    ]
-    node_sum = add(at_hub(0), *arrived).astype(jnp.bfloat16)
+    relayed = send(far_hub[1], 1)
+    from_ahead = send(last_hub[1], -1)
+    relay_sum = add(next_hub[1], relayed).astype(jnp.bfloat16)
+    relay_sum, held_back = lax.optimization_barrier((relay_sum, last_hub[0]))
+    from_behind = send(relay_sum, 1)
+    terms = []
+    for i in range(move // slot_dev):
+        at = slice(i * slot_dev, (i + 1) * slot_dev)
+        block = add(here[1][at], from_ahead[at], from_behind[at]).astype(jnp.bfloat16)
+        terms.append(send(block, (i + 1) * SUM_APART))
+    terms += [here[0], send(held_back, -1)]
+    terms.append(send(add(next_hub[0], send(far_hub[0], 1)).astype(jnp.bfloat16), 1))
+    node_sum = add(*terms).astype(jnp.bfloat16)
 
     owner_node = node_ids[0] // (VOCAB // node_count)
     same_owner = owner_node[:, None] == owner_node[None, :]

time: 174 us -> 173 us (level)
  starting transfers between devices: 78.6 us -> 88.3 us
  blocking collectives: 28.9 us -> 21.1 us
  waiting for transfers between devices: 51.8 us -> 47.4 us
    all_gather x1, blocking collectives: 28.9 us -> 21.1 us  [on_device(): lax.all_gather(rows, 'z', axis=0, tiled=True, axis_index_groups=GROUPS)]
    ppermute x12, starting transfers between devices: 39.9 us -> 46.4 us  [send(): return lax.ppermute(rows, ('z', 'c'), neighbour(steps))]
    ppermute x2, starting transfers between devices: 6.84 us -> 11.2 us  [on_device(): lax.ppermute(theirs, 'c', SWAP)]
    ppermute x12, waiting for transfers between devices: 21.4 us -> 17.4 us  [send(): return lax.ppermute(rows, ('z', 'c'), neighbour(steps))]
  transfers between devices with their start and end apart: 18 -> 18, of which waited for: 9 -> 8; matrix products, arithmetic and copies ran while one was open for 2% -> 2% of each run, Pallas kernels for 0% -> 0%
where the time goes in v8:
time: 173 us; the launch traced here: 171 us
  starting transfers between devices  88.3 us (51%)
  waiting for transfers between devices  47.4 us (27%)
  blocking collectives  21.1 us (12%)
  local copies, waits for them, and re-layouts  5.13 us (3%)
  other arithmetic  3.36 us (2%)
  matrix products  2.87 us (2%)
    ppermute x12, starting transfers between devices, send(): return lax.ppermute(rows, ('z', 'c'), neighbour(steps))  46.4 us
    all_to_all x2, waiting for transfers between devices, exchange(): lax.all_to_all(rows.astype(jnp.bfloat16).reshape(node_count, capacity, wi...  28.3 us
    all_gather x1, blocking collectives, on_device(): lax.all_gather(rows, 'z', axis=0, tiled=True, axis_index_groups=GROUPS)  21.1 us
    ppermute x12, waiting for transfers between devices, send(): return lax.ppermute(rows, ('z', 'c'), neighbour(steps))  17.4 us
    all_to_all x2, starting transfers between devices, exchange(): lax.all_to_all(rows.astype(jnp.bfloat16).reshape(node_count, capacity, wi...  16.3 us
    ppermute x1, starting transfers between devices, on_device(): other_grads = lax.ppermute(grads, 'c', SWAP)  12.4 us
    ppermute x2, starting transfers between devices, on_device(): lax.ppermute(theirs, 'c', SWAP)  11.2 us
  transfers between devices with their start and end apart: 18, of which 8 were waited for; matrix products, arithmetic and copies ran while one was open for 2% of the time, Pallas kernels for 0%

profile of v8, /device:TPU:1, one launch (start us, length us, event | category | flops | bytes accessed | tf_op | source)
XLA Modules:
  0.0 170.6 jit_solution(7050918195432854386)
XLA Ops:
  0.6 12.4 %collective-permute-start.1 = (bf16[128,5376]{1,0:T(8,128)(2,1)}, bf16[128,5376]{1,0:T(8,128)(2,1)S(1)}, u32[]{:S(2)}, u32[]{:S(2)}) collective-permute-start(bf16[128,5376]{1,0:T(8,128)(2,1)} %own_ref.1), channel_id=1, source_target_pairs={{0,1},{1,0},{2,3},{3,2},{4,5},{5,4},{6,7},{7,6},{8,9},{9,8},{10,11... | collective-permute-start | bytes 4128776 | tf_op jit(solution)/shard_map/ppermute | solution.py:101
  13.1 1.9 %collective-permute-start = (s32[128]{0:T(128)}, s32[128]{0:T(128)S(1)}, u32[]{:S(2)}, u32[]{:S(2)}) collective-permute-start(s32[128]{0:T(128)} %param.9), channel_id=1, source_target_pairs={{0,1},{1,0},{2,3},{3,2},{4,5},{5,4},{6,7},{7,6},{8,9},{9,8},{10,11... | collective-permute-start | bytes 1544 | tf_op jit(solution)/shard_map/ppermute | solution.py:102
  15.3 1.0 collective-permute-done
  16.2 1.3 copy-done
  18.2 1.3 shard_map.111
  19.5 5.3 %collective-permute-start.3 = (bf16[32,5376]{1,0:T(8,128)(2,1)S(1)}, bf16[32,5376]{1,0:T(8,128)(2,1)S(1)}, u32[]{:S(2)}, u32[]{:S(2)}) collective-permute-start(bf16[32,5376]{1,0:T(8,128)(2,1)S(1)} %get-tuple-element.21), channel_id=1, source_target_pairs={{0,2},{1,23},{2,4},{3,1},{4,6},{5,3},{6,8},{7,5},{8,10},{9,7},{10,... | collective-permute-start | bytes 1032200 | tf_op jit(solution)/shard_map/ppermute | solution.py:120
  25.0 2.2 %collective-permute-start.8 = (bf16[16,5376]{1,0:T(8,128)(2,1)S(1)}, bf16[16,5376]{1,0:T(8,128)(2,1)S(1)}, u32[]{:S(2)}, u32[]{:S(2)}) collective-permute-start(bf16[16,5376]{1,0:T(8,128)(2,1)S(1)} %get-tuple-element.27), channel_id=1, source_target_pairs={{0,2},{1,23},{2,4},{3,1},{4,6},{5,3},{6,8},{7,5},{8,10},{9,7},{10,... | collective-permute-start | bytes 516104 | tf_op jit(solution)/shard_map/ppermute | solution.py:120
  27.2 3.1 %collective-permute-start.2 = (bf16[32,5376]{1,0:T(8,128)(2,1)S(1)}, bf16[32,5376]{1,0:T(8,128)(2,1)S(1)}, u32[]{:S(2)}, u32[]{:S(2)}) collective-permute-start(bf16[32,5376]{1,0:T(8,128)(2,1)S(1)} %get-tuple-element.19), channel_id=1, source_target_pairs={{0,22},{1,3},{2,0},{3,5},{4,2},{5,7},{6,4},{7,9},{8,6},{9,11},{10,... | collective-permute-start | bytes 1032200 | tf_op jit(solution)/shard_map/ppermute | solution.py:120
  30.4 3.7 %collective-permute-start.4 = (bf16[32,5376]{1,0:T(8,128)(2,1)S(1)}, bf16[32,5376]{1,0:T(8,128)(2,1)S(1)}, u32[]{:S(2)}, u32[]{:S(2)}) collective-permute-start(bf16[32,5376]{1,0:T(8,128)(2,1)S(1)} %add_convert_fusion), channel_id=1, source_target_pairs={{0,2},{1,23},{2,4},{3,1},{4,6},{5,3},{6,8},{7,5},{8,10},{9,7},{10,... | collective-permute-start | bytes 1032200 | tf_op jit(solution)/shard_map/ppermute | solution.py:120
  34.1 2.7 %collective-permute-start.9 = (bf16[16,5376]{1,0:T(8,128)(2,1)S(1)}, bf16[16,5376]{1,0:T(8,128)(2,1)S(1)}, u32[]{:S(2)}, u32[]{:S(2)}) collective-permute-start(bf16[16,5376]{1,0:T(8,128)(2,1)S(1)} %add_convert_fusion.2), channel_id=1, source_target_pairs={{0,2},{1,23},{2,4},{3,1},{4,6},{5,3},{6,8},{7,5},{8,10},{9,7},{10,... | collective-permute-start | bytes 516104 | tf_op jit(solution)/shard_map/ppermute | solution.py:120
  36.9 2.5 %collective-permute-start.7 = (bf16[16,5376]{1,0:T(8,128)(2,1)S(1)}, bf16[16,5376]{1,0:T(8,128)(2,1)S(1)}, u32[]{:S(2)}, u32[]{:S(2)}) collective-permute-start(bf16[16,5376]{1,0:T(8,128)(2,1)S(1)} %get-tuple-element.25), channel_id=1, source_target_pairs={{0,22},{1,3},{2,0},{3,5},{4,2},{5,7},{6,4},{7,9},{8,6},{9,11},{10,... | collective-permute-start | bytes 516104 | tf_op jit(solution)/shard_map/ppermute | solution.py:120
  39.6 3.2 %collective-permute-start.6 = (bf16[16,5376]{1,0:T(8,128)(2,1)S(1)}, bf16[16,5376]{1,0:T(8,128)(2,1)S(1)}, u32[]{:S(2)}, u32[]{:S(2)}) collective-permute-start(bf16[16,5376]{1,0:T(8,128)(2,1)S(1)} %get-tuple-element.33), channel_id=1, source_target_pairs={{0,16},{1,9},{2,18},{3,11},{4,20},{5,13},{6,22},{7,15},{8,0},{9,17... | collective-permute-start | bytes 516104 | tf_op jit(solution)/shard_map/ppermute | solution.py:120
  42.8 6.0 %collective-permute-start.5 = (bf16[16,5376]{1,0:T(8,128)(2,1)S(1)}, bf16[16,5376]{1,0:T(8,128)(2,1)S(1)}, u32[]{:S(2)}, u32[]{:S(2)}) collective-permute-start(bf16[16,5376]{1,0:T(8,128)(2,1)S(1)} %get-tuple-element.32), channel_id=1, source_target_pairs={{0,8},{1,17},{2,10},{3,19},{4,12},{5,21},{6,14},{7,23},{8,16},{9,1... | collective-permute-start | bytes 516104 | tf_op jit(solution)/shard_map/ppermute | solution.py:120
  48.9 3.0 %collective-permute-done.6 = bf16[16,5376]{1,0:T(8,128)(2,1)S(1)} collective-permute-done((bf16[16,5376]{1,0:T(8,128)(2,1)S(1)}, bf16[16,5376]{1,0:T(8,128)(2,1)S(1)}, u32[]{:S(2)}, u32[]{:S(2)}) %collective-permute-start.6) | collective-permute-done | bytes 172064 | tf_op jit(solution)/shard_map/ppermute | solution.py:120
  51.8 11.9 %collective-permute-done.5 = bf16[16,5376]{1,0:T(8,128)(2,1)S(1)} collective-permute-done((bf16[16,5376]{1,0:T(8,128)(2,1)S(1)}, bf16[16,5376]{1,0:T(8,128)(2,1)S(1)}, u32[]{:S(2)}, u32[]{:S(2)}) %collective-permute-start.5) | collective-permute-done | bytes 172064 | tf_op jit(solution)/shard_map/ppermute | solution.py:120
  64.1 1.1 reshape.68
  65.2 8.2 %all-to-all-start = ((bf16[32,2,5376]{2,1,0:T(2,128)(2,1)}), bf16[32,2,5376]{2,1,0:T(2,128)(2,1)S(1)}, u32[]{:S(2)}, u32[]{:S(2)}) async-start(bf16[32,2,5376]{2,1,0:T(2,128)(2,1)} %reshape.68), calls=%async_computation | async-start | bytes 1376256 | tf_op jit(solution)/shard_map/all_to_all | solution.py:155
  73.7 15.1 %all-to-all-done = bf16[32,2,5376]{2,1,0:T(2,128)(2,1)S(1)} async-done(((bf16[32,2,5376]{2,1,0:T(2,128)(2,1)}), bf16[32,2,5376]{2,1,0:T(2,128)(2,1)S(1)}, u32[]{:S(2)}, u32[]{:S(2)}) %all-to-all-start) | async-done | bytes 688160 | tf_op jit(solution)/shard_map/all_to_all | solution.py:155
  89.7 1.1 reshape.70
  90.8 8.1 %all-to-all-start.1 = ((bf16[32,2,5376]{2,1,0:T(2,128)(2,1)}), bf16[32,2,5376]{2,1,0:T(2,128)(2,1)S(1)}, u32[]{:S(2)}, u32[]{:S(2)}) async-start(bf16[32,2,5376]{2,1,0:T(2,128)(2,1)} %reshape.70), calls=%async_computation.1 | async-start | bytes 1376256 | tf_op jit(solution)/shard_map/all_to_all | solution.py:155
  99.0 1.1 subtract_select_fusion
  100.1 13.2 %all-to-all-done.1 = bf16[32,2,5376]{2,1,0:T(2,128)(2,1)S(1)} async-done(((bf16[32,2,5376]{2,1,0:T(2,128)(2,1)}), bf16[32,2,5376]{2,1,0:T(2,128)(2,1)S(1)}, u32[]{:S(2)}, u32[]{:S(2)}) %all-to-all-start.1) | async-done | bytes 688160 | tf_op jit(solution)/shard_map/all_to_all | solution.py:155
  113.9 21.1 %all_gather.3 = bf16[64,5376]{1,0:T(8,128)(2,1)S(1)} all-gather(bf16[16,5376]{1,0:T(8,128)(2,1)S(1)} %convolution_convert_fusion.2), channel_id=1, replica_groups={{0,6,12,18},{2,8,14,20},{4,10,16,22},{1,7,13,19},{3,9,15,21},{5,11,17,2..., dimensions={0}, use_global_device_ids=true | all-gather | bytes 860160 | tf_op jit(solution)/shard_map/all_gather | solution.py:174
  135.1 7.6 %collective-permute-start.14 = (bf16[64,2688]{1,0:T(8,128)(2,1)S(1)}, bf16[64,2688]{1,0:T(8,128)(2,1)S(1)}, u32[]{:S(2)}, u32[]{:S(2)}) collective-permute-start(bf16[64,2688]{1,0:T(8,128)(2,1)S(1)} %get-tuple-element.38), channel_id=1, source_target_pairs={{0,2},{1,23},{2,4},{3,1},{4,6},{5,3},{6,8},{7,5},{8,10},{9,7},{10,... | collective-permute-start | bytes 1032200 | tf_op jit(solution)/shard_map/ppermute | solution.py:120
  142.7 4.8 %collective-permute-start.13 = (bf16[64,2688]{1,0:T(8,128)(2,1)S(1)}, bf16[64,2688]{1,0:T(8,128)(2,1)S(1)}, u32[]{:S(2)}, u32[]{:S(2)}) collective-permute-start(bf16[64,2688]{1,0:T(8,128)(2,1)S(1)} %get-tuple-element.38), channel_id=1, source_target_pairs={{0,22},{1,3},{2,0},{3,5},{4,2},{5,7},{6,4},{7,9},{8,6},{9,11},{10,... | collective-permute-start | bytes 1032200 | tf_op jit(solution)/shard_map/ppermute | solution.py:120
  147.6 2.8 %collective-permute-start.11 = (bf16[64,2688]{1,0:T(8,128)(2,1)S(1)}, bf16[64,2688]{1,0:T(8,128)(2,1)S(1)}, u32[]{:S(2)}, u32[]{:S(2)}) collective-permute-start(bf16[64,2688]{1,0:T(8,128)(2,1)S(1)} %get-tuple-element.37), channel_id=1, source_target_pairs={{0,2},{1,23},{2,4},{3,1},{4,6},{5,3},{6,8},{7,5},{8,10},{9,7},{10,... | collective-permute-start | bytes 1032200 | tf_op jit(solution)/shard_map/ppermute | solution.py:120
  150.3 2.5 %collective-permute-start.10 = (bf16[64,2688]{1,0:T(8,128)(2,1)S(1)}, bf16[64,2688]{1,0:T(8,128)(2,1)S(1)}, u32[]{:S(2)}, u32[]{:S(2)}) collective-permute-start(bf16[64,2688]{1,0:T(8,128)(2,1)S(1)} %get-tuple-element.37), channel_id=1, source_target_pairs={{0,22},{1,3},{2,0},{3,5},{4,2},{5,7},{6,4},{7,9},{8,6},{9,11},{10,... | collective-permute-start | bytes 1032200 | tf_op jit(solution)/shard_map/ppermute | solution.py:120
  152.9 2.1 %collective-permute-done.13 = bf16[64,2688]{1,0:T(8,128)(2,1)S(1)} collective-permute-done((bf16[64,2688]{1,0:T(8,128)(2,1)S(1)}, bf16[64,2688]{1,0:T(8,128)(2,1)S(1)}, u32[]{:S(2)}, u32[]{:S(2)}) %collective-permute-start.13) | collective-permute-done | bytes 344096 | tf_op jit(solution)/shard_map/ppermute | solution.py:120
  155.5 6.8 %collective-permute-start.15 = (bf16[128,2688]{1,0:T(8,128)(2,1)S(1)}, bf16[128,2688]{1,0:T(8,128)(2,1)S(1)}, u32[]{:S(2)}, u32[]{:S(2)}) collective-permute-start(bf16[128,2688]{1,0:T(8,128)(2,1)S(1)} %convolution_convert_fusion.3), channel_id=1, source_target_pairs={{0,1},{1,0},{2,3},{3,2},{4,5},{5,4},{6,7},{7,6},{8,9},{9,8},{10,11... | collective-permute-start | bytes 2064392 | tf_op jit(solution)/shard_map/ppermute | solution.py:190
  163.1 4.4 %collective-permute-start.12 = (bf16[128,2688]{1,0:T(8,128)(2,1)S(1)}, bf16[128,2688]{1,0:T(8,128)(2,1)S(1)}, u32[]{:S(2)}, u32[]{:S(2)}) collective-permute-start(bf16[128,2688]{1,0:T(8,128)(2,1)S(1)} %convolution_convert_fusion.5), channel_id=1, source_target_pairs={{0,1},{1,0},{2,3},{3,2},{4,5},{5,4},{6,7},{7,6},{8,9},{9,8},{10,11... | collective-permute-start | bytes 2064392 | tf_op jit(solution)/shard_map/ppermute | solution.py:190
  168.5 0.7 collective-permute-done.12
  169.4 1.2 pad_maximum_fusion
  (59 shorter events, 5.9 us)
Async XLA Ops:
  0.6 15.6 %collective-permute-start.1 = (bf16[128,5376]{1,0:T(8,128)(2,1)}, bf16[128,5376]{1,0:T(8,128)(2,1)S(1)}, u32[]{:S(2)}, u32[]{:S(2)}) collective-permute-start(bf16[128,5376]{1,0:T(8,128)(2,1)} %own_ref.1), channel_id=1, source_target_pairs={{0,1},{1,0},{2,3},{3,2},{4,5},{5,4},{6,7},{7,6},{8,9},{9,8},{10,11... | collective-permute-start | bytes 4128776 | tf_op jit(solution)/shard_map/ppermute | solution.py:101
  13.1 3.2 %collective-permute-start = (s32[128]{0:T(128)}, s32[128]{0:T(128)S(1)}, u32[]{:S(2)}, u32[]{:S(2)}) collective-permute-start(s32[128]{0:T(128)} %param.9), channel_id=1, source_target_pairs={{0,1},{1,0},{2,3},{3,2},{4,5},{5,4},{6,7},{7,6},{8,9},{9,8},{10,11... | collective-permute-start | bytes 1544 | tf_op jit(solution)/shard_map/ppermute | solution.py:102
  16.2 1.3 copy-start
  17.6 0.7 copy-start.1
  18.2 6.6 %copy-start.8 = (s32[1,16]{1,0:T(1,128)S(1)}, s32[1,16]{1,0:T(1,128)}, u32[]{:S(2)}) copy-start(s32[1,16]{1,0:T(1,128)} %param.10) | copy-start | bytes 196
  19.5 10.8 %collective-permute-start.3 = (bf16[32,5376]{1,0:T(8,128)(2,1)S(1)}, bf16[32,5376]{1,0:T(8,128)(2,1)S(1)}, u32[]{:S(2)}, u32[]{:S(2)}) collective-permute-start(bf16[32,5376]{1,0:T(8,128)(2,1)S(1)} %get-tuple-element.21), channel_id=1, source_target_pairs={{0,2},{1,23},{2,4},{3,1},{4,6},{5,3},{6,8},{7,5},{8,10},{9,7},{10,... | collective-permute-start | bytes 1032200 | tf_op jit(solution)/shard_map/ppermute | solution.py:120
  25.0 9.1 %collective-permute-start.8 = (bf16[16,5376]{1,0:T(8,128)(2,1)S(1)}, bf16[16,5376]{1,0:T(8,128)(2,1)S(1)}, u32[]{:S(2)}, u32[]{:S(2)}) collective-permute-start(bf16[16,5376]{1,0:T(8,128)(2,1)S(1)} %get-tuple-element.27), channel_id=1, source_target_pairs={{0,2},{1,23},{2,4},{3,1},{4,6},{5,3},{6,8},{7,5},{8,10},{9,7},{10,... | collective-permute-start | bytes 516104 | tf_op jit(solution)/shard_map/ppermute | solution.py:120
  27.2 12.2 %collective-permute-start.2 = (bf16[32,5376]{1,0:T(8,128)(2,1)S(1)}, bf16[32,5376]{1,0:T(8,128)(2,1)S(1)}, u32[]{:S(2)}, u32[]{:S(2)}) collective-permute-start(bf16[32,5376]{1,0:T(8,128)(2,1)S(1)} %get-tuple-element.19), channel_id=1, source_target_pairs={{0,22},{1,3},{2,0},{3,5},{4,2},{5,7},{6,4},{7,9},{8,6},{9,11},{10,... | collective-permute-start | bytes 1032200 | tf_op jit(solution)/shard_map/ppermute | solution.py:120
  30.4 9.0 %collective-permute-start.4 = (bf16[32,5376]{1,0:T(8,128)(2,1)S(1)}, bf16[32,5376]{1,0:T(8,128)(2,1)S(1)}, u32[]{:S(2)}, u32[]{:S(2)}) collective-permute-start(bf16[32,5376]{1,0:T(8,128)(2,1)S(1)} %add_convert_fusion), channel_id=1, source_target_pairs={{0,2},{1,23},{2,4},{3,1},{4,6},{5,3},{6,8},{7,5},{8,10},{9,7},{10,... | collective-permute-start | bytes 1032200 | tf_op jit(solution)/shard_map/ppermute | solution.py:120
  34.1 14.7 %collective-permute-start.9 = (bf16[16,5376]{1,0:T(8,128)(2,1)S(1)}, bf16[16,5376]{1,0:T(8,128)(2,1)S(1)}, u32[]{:S(2)}, u32[]{:S(2)}) collective-permute-start(bf16[16,5376]{1,0:T(8,128)(2,1)S(1)} %add_convert_fusion.2), channel_id=1, source_target_pairs={{0,2},{1,23},{2,4},{3,1},{4,6},{5,3},{6,8},{7,5},{8,10},{9,7},{10,... | collective-permute-start | bytes 516104 | tf_op jit(solution)/shard_map/ppermute | solution.py:120
  36.9 11.9 %collective-permute-start.7 = (bf16[16,5376]{1,0:T(8,128)(2,1)S(1)}, bf16[16,5376]{1,0:T(8,128)(2,1)S(1)}, u32[]{:S(2)}, u32[]{:S(2)}) collective-permute-start(bf16[16,5376]{1,0:T(8,128)(2,1)S(1)} %get-tuple-element.25), channel_id=1, source_target_pairs={{0,22},{1,3},{2,0},{3,5},{4,2},{5,7},{6,4},{7,9},{8,6},{9,11},{10,... | collective-permute-start | bytes 516104 | tf_op jit(solution)/shard_map/ppermute | solution.py:120
  39.6 12.2 %collective-permute-start.6 = (bf16[16,5376]{1,0:T(8,128)(2,1)S(1)}, bf16[16,5376]{1,0:T(8,128)(2,1)S(1)}, u32[]{:S(2)}, u32[]{:S(2)}) collective-permute-start(bf16[16,5376]{1,0:T(8,128)(2,1)S(1)} %get-tuple-element.33), channel_id=1, source_target_pairs={{0,16},{1,9},{2,18},{3,11},{4,20},{5,13},{6,22},{7,15},{8,0},{9,17... | collective-permute-start | bytes 516104 | tf_op jit(solution)/shard_map/ppermute | solution.py:120
  42.8 20.9 %collective-permute-start.5 = (bf16[16,5376]{1,0:T(8,128)(2,1)S(1)}, bf16[16,5376]{1,0:T(8,128)(2,1)S(1)}, u32[]{:S(2)}, u32[]{:S(2)}) collective-permute-start(bf16[16,5376]{1,0:T(8,128)(2,1)S(1)} %get-tuple-element.32), channel_id=1, source_target_pairs={{0,8},{1,17},{2,10},{3,19},{4,12},{5,21},{6,14},{7,23},{8,16},{9,1... | collective-permute-start | bytes 516104 | tf_op jit(solution)/shard_map/ppermute | solution.py:120
  64.0 9.3 %copy-start.6 = (s32[1,32,2]{1,2,0:T(2,128)S(1)}, s32[1,32,2]{1,2,0:T(2,128)}, u32[]{:S(2)}) copy-start(s32[1,32,2]{1,2,0:T(2,128)} %param.12) | copy-start | bytes 772
  64.0 9.6 %copy-start.7 = (s32[16]{0:T(128)S(1)}, s32[16]{0:T(128)}, u32[]{:S(2)}) copy-start(s32[16]{0:T(128)} %param.11) | copy-start | bytes 196
  65.2 23.6 %all-to-all-start = ((bf16[32,2,5376]{2,1,0:T(2,128)(2,1)}), bf16[32,2,5376]{2,1,0:T(2,128)(2,1)S(1)}, u32[]{:S(2)}, u32[]{:S(2)}) async-start(bf16[32,2,5376]{2,1,0:T(2,128)(2,1)} %reshape.68), calls=%async_computation | async-start | bytes 1376256 | tf_op jit(solution)/shard_map/all_to_all | solution.py:155
  73.4 15.9 %copy-start.3 = (f32[16,5376]{1,0:T(8,128)S(1)}, f32[16,5376]{1,0:T(8,128)}, u32[]{:S(2)}) copy-start(f32[16,5376]{1,0:T(8,128)} %param.15) | copy-start | bytes 1032196
  73.4 15.8 %copy-start.4 = (f32[16,5376]{1,0:T(8,128)S(1)}, f32[16,5376]{1,0:T(8,128)}, u32[]{:S(2)}) copy-start(f32[16,5376]{1,0:T(8,128)} %param.14) | copy-start | bytes 1032196
  73.4 15.8 %copy-start.5 = (f32[16,5376]{1,0:T(8,128)S(1)}, f32[16,5376]{1,0:T(8,128)}, u32[]{:S(2)}) copy-start(f32[16,5376]{1,0:T(8,128)} %param.13) | copy-start | bytes 1032196
  90.8 22.5 %all-to-all-start.1 = ((bf16[32,2,5376]{2,1,0:T(2,128)(2,1)}), bf16[32,2,5376]{2,1,0:T(2,128)(2,1)S(1)}, u32[]{:S(2)}, u32[]{:S(2)}) async-start(bf16[32,2,5376]{2,1,0:T(2,128)(2,1)} %reshape.70), calls=%async_computation.1 | async-start | bytes 1376256 | tf_op jit(solution)/shard_map/all_to_all | solution.py:155
  135.1 17.9 %collective-permute-start.14 = (bf16[64,2688]{1,0:T(8,128)(2,1)S(1)}, bf16[64,2688]{1,0:T(8,128)(2,1)S(1)}, u32[]{:S(2)}, u32[]{:S(2)}) collective-permute-start(bf16[64,2688]{1,0:T(8,128)(2,1)S(1)} %get-tuple-element.38), channel_id=1, source_target_pairs={{0,2},{1,23},{2,4},{3,1},{4,6},{5,3},{6,8},{7,5},{8,10},{9,7},{10,... | collective-permute-start | bytes 1032200 | tf_op jit(solution)/shard_map/ppermute | solution.py:120
  142.7 12.4 %collective-permute-start.13 = (bf16[64,2688]{1,0:T(8,128)(2,1)S(1)}, bf16[64,2688]{1,0:T(8,128)(2,1)S(1)}, u32[]{:S(2)}, u32[]{:S(2)}) collective-permute-start(bf16[64,2688]{1,0:T(8,128)(2,1)S(1)} %get-tuple-element.38), channel_id=1, source_target_pairs={{0,22},{1,3},{2,0},{3,5},{4,2},{5,7},{6,4},{7,9},{8,6},{9,11},{10,... | collective-permute-start | bytes 1032200 | tf_op jit(solution)/shard_map/ppermute | solution.py:120
  147.6 14.7 %collective-permute-start.11 = (bf16[64,2688]{1,0:T(8,128)(2,1)S(1)}, bf16[64,2688]{1,0:T(8,128)(2,1)S(1)}, u32[]{:S(2)}, u32[]{:S(2)}) collective-permute-start(bf16[64,2688]{1,0:T(8,128)(2,1)S(1)} %get-tuple-element.37), channel_id=1, source_target_pairs={{0,2},{1,23},{2,4},{3,1},{4,6},{5,3},{6,8},{7,5},{8,10},{9,7},{10,... | collective-permute-start | bytes 1032200 | tf_op jit(solution)/shard_map/ppermute | solution.py:120
  150.3 12.3 %collective-permute-start.10 = (bf16[64,2688]{1,0:T(8,128)(2,1)S(1)}, bf16[64,2688]{1,0:T(8,128)(2,1)S(1)}, u32[]{:S(2)}, u32[]{:S(2)}) collective-permute-start(bf16[64,2688]{1,0:T(8,128)(2,1)S(1)} %get-tuple-element.37), channel_id=1, source_target_pairs={{0,22},{1,3},{2,0},{3,5},{4,2},{5,7},{6,4},{7,9},{8,6},{9,11},{10,... | collective-permute-start | bytes 1032200 | tf_op jit(solution)/shard_map/ppermute | solution.py:120
  155.5 12.0 %copy-start.2 = (s32[128]{0:T(128)S(1)}, s32[128]{0:T(128)}, u32[]{:S(2)}) copy-start(s32[128]{0:T(128)} %param.9) | copy-start | bytes 1540
  155.5 12.9 %collective-permute-start.15 = (bf16[128,2688]{1,0:T(8,128)(2,1)S(1)}, bf16[128,2688]{1,0:T(8,128)(2,1)S(1)}, u32[]{:S(2)}, u32[]{:S(2)}) collective-permute-start(bf16[128,2688]{1,0:T(8,128)(2,1)S(1)} %convolution_convert_fusion.3), channel_id=1, source_target_pairs={{0,1},{1,0},{2,3},{3,2},{4,5},{5,4},{6,7},{7,6},{8,9},{9,8},{10,11... | collective-permute-start | bytes 2064392 | tf_op jit(solution)/shard_map/ppermute | solution.py:190
  163.1 6.2 %collective-permute-start.12 = (bf16[128,2688]{1,0:T(8,128)(2,1)S(1)}, bf16[128,2688]{1,0:T(8,128)(2,1)S(1)}, u32[]{:S(2)}, u32[]{:S(2)}) collective-permute-start(bf16[128,2688]{1,0:T(8,128)(2,1)S(1)} %convolution_convert_fusion.5), channel_id=1, source_target_pairs={{0,1},{1,0},{2,3},{3,2},{4,5},{5,4},{6,7},{7,6},{8,9},{9,8},{10,11... | collective-permute-start | bytes 2064392 | tf_op jit(solution)/shard_map/ppermute | solution.py:190

commit v9 on v8

--- a/solution.py
+++ b/solution.py
@@ -1,3 +1,5 @@
+import functools
+
 import jax
 import jax.numpy as jnp
 from jax import lax
@@ -58,13 +60,16 @@
     return jnp.dot(a, b, preferred_element_type=jnp.float32)
 
 
-def sum_kernel(rows_ref, own_slot_ref, other_slot_ref, own_ref, other_ref, *out_refs):
+def sum_kernel(count, has_base, rows_ref, *refs):
+    pairs, refs = refs[: 2 * count], refs[2 * count :]
+    base_ref, out_refs = (refs[0], refs[1:]) if has_base else (None, refs)
     rows = rows_ref[...]
-    own = (rows == own_slot_ref[...]).astype(jnp.bfloat16)
-    other = (rows == other_slot_ref[...]).astype(jnp.bfloat16)
-    for start in range(0, own_ref.shape[1], BLOCK_COLS):
+    chosen = [(rows == slot_ref[...]).astype(jnp.bfloat16) for slot_ref in pairs[::2]]
+    for start in range(0, pairs[1].shape[1], BLOCK_COLS):
         at = pl.ds(start, BLOCK_COLS)
-        total = dot32(own, own_ref[:, at]) + dot32(other, other_ref[:, at])
+        total = sum(dot32(a, ref[:, at]) for a, ref in zip(chosen, pairs[1::2]))
+        if base_ref is not None:
+            total += base_ref[:, at]
         first = 0
         for out_ref in out_refs:
             height = out_ref.shape[0]
@@ -72,21 +77,26 @@
             first += height
 
 
-def slot_sums(rows, own_slot, other_slot, own, other, heights):
-    count, width = own.shape
+def slot_sums(rows, pairs, heights, base=None, out_dtype=jnp.bfloat16):
+    count, width = pairs[0][1].shape
+    operands = [rows[:, None]]
+    for slots, tokens in pairs:
+        operands += [slots[None, :], tokens]
+    if base is not None:
+        operands.append(base)
     in_vmem = pl.BlockSpec(memory_space=pltpu.VMEM)
     return pl.pallas_call(
-        sum_kernel,
-        in_specs=[in_vmem] * 5,
+        functools.partial(sum_kernel, len(pairs), base is not None),
+        in_specs=[in_vmem] * len(operands),
         out_specs=[in_vmem] * len(heights),
-        out_shape=[jax.ShapeDtypeStruct((height, width), jnp.bfloat16) for height in heights],
+        out_shape=[jax.ShapeDtypeStruct((height, width), out_dtype) for height in heights],
         cost_estimate=pl.CostEstimate(
-            flops=4 * rows.shape[0] * count * width,
-            bytes_accessed=2 * (2 * count + rows.shape[0]) * width,
+            flops=2 * len(pairs) * rows.shape[0] * count * width,
+            bytes_accessed=2 * (len(pairs) * count + rows.shape[0]) * width,
             transcendentals=0,
         ),
         compiler_params=pltpu.CompilerParams(vmem_limit_bytes=16 * 2**20),
-    )(rows[:, None], own_slot[None, :], other_slot[None, :], own, other)
+    )(*operands)
 
 
 def on_device(grads, token_slot, node_ids, touched_ids, owner_map, moment, second, master):
@@ -122,23 +132,30 @@
     def add(*terms):
         return sum(term.astype(jnp.float32) for term in terms)
 
-    summed = jnp.concatenate([hub_rows(shift) for shift in (0, 1, -1, 2)])
     stay, move = slot_dev, (Z_SIZE // SUM_APART - 1) * slot_dev
-    parts = slot_sums(summed, token_slot, other_slot, grads, other_grads, [stay, move] * 4)
-    here, next_hub, last_hub, far_hub = zip(parts[::2], parts[1::2])
-
-    relayed = send(far_hub[1], 1)
-    from_ahead = send(last_hub[1], -1)
-    relay_sum = add(next_hub[1], relayed).astype(jnp.bfloat16)
-    relay_sum, held_back = lax.optimization_barrier((relay_sum, last_hub[0]))
+    here, next_hub, last_hub, far_hub = map(hub_rows, (0, 1, -1, 2))
+    own, other = (token_slot, grads), (other_slot, other_grads)
+    first = jnp.concatenate([far_hub[stay:], last_hub[stay:]])
+    (own_first,) = slot_sums(first, [own], [2 * move], out_dtype=jnp.float32)
+    far_move, last_move = slot_sums(first, [other], [move, move], own_first)
+    later = jnp.concatenate([far_hub[:stay], last_hub[:stay], next_hub, here])
+    far_move, last_move, later = lax.optimization_barrier((far_move, last_move, later))
+    far_stay, last_stay, next_stay, next_move, here_stay, here_move = slot_sums(
+        later, [own, other], [stay, stay, stay, move, stay, move]
+    )
+
+    relayed = send(far_move, 1)
+    from_ahead = send(last_move, -1)
+    relay_sum = add(next_move, relayed).astype(jnp.bfloat16)
+    relay_sum, last_stay = lax.optimization_barrier((relay_sum, last_stay))
     from_behind = send(relay_sum, 1)
     terms = []
     for i in range(move // slot_dev):
         at = slice(i * slot_dev, (i + 1) * slot_dev)
-        block = add(here[1][at], from_ahead[at], from_behind[at]).astype(jnp.bfloat16)
+        block = add(here_move[at], from_ahead[at], from_behind[at]).astype(jnp.bfloat16)
         terms.append(send(block, (i + 1) * SUM_APART))
-    terms += [here[0], send(held_back, -1)]
-    terms.append(send(add(next_hub[0], send(far_hub[0], 1)).astype(jnp.bfloat16), 1))
+    terms += [here_stay, send(last_stay, -1)]
+    terms.append(send(add(next_stay, send(far_stay, 1)).astype(jnp.bfloat16), 1))
     node_sum = add(*terms).astype(jnp.bfloat16)
 
     owner_node = node_ids[0] // (VOCAB // node_count)

time: 173 us -> 173 us (level)
  starting transfers between devices: 88.3 us -> 81.7 us
  waiting for transfers between devices: 47.4 us -> 51.2 us
    ppermute x12, starting transfers between devices: 46.4 us -> 39 us  [send(): return lax.ppermute(rows, ('z', 'c'), neighbour(steps))]
    all_to_all x2, waiting for transfers between devices: 28.3 us -> 32.8 us  [exchange(): lax.all_to_all(rows.astype(jnp.bfloat16).reshape(node_count, capacity, wi...]
  transfers between devices with their start and end apart: 18 -> 18, of which waited for: 8 -> 7; matrix products, arithmetic and copies ran while one was open for 2% -> 3% of each run, Pallas kernels for 0% -> 1%
where the time goes in v9:
time: 173 us; the launch traced here: 171 us
  starting transfers between devices  81.7 us (47%)
  waiting for transfers between devices  51.2 us (30%)
  blocking collectives  22.2 us (13%)
  local copies, waits for them, and re-layouts  5.37 us (3%)
  other arithmetic  5.07 us (3%)
  matrix products  2.87 us (2%)
  Pallas kernels  1.79 us (1%)
    ppermute x12, starting transfers between devices, send(): return lax.ppermute(rows, ('z', 'c'), neighbour(steps))  39 us
    all_to_all x2, waiting for transfers between devices, exchange(): lax.all_to_all(rows.astype(jnp.bfloat16).reshape(node_count, capacity, wi...  32.8 us
    all_gather x1, blocking collectives, on_device(): lax.all_gather(rows, 'z', axis=0, tiled=True, axis_index_groups=GROUPS)  22.2 us
    all_to_all x2, starting transfers between devices, exchange(): lax.all_to_all(rows.astype(jnp.bfloat16).reshape(node_count, capacity, wi...  17.7 us
    ppermute x12, waiting for transfers between devices, send(): return lax.ppermute(rows, ('z', 'c'), neighbour(steps))  17.6 us
    ppermute x1, starting transfers between devices, on_device(): other_grads = lax.ppermute(grads, 'c', SWAP)  12.4 us
    ppermute x2, starting transfers between devices, on_device(): lax.ppermute(theirs, 'c', SWAP)  10.6 us
  transfers between devices with their start and end apart: 18, of which 7 were waited for; matrix products, arithmetic and copies ran while one was open for 3% of the time, Pallas kernels for 1%

profile of v9, /device:TPU:1, one launch (start us, length us, event | category | flops | bytes accessed | tf_op | source)
XLA Modules:
  0.0 171.3 jit_solution(10001799989324735761)
XLA Ops:
  0.6 12.4 %collective-permute-start.1 = (bf16[128,5376]{1,0:T(8,128)(2,1)}, bf16[128,5376]{1,0:T(8,128)(2,1)S(1)}, u32[]{:S(2)}, u32[]{:S(2)}) collective-permute-start(bf16[128,5376]{1,0:T(8,128)(2,1)} %refs_1_.3), channel_id=1, source_target_pairs={{0,1},{1,0},{2,3},{3,2},{4,5},{5,4},{6,7},{7,6},{8,9},{9,8},{10,11... | collective-permute-start | bytes 4128776 | tf_op jit(solution)/shard_map/ppermute | solution.py:111
  13.1 1.9 %collective-permute-start = (s32[128]{0:T(128)}, s32[128]{0:T(128)S(1)}, u32[]{:S(2)}, u32[]{:S(2)}) collective-permute-start(s32[128]{0:T(128)} %param.9), channel_id=1, source_target_pairs={{0,1},{1,0},{2,3},{3,2},{4,5},{5,4},{6,7},{7,6},{8,9},{9,8},{10,11... | collective-permute-start | bytes 1544 | tf_op jit(solution)/shard_map/ppermute | solution.py:112
  16.1 1.3 copy-done
  19.0 5.3 %collective-permute-start.3 = (bf16[32,5376]{1,0:T(8,128)(2,1)S(1)}, bf16[32,5376]{1,0:T(8,128)(2,1)}, u32[]{:S(2)}, u32[]{:S(2)}) collective-permute-start(bf16[32,5376]{1,0:T(8,128)(2,1)S(1)} %get-tuple-element.27), channel_id=1, source_target_pairs={{0,2},{1,23},{2,4},{3,1},{4,6},{5,3},{6,8},{7,5},{8,10},{9,7},{10,... | collective-permute-start | bytes 1032200 | tf_op jit(solution)/shard_map/ppermute | solution.py:130
  24.7 0.9 shard_map.113
  25.6 2.2 %collective-permute-start.8 = (bf16[16,5376]{1,0:T(8,128)(2,1)S(1)}, bf16[16,5376]{1,0:T(8,128)(2,1)S(1)}, u32[]{:S(2)}, u32[]{:S(2)}) collective-permute-start(bf16[16,5376]{1,0:T(8,128)(2,1)S(1)} %get-tuple-element.33), channel_id=1, source_target_pairs={{0,2},{1,23},{2,4},{3,1},{4,6},{5,3},{6,8},{7,5},{8,10},{9,7},{10,... | collective-permute-start | bytes 516104 | tf_op jit(solution)/shard_map/ppermute | solution.py:130
  27.8 3.1 %collective-permute-start.2 = (bf16[32,5376]{1,0:T(8,128)(2,1)S(1)}, bf16[32,5376]{1,0:T(8,128)(2,1)S(1)}, u32[]{:S(2)}, u32[]{:S(2)}) collective-permute-start(bf16[32,5376]{1,0:T(8,128)(2,1)S(1)} %get-tuple-element.25), channel_id=1, source_target_pairs={{0,22},{1,3},{2,0},{3,5},{4,2},{5,7},{6,4},{7,9},{8,6},{9,11},{10,... | collective-permute-start | bytes 1032200 | tf_op jit(solution)/shard_map/ppermute | solution.py:130
  30.9 1.1 add_convert_fusion
  32.0 3.4 %collective-permute-start.4 = (bf16[32,5376]{1,0:T(8,128)(2,1)S(1)}, bf16[32,5376]{1,0:T(8,128)(2,1)S(1)}, u32[]{:S(2)}, u32[]{:S(2)}) collective-permute-start(bf16[32,5376]{1,0:T(8,128)(2,1)S(1)} %add_convert_fusion), channel_id=1, source_target_pairs={{0,2},{1,23},{2,4},{3,1},{4,6},{5,3},{6,8},{7,5},{8,10},{9,7},{10,... | collective-permute-start | bytes 1032200 | tf_op jit(solution)/shard_map/ppermute | solution.py:130
  35.5 1.9 %collective-permute-start.9 = (bf16[16,5376]{1,0:T(8,128)(2,1)S(1)}, bf16[16,5376]{1,0:T(8,128)(2,1)S(1)}, u32[]{:S(2)}, u32[]{:S(2)}) collective-permute-start(bf16[16,5376]{1,0:T(8,128)(2,1)S(1)} %add_convert_fusion.2), channel_id=1, source_target_pairs={{0,2},{1,23},{2,4},{3,1},{4,6},{5,3},{6,8},{7,5},{8,10},{9,7},{10,... | collective-permute-start | bytes 516104 | tf_op jit(solution)/shard_map/ppermute | solution.py:130
  37.4 3.4 %collective-permute-start.7 = (bf16[16,5376]{1,0:T(8,128)(2,1)S(1)}, bf16[16,5376]{1,0:T(8,128)(2,1)S(1)}, u32[]{:S(2)}, u32[]{:S(2)}) collective-permute-start(bf16[16,5376]{1,0:T(8,128)(2,1)S(1)} %get-tuple-element.31), channel_id=1, source_target_pairs={{0,22},{1,3},{2,0},{3,5},{4,2},{5,7},{6,4},{7,9},{8,6},{9,11},{10,... | collective-permute-start | bytes 516104 | tf_op jit(solution)/shard_map/ppermute | solution.py:130
  40.9 2.7 %collective-permute-start.6 = (bf16[16,5376]{1,0:T(8,128)(2,1)S(1)}, bf16[16,5376]{1,0:T(8,128)(2,1)S(1)}, u32[]{:S(2)}, u32[]{:S(2)}) collective-permute-start(bf16[16,5376]{1,0:T(8,128)(2,1)S(1)} %get-tuple-element.39), channel_id=1, source_target_pairs={{0,16},{1,9},{2,18},{3,11},{4,20},{5,13},{6,22},{7,15},{8,0},{9,17... | collective-permute-start | bytes 516104 | tf_op jit(solution)/shard_map/ppermute | solution.py:130
  43.6 6.5 %collective-permute-start.5 = (bf16[16,5376]{1,0:T(8,128)(2,1)S(1)}, bf16[16,5376]{1,0:T(8,128)(2,1)S(1)}, u32[]{:S(2)}, u32[]{:S(2)}) collective-permute-start(bf16[16,5376]{1,0:T(8,128)(2,1)S(1)} %get-tuple-element.38), channel_id=1, source_target_pairs={{0,8},{1,17},{2,10},{3,19},{4,12},{5,21},{6,14},{7,23},{8,16},{9,1... | collective-permute-start | bytes 516104 | tf_op jit(solution)/shard_map/ppermute | solution.py:130
  50.2 3.0 %collective-permute-done.6 = bf16[16,5376]{1,0:T(8,128)(2,1)S(1)} collective-permute-done((bf16[16,5376]{1,0:T(8,128)(2,1)S(1)}, bf16[16,5376]{1,0:T(8,128)(2,1)S(1)}, u32[]{:S(2)}, u32[]{:S(2)}) %collective-permute-start.6) | collective-permute-done | bytes 172064 | tf_op jit(solution)/shard_map/ppermute | solution.py:130
  53.1 11.5 %collective-permute-done.5 = bf16[16,5376]{1,0:T(8,128)(2,1)S(1)} collective-permute-done((bf16[16,5376]{1,0:T(8,128)(2,1)S(1)}, bf16[16,5376]{1,0:T(8,128)(2,1)S(1)}, u32[]{:S(2)}, u32[]{:S(2)}) %collective-permute-start.5) | collective-permute-done | bytes 172064 | tf_op jit(solution)/shard_map/ppermute | solution.py:130
  65.0 1.1 reshape.68
  66.1 9.7 %all-to-all-start = ((bf16[32,2,5376]{2,1,0:T(2,128)(2,1)}), bf16[32,2,5376]{2,1,0:T(2,128)(2,1)S(1)}, u32[]{:S(2)}, u32[]{:S(2)}) async-start(bf16[32,2,5376]{2,1,0:T(2,128)(2,1)} %reshape.68), calls=%async_computation | async-start | bytes 1376256 | tf_op jit(solution)/shard_map/all_to_all | solution.py:172
  76.1 16.8 %all-to-all-done = bf16[32,2,5376]{2,1,0:T(2,128)(2,1)S(1)} async-done(((bf16[32,2,5376]{2,1,0:T(2,128)(2,1)}), bf16[32,2,5376]{2,1,0:T(2,128)(2,1)S(1)}, u32[]{:S(2)}, u32[]{:S(2)}) %all-to-all-start) | async-done | bytes 688160 | tf_op jit(solution)/shard_map/all_to_all | solution.py:172
  93.9 1.1 reshape.70
  95.0 8.1 %all-to-all-start.1 = ((bf16[32,2,5376]{2,1,0:T(2,128)(2,1)}), bf16[32,2,5376]{2,1,0:T(2,128)(2,1)S(1)}, u32[]{:S(2)}, u32[]{:S(2)}) async-start(bf16[32,2,5376]{2,1,0:T(2,128)(2,1)} %reshape.70), calls=%async_computation.1 | async-start | bytes 1376256 | tf_op jit(solution)/shard_map/all_to_all | solution.py:172
  103.1 1.2 subtract_select_fusion
  104.2 16.0 %all-to-all-done.1 = bf16[32,2,5376]{2,1,0:T(2,128)(2,1)S(1)} async-done(((bf16[32,2,5376]{2,1,0:T(2,128)(2,1)}), bf16[32,2,5376]{2,1,0:T(2,128)(2,1)S(1)}, u32[]{:S(2)}, u32[]{:S(2)}) %all-to-all-start.1) | async-done | bytes 688160 | tf_op jit(solution)/shard_map/all_to_all | solution.py:172
  120.8 22.2 %all_gather.3 = bf16[64,5376]{1,0:T(8,128)(2,1)S(1)} all-gather(bf16[16,5376]{1,0:T(8,128)(2,1)S(1)} %convolution_convert_fusion.2), channel_id=1, replica_groups={{0,6,12,18},{2,8,14,20},{4,10,16,22},{1,7,13,19},{3,9,15,21},{5,11,17,2..., dimensions={0}, use_global_device_ids=true | all-gather | bytes 860160 | tf_op jit(solution)/shard_map/all_gather | solution.py:191
  143.0 1.9 %collective-permute-start.14 = (bf16[64,2688]{1,0:T(8,128)(2,1)S(1)}, bf16[64,2688]{1,0:T(8,128)(2,1)S(1)}, u32[]{:S(2)}, u32[]{:S(2)}) collective-permute-start(bf16[64,2688]{1,0:T(8,128)(2,1)S(1)} %get-tuple-element.44), channel_id=1, source_target_pairs={{0,2},{1,23},{2,4},{3,1},{4,6},{5,3},{6,8},{7,5},{8,10},{9,7},{10,... | collective-permute-start | bytes 1032200 | tf_op jit(solution)/shard_map/ppermute | solution.py:130
  144.9 3.4 %collective-permute-start.13 = (bf16[64,2688]{1,0:T(8,128)(2,1)S(1)}, bf16[64,2688]{1,0:T(8,128)(2,1)S(1)}, u32[]{:S(2)}, u32[]{:S(2)}) collective-permute-start(bf16[64,2688]{1,0:T(8,128)(2,1)S(1)} %get-tuple-element.44), channel_id=1, source_target_pairs={{0,22},{1,3},{2,0},{3,5},{4,2},{5,7},{6,4},{7,9},{8,6},{9,11},{10,... | collective-permute-start | bytes 1032200 | tf_op jit(solution)/shard_map/ppermute | solution.py:130
  148.3 3.1 %collective-permute-start.11 = (bf16[64,2688]{1,0:T(8,128)(2,1)S(1)}, bf16[64,2688]{1,0:T(8,128)(2,1)S(1)}, u32[]{:S(2)}, u32[]{:S(2)}) collective-permute-start(bf16[64,2688]{1,0:T(8,128)(2,1)S(1)} %get-tuple-element.43), channel_id=1, source_target_pairs={{0,2},{1,23},{2,4},{3,1},{4,6},{5,3},{6,8},{7,5},{8,10},{9,7},{10,... | collective-permute-start | bytes 1032200 | tf_op jit(solution)/shard_map/ppermute | solution.py:130
  151.5 2.2 %collective-permute-start.10 = (bf16[64,2688]{1,0:T(8,128)(2,1)S(1)}, bf16[64,2688]{1,0:T(8,128)(2,1)S(1)}, u32[]{:S(2)}, u32[]{:S(2)}) collective-permute-start(bf16[64,2688]{1,0:T(8,128)(2,1)S(1)} %get-tuple-element.43), channel_id=1, source_target_pairs={{0,22},{1,3},{2,0},{3,5},{4,2},{5,7},{6,4},{7,9},{8,6},{9,11},{10,... | collective-permute-start | bytes 1032200 | tf_op jit(solution)/shard_map/ppermute | solution.py:130
  153.7 2.4 %collective-permute-done.13 = bf16[64,2688]{1,0:T(8,128)(2,1)S(1)} collective-permute-done((bf16[64,2688]{1,0:T(8,128)(2,1)S(1)}, bf16[64,2688]{1,0:T(8,128)(2,1)S(1)}, u32[]{:S(2)}, u32[]{:S(2)}) %collective-permute-start.13) | collective-permute-done | bytes 344096 | tf_op jit(solution)/shard_map/ppermute | solution.py:130
  156.5 6.5 %collective-permute-start.15 = (bf16[128,2688]{1,0:T(8,128)(2,1)S(1)}, bf16[128,2688]{1,0:T(8,128)(2,1)S(1)}, u32[]{:S(2)}, u32[]{:S(2)}) collective-permute-start(bf16[128,2688]{1,0:T(8,128)(2,1)S(1)} %convolution_convert_fusion.3), channel_id=1, source_target_pairs={{0,1},{1,0},{2,3},{3,2},{4,5},{5,4},{6,7},{7,6},{8,9},{9,8},{10,11... | collective-permute-start | bytes 2064392 | tf_op jit(solution)/shard_map/ppermute | solution.py:207
  164.1 4.1 %collective-permute-start.12 = (bf16[128,2688]{1,0:T(8,128)(2,1)S(1)}, bf16[128,2688]{1,0:T(8,128)(2,1)S(1)}, u32[]{:S(2)}, u32[]{:S(2)}) collective-permute-start(bf16[128,2688]{1,0:T(8,128)(2,1)S(1)} %convolution_convert_fusion.5), channel_id=1, source_target_pairs={{0,1},{1,0},{2,3},{3,2},{4,5},{5,4},{6,7},{7,6},{8,9},{9,8},{10,11... | collective-permute-start | bytes 2064392 | tf_op jit(solution)/shard_map/ppermute | solution.py:207
  169.2 0.8 collective-permute-done.12
  170.1 1.2 pad_maximum_fusion
  (67 shorter events, 7.9 us)
Async XLA Ops:
  0.6 17.9 %collective-permute-start.1 = (bf16[128,5376]{1,0:T(8,128)(2,1)}, bf16[128,5376]{1,0:T(8,128)(2,1)S(1)}, u32[]{:S(2)}, u32[]{:S(2)}) collective-permute-start(bf16[128,5376]{1,0:T(8,128)(2,1)} %refs_1_.3), channel_id=1, source_target_pairs={{0,1},{1,0},{2,3},{3,2},{4,5},{5,4},{6,7},{7,6},{8,9},{9,8},{10,11... | collective-permute-start | bytes 4128776 | tf_op jit(solution)/shard_map/ppermute | solution.py:111
  13.1 5.5 %collective-permute-start = (s32[128]{0:T(128)}, s32[128]{0:T(128)S(1)}, u32[]{:S(2)}, u32[]{:S(2)}) collective-permute-start(s32[128]{0:T(128)} %param.9), channel_id=1, source_target_pairs={{0,1},{1,0},{2,3},{3,2},{4,5},{5,4},{6,7},{7,6},{8,9},{9,8},{10,11... | collective-permute-start | bytes 1544 | tf_op jit(solution)/shard_map/ppermute | solution.py:112
  16.1 1.3 copy-start
  17.5 0.7 copy-start.2
  18.6 5.8 %copy-start.9 = (s32[1,16]{1,0:T(1,128)S(1)}, s32[1,16]{1,0:T(1,128)}, u32[]{:S(2)}) copy-start(s32[1,16]{1,0:T(1,128)} %param.10) | copy-start | bytes 196
  18.6 6.1 %copy-start.1 = (bf16[128,5376]{1,0:T(8,128)(2,1)S(1)}, bf16[128,5376]{1,0:T(8,128)(2,1)}, u32[]{:S(2)}) copy-start(bf16[128,5376]{1,0:T(8,128)(2,1)} %refs_1_.3) | copy-start | bytes 4128772
  18.6 6.1 %copy-start.3 = (s32[128]{0:T(128)S(1)}, s32[128]{0:T(128)}, u32[]{:S(2)}) copy-start(s32[128]{0:T(128)} %param.9) | copy-start | bytes 1540
  19.0 11.9 %collective-permute-start.3 = (bf16[32,5376]{1,0:T(8,128)(2,1)S(1)}, bf16[32,5376]{1,0:T(8,128)(2,1)}, u32[]{:S(2)}, u32[]{:S(2)}) collective-permute-start(bf16[32,5376]{1,0:T(8,128)(2,1)S(1)} %get-tuple-element.27), channel_id=1, source_target_pairs={{0,2},{1,23},{2,4},{3,1},{4,6},{5,3},{6,8},{7,5},{8,10},{9,7},{10,... | collective-permute-start | bytes 1032200 | tf_op jit(solution)/shard_map/ppermute | solution.py:130
  25.6 9.8 %collective-permute-start.8 = (bf16[16,5376]{1,0:T(8,128)(2,1)S(1)}, bf16[16,5376]{1,0:T(8,128)(2,1)S(1)}, u32[]{:S(2)}, u32[]{:S(2)}) collective-permute-start(bf16[16,5376]{1,0:T(8,128)(2,1)S(1)} %get-tuple-element.33), channel_id=1, source_target_pairs={{0,2},{1,23},{2,4},{3,1},{4,6},{5,3},{6,8},{7,5},{8,10},{9,7},{10,... | collective-permute-start | bytes 516104 | tf_op jit(solution)/shard_map/ppermute | solution.py:130
  27.8 12.9 %collective-permute-start.2 = (bf16[32,5376]{1,0:T(8,128)(2,1)S(1)}, bf16[32,5376]{1,0:T(8,128)(2,1)S(1)}, u32[]{:S(2)}, u32[]{:S(2)}) collective-permute-start(bf16[32,5376]{1,0:T(8,128)(2,1)S(1)} %get-tuple-element.25), channel_id=1, source_target_pairs={{0,22},{1,3},{2,0},{3,5},{4,2},{5,7},{6,4},{7,9},{8,6},{9,11},{10,... | collective-permute-start | bytes 1032200 | tf_op jit(solution)/shard_map/ppermute | solution.py:130
  32.0 8.8 %collective-permute-start.4 = (bf16[32,5376]{1,0:T(8,128)(2,1)S(1)}, bf16[32,5376]{1,0:T(8,128)(2,1)S(1)}, u32[]{:S(2)}, u32[]{:S(2)}) collective-permute-start(bf16[32,5376]{1,0:T(8,128)(2,1)S(1)} %add_convert_fusion), channel_id=1, source_target_pairs={{0,2},{1,23},{2,4},{3,1},{4,6},{5,3},{6,8},{7,5},{8,10},{9,7},{10,... | collective-permute-start | bytes 1032200 | tf_op jit(solution)/shard_map/ppermute | solution.py:130
  35.5 14.7 %collective-permute-start.9 = (bf16[16,5376]{1,0:T(8,128)(2,1)S(1)}, bf16[16,5376]{1,0:T(8,128)(2,1)S(1)}, u32[]{:S(2)}, u32[]{:S(2)}) collective-permute-start(bf16[16,5376]{1,0:T(8,128)(2,1)S(1)} %add_convert_fusion.2), channel_id=1, source_target_pairs={{0,2},{1,23},{2,4},{3,1},{4,6},{5,3},{6,8},{7,5},{8,10},{9,7},{10,... | collective-permute-start | bytes 516104 | tf_op jit(solution)/shard_map/ppermute | solution.py:130
  37.4 12.8 %collective-permute-start.7 = (bf16[16,5376]{1,0:T(8,128)(2,1)S(1)}, bf16[16,5376]{1,0:T(8,128)(2,1)S(1)}, u32[]{:S(2)}, u32[]{:S(2)}) collective-permute-start(bf16[16,5376]{1,0:T(8,128)(2,1)S(1)} %get-tuple-element.31), channel_id=1, source_target_pairs={{0,22},{1,3},{2,0},{3,5},{4,2},{5,7},{6,4},{7,9},{8,6},{9,11},{10,... | collective-permute-start | bytes 516104 | tf_op jit(solution)/shard_map/ppermute | solution.py:130
  40.9 12.2 %collective-permute-start.6 = (bf16[16,5376]{1,0:T(8,128)(2,1)S(1)}, bf16[16,5376]{1,0:T(8,128)(2,1)S(1)}, u32[]{:S(2)}, u32[]{:S(2)}) collective-permute-start(bf16[16,5376]{1,0:T(8,128)(2,1)S(1)} %get-tuple-element.39), channel_id=1, source_target_pairs={{0,16},{1,9},{2,18},{3,11},{4,20},{5,13},{6,22},{7,15},{8,0},{9,17... | collective-permute-start | bytes 516104 | tf_op jit(solution)/shard_map/ppermute | solution.py:130
  43.6 21.1 %collective-permute-start.5 = (bf16[16,5376]{1,0:T(8,128)(2,1)S(1)}, bf16[16,5376]{1,0:T(8,128)(2,1)S(1)}, u32[]{:S(2)}, u32[]{:S(2)}) collective-permute-start(bf16[16,5376]{1,0:T(8,128)(2,1)S(1)} %get-tuple-element.38), channel_id=1, source_target_pairs={{0,8},{1,17},{2,10},{3,19},{4,12},{5,21},{6,14},{7,23},{8,16},{9,1... | collective-permute-start | bytes 516104 | tf_op jit(solution)/shard_map/ppermute | solution.py:130
  65.0 10.8 %copy-start.7 = (s32[1,32,2]{1,2,0:T(2,128)S(1)}, s32[1,32,2]{1,2,0:T(2,128)}, u32[]{:S(2)}) copy-start(s32[1,32,2]{1,2,0:T(2,128)} %param.12) | copy-start | bytes 772
  65.0 11.0 %copy-start.8 = (s32[16]{0:T(128)S(1)}, s32[16]{0:T(128)}, u32[]{:S(2)}) copy-start(s32[16]{0:T(128)} %param.11) | copy-start | bytes 196
  66.1 26.8 %all-to-all-start = ((bf16[32,2,5376]{2,1,0:T(2,128)(2,1)}), bf16[32,2,5376]{2,1,0:T(2,128)(2,1)S(1)}, u32[]{:S(2)}, u32[]{:S(2)}) async-start(bf16[32,2,5376]{2,1,0:T(2,128)(2,1)} %reshape.68), calls=%async_computation | async-start | bytes 1376256 | tf_op jit(solution)/shard_map/all_to_all | solution.py:172
  75.8 17.6 %copy-start.4 = (f32[16,5376]{1,0:T(8,128)S(1)}, f32[16,5376]{1,0:T(8,128)}, u32[]{:S(2)}) copy-start(f32[16,5376]{1,0:T(8,128)} %param.15) | copy-start | bytes 1032196
  75.8 17.6 %copy-start.5 = (f32[16,5376]{1,0:T(8,128)S(1)}, f32[16,5376]{1,0:T(8,128)}, u32[]{:S(2)}) copy-start(f32[16,5376]{1,0:T(8,128)} %param.14) | copy-start | bytes 1032196
  75.8 17.6 %copy-start.6 = (f32[16,5376]{1,0:T(8,128)S(1)}, f32[16,5376]{1,0:T(8,128)}, u32[]{:S(2)}) copy-start(f32[16,5376]{1,0:T(8,128)} %param.13) | copy-start | bytes 1032196
  95.0 25.3 %all-to-all-start.1 = ((bf16[32,2,5376]{2,1,0:T(2,128)(2,1)}), bf16[32,2,5376]{2,1,0:T(2,128)(2,1)S(1)}, u32[]{:S(2)}, u32[]{:S(2)}) async-start(bf16[32,2,5376]{2,1,0:T(2,128)(2,1)} %reshape.70), calls=%async_computation.1 | async-start | bytes 1376256 | tf_op jit(solution)/shard_map/all_to_all | solution.py:172
  143.0 10.7 %collective-permute-start.14 = (bf16[64,2688]{1,0:T(8,128)(2,1)S(1)}, bf16[64,2688]{1,0:T(8,128)(2,1)S(1)}, u32[]{:S(2)}, u32[]{:S(2)}) collective-permute-start(bf16[64,2688]{1,0:T(8,128)(2,1)S(1)} %get-tuple-element.44), channel_id=1, source_target_pairs={{0,2},{1,23},{2,4},{3,1},{4,6},{5,3},{6,8},{7,5},{8,10},{9,7},{10,... | collective-permute-start | bytes 1032200 | tf_op jit(solution)/shard_map/ppermute | solution.py:130
  144.9 11.2 %collective-permute-start.13 = (bf16[64,2688]{1,0:T(8,128)(2,1)S(1)}, bf16[64,2688]{1,0:T(8,128)(2,1)S(1)}, u32[]{:S(2)}, u32[]{:S(2)}) collective-permute-start(bf16[64,2688]{1,0:T(8,128)(2,1)S(1)} %get-tuple-element.44), channel_id=1, source_target_pairs={{0,22},{1,3},{2,0},{3,5},{4,2},{5,7},{6,4},{7,9},{8,6},{9,11},{10,... | collective-permute-start | bytes 1032200 | tf_op jit(solution)/shard_map/ppermute | solution.py:130
  148.3 14.7 %collective-permute-start.11 = (bf16[64,2688]{1,0:T(8,128)(2,1)S(1)}, bf16[64,2688]{1,0:T(8,128)(2,1)S(1)}, u32[]{:S(2)}, u32[]{:S(2)}) collective-permute-start(bf16[64,2688]{1,0:T(8,128)(2,1)S(1)} %get-tuple-element.43), channel_id=1, source_target_pairs={{0,2},{1,23},{2,4},{3,1},{4,6},{5,3},{6,8},{7,5},{8,10},{9,7},{10,... | collective-permute-start | bytes 1032200 | tf_op jit(solution)/shard_map/ppermute | solution.py:130
  151.5 12.2 %collective-permute-start.10 = (bf16[64,2688]{1,0:T(8,128)(2,1)S(1)}, bf16[64,2688]{1,0:T(8,128)(2,1)S(1)}, u32[]{:S(2)}, u32[]{:S(2)}) collective-permute-start(bf16[64,2688]{1,0:T(8,128)(2,1)S(1)} %get-tuple-element.43), channel_id=1, source_target_pairs={{0,22},{1,3},{2,0},{3,5},{4,2},{5,7},{6,4},{7,9},{8,6},{9,11},{10,... | collective-permute-start | bytes 1032200 | tf_op jit(solution)/shard_map/ppermute | solution.py:130
  156.5 12.5 %collective-permute-start.15 = (bf16[128,2688]{1,0:T(8,128)(2,1)S(1)}, bf16[128,2688]{1,0:T(8,128)(2,1)S(1)}, u32[]{:S(2)}, u32[]{:S(2)}) collective-permute-start(bf16[128,2688]{1,0:T(8,128)(2,1)S(1)} %convolution_convert_fusion.3), channel_id=1, source_target_pairs={{0,1},{1,0},{2,3},{3,2},{4,5},{5,4},{6,7},{7,6},{8,9},{9,8},{10,11... | collective-permute-start | bytes 2064392 | tf_op jit(solution)/shard_map/ppermute | solution.py:207
  164.1 5.8 %collective-permute-start.12 = (bf16[128,2688]{1,0:T(8,128)(2,1)S(1)}, bf16[128,2688]{1,0:T(8,128)(2,1)S(1)}, u32[]{:S(2)}, u32[]{:S(2)}) collective-permute-start(bf16[128,2688]{1,0:T(8,128)(2,1)S(1)} %convolution_convert_fusion.5), channel_id=1, source_target_pairs={{0,1},{1,0},{2,3},{3,2},{4,5},{5,4},{6,7},{7,6},{8,9},{9,8},{10,11... | collective-permute-start | bytes 2064392 | tf_op jit(solution)/shard_map/ppermute | solution.py:207

commit v10 on v8

--- a/solution.py
+++ b/solution.py
@@ -1,3 +1,5 @@
+import functools
+
 import jax
 import jax.numpy as jnp
 from jax import lax
@@ -89,6 +91,32 @@
     )(rows[:, None], own_slot[None, :], other_slot[None, :], own, other)
 
 
+def place_kernel(start, mine_ref, theirs_ref, *refs):
+    whole_ref, held, done = refs[-3:]
+    held[...] = mine_ref[...] + theirs_ref[...]
+    at = pl.ds(start, held.shape[1])
+    copy = pltpu.make_async_copy(held, whole_ref.at[:, at], done)
+    copy.start()
+    copy.wait()
+
+
+def place_sum(mine, theirs, start, width, whole=None):
+    in_vmem, in_hbm = pl.BlockSpec(memory_space=pltpu.VMEM), pl.BlockSpec(memory_space=pltpu.HBM)
+    operands = [mine, theirs] + ([] if whole is None else [whole])
+    return pl.pallas_call(
+        functools.partial(place_kernel, start),
+        in_specs=[in_vmem, in_vmem] + [in_hbm] * (len(operands) - 2),
+        out_specs=in_hbm,
+        out_shape=jax.ShapeDtypeStruct((mine.shape[0], width), mine.dtype),
+        scratch_shapes=[pltpu.VMEM(mine.shape, mine.dtype), pltpu.SemaphoreType.DMA],
+        input_output_aliases={} if whole is None else {2: 0},
+        cost_estimate=pl.CostEstimate(
+            flops=mine.size, bytes_accessed=6 * mine.size, transcendentals=0
+        ),
+        compiler_params=pltpu.CompilerParams(vmem_limit_bytes=16 * 2**20),
+    )(*operands)
+
+
 def on_device(grads, token_slot, node_ids, touched_ids, owner_map, moment, second, master):
     slot_dev = node_ids.shape[1]
     width = grads.shape[1]
@@ -183,12 +211,12 @@
         )
         for half in halves
     ]
-    tokens = []
-    for gathered in map(jnp.concatenate, arrived):
+    token_rows = None
+    for i, gathered in enumerate(map(jnp.concatenate, arrived)):
         theirs = dot32(other_choice, gathered).astype(jnp.bfloat16)
         mine = dot32(own_choice, gathered).astype(jnp.bfloat16)
-        tokens.append(lax.optimization_barrier(mine) + lax.ppermute(theirs, "c", SWAP))
-    token_rows = jnp.concatenate(tokens, axis=1)
+        theirs = lax.ppermute(theirs, "c", SWAP)
+        token_rows = place_sum(mine, theirs, i * step, width, token_rows)
     return token_rows, moment_out, second_out, master_out
 
 

time: 173 us -> 174 us (level); the launches traced: 171 us -> 174 us
  waiting for transfers between devices: 47.4 us -> 50.3 us
  Pallas kernels: 1.27 us -> 3.13 us
    ppermute x12, starting transfers between devices: 46.4 us -> 40.3 us  [send(): return lax.ppermute(rows, ('z', 'c'), neighbour(steps))]
    ppermute x2, starting transfers between devices: 11.2 us -> 16.8 us  [on_device(): theirs = lax.ppermute(theirs, 'c', SWAP)]
    all_to_all x2, waiting for transfers between devices: 28.3 us -> 32.9 us  [exchange(): lax.all_to_all(rows.astype(jnp.bfloat16).reshape(node_count, capacity, wi...]
    pallas_call x0 -> x2, Pallas kernels: none -> 1.86 us  [place_sum(): pl.pallas_call(functools.partial(place_kernel, start), in_specs=[in_vmem,...]
    all_to_all x2, starting transfers between devices: 16.3 us -> 18.1 us  [exchange(): lax.all_to_all(rows.astype(jnp.bfloat16).reshape(node_count, capacity, wi...]
  transfers between devices with their start and end apart: 18 -> 18, of which waited for: 8 -> 6; matrix products, arithmetic and copies ran while one was open for 2% -> 2% of each run, Pallas kernels for 0% -> 1%
where the time goes in v10:
time: 174 us
  starting transfers between devices  89.6 us (51%)
  waiting for transfers between devices  50.3 us (29%)
  blocking collectives  19.7 us (11%)
  local copies, waits for them, and re-layouts  5.13 us (3%)
  Pallas kernels  3.13 us (2%)
  matrix products  2.87 us (2%)
  other arithmetic  1.87 us (1%)
    ppermute x12, starting transfers between devices, send(): return lax.ppermute(rows, ('z', 'c'), neighbour(steps))  40.3 us
    all_to_all x2, waiting for transfers between devices, exchange(): lax.all_to_all(rows.astype(jnp.bfloat16).reshape(node_count, capacity, wi...  32.9 us
    all_gather x1, blocking collectives, on_device(): lax.all_gather(rows, 'z', axis=0, tiled=True, axis_index_groups=GROUPS)  19.7 us
    all_to_all x2, starting transfers between devices, exchange(): lax.all_to_all(rows.astype(jnp.bfloat16).reshape(node_count, capacity, wi...  18.1 us
    ppermute x2, starting transfers between devices, on_device(): theirs = lax.ppermute(theirs, 'c', SWAP)  16.8 us
    ppermute x12, waiting for transfers between devices, send(): return lax.ppermute(rows, ('z', 'c'), neighbour(steps))  16.4 us
    ppermute x1, starting transfers between devices, on_device(): other_grads = lax.ppermute(grads, 'c', SWAP)  12.4 us
  transfers between devices with their start and end apart: 18, of which 6 were waited for; matrix products, arithmetic and copies ran while one was open for 2% of the time, Pallas kernels for 1%

profile of v10, /device:TPU:1, one launch (start us, length us, event | category | flops | bytes accessed | tf_op | source)
XLA Modules:
  0.0 173.7 jit_solution(14009124850329217822)
XLA Ops:
  0.6 12.4 %collective-permute-start.1 = (bf16[128,5376]{1,0:T(8,128)(2,1)}, bf16[128,5376]{1,0:T(8,128)(2,1)S(1)}, u32[]{:S(2)}, u32[]{:S(2)}) collective-permute-start(bf16[128,5376]{1,0:T(8,128)(2,1)} %own_ref.1), channel_id=1, source_target_pairs={{0,1},{1,0},{2,3},{3,2},{4,5},{5,4},{6,7},{7,6},{8,9},{9,8},{10,11... | collective-permute-start | bytes 4128776 | tf_op jit(solution)/shard_map/ppermute | solution.py:129
  13.1 1.9 %collective-permute-start = (s32[128]{0:T(128)}, s32[128]{0:T(128)S(1)}, u32[]{:S(2)}, u32[]{:S(2)}) collective-permute-start(s32[128]{0:T(128)} %param.9), channel_id=1, source_target_pairs={{0,1},{1,0},{2,3},{3,2},{4,5},{5,4},{6,7},{7,6},{8,9},{9,8},{10,11... | collective-permute-start | bytes 1544 | tf_op jit(solution)/shard_map/ppermute | solution.py:130
  15.3 1.0 collective-permute-done
  16.2 1.3 copy-done
  17.6 0.7 copy-done.1
  18.2 1.3 shard_map.111
  19.5 5.3 %collective-permute-start.3 = (bf16[32,5376]{1,0:T(8,128)(2,1)S(1)}, bf16[32,5376]{1,0:T(8,128)(2,1)S(1)}, u32[]{:S(2)}, u32[]{:S(2)}) collective-permute-start(bf16[32,5376]{1,0:T(8,128)(2,1)S(1)} %get-tuple-element.21), channel_id=1, source_target_pairs={{0,2},{1,23},{2,4},{3,1},{4,6},{5,3},{6,8},{7,5},{8,10},{9,7},{10,... | collective-permute-start | bytes 1032200 | tf_op jit(solution)/shard_map/ppermute | solution.py:148
  25.0 2.2 %collective-permute-start.8 = (bf16[16,5376]{1,0:T(8,128)(2,1)S(1)}, bf16[16,5376]{1,0:T(8,128)(2,1)S(1)}, u32[]{:S(2)}, u32[]{:S(2)}) collective-permute-start(bf16[16,5376]{1,0:T(8,128)(2,1)S(1)} %get-tuple-element.27), channel_id=1, source_target_pairs={{0,2},{1,23},{2,4},{3,1},{4,6},{5,3},{6,8},{7,5},{8,10},{9,7},{10,... | collective-permute-start | bytes 516104 | tf_op jit(solution)/shard_map/ppermute | solution.py:148
  27.2 3.1 %collective-permute-start.2 = (bf16[32,5376]{1,0:T(8,128)(2,1)S(1)}, bf16[32,5376]{1,0:T(8,128)(2,1)S(1)}, u32[]{:S(2)}, u32[]{:S(2)}) collective-permute-start(bf16[32,5376]{1,0:T(8,128)(2,1)S(1)} %get-tuple-element.19), channel_id=1, source_target_pairs={{0,22},{1,3},{2,0},{3,5},{4,2},{5,7},{6,4},{7,9},{8,6},{9,11},{10,... | collective-permute-start | bytes 1032200 | tf_op jit(solution)/shard_map/ppermute | solution.py:148
  30.4 3.7 %collective-permute-start.4 = (bf16[32,5376]{1,0:T(8,128)(2,1)S(1)}, bf16[32,5376]{1,0:T(8,128)(2,1)S(1)}, u32[]{:S(2)}, u32[]{:S(2)}) collective-permute-start(bf16[32,5376]{1,0:T(8,128)(2,1)S(1)} %add_convert_fusion), channel_id=1, source_target_pairs={{0,2},{1,23},{2,4},{3,1},{4,6},{5,3},{6,8},{7,5},{8,10},{9,7},{10,... | collective-permute-start | bytes 1032200 | tf_op jit(solution)/shard_map/ppermute | solution.py:148
  34.1 2.7 %collective-permute-start.9 = (bf16[16,5376]{1,0:T(8,128)(2,1)S(1)}, bf16[16,5376]{1,0:T(8,128)(2,1)S(1)}, u32[]{:S(2)}, u32[]{:S(2)}) collective-permute-start(bf16[16,5376]{1,0:T(8,128)(2,1)S(1)} %add_convert_fusion.2), channel_id=1, source_target_pairs={{0,2},{1,23},{2,4},{3,1},{4,6},{5,3},{6,8},{7,5},{8,10},{9,7},{10,... | collective-permute-start | bytes 516104 | tf_op jit(solution)/shard_map/ppermute | solution.py:148
  36.9 2.5 %collective-permute-start.7 = (bf16[16,5376]{1,0:T(8,128)(2,1)S(1)}, bf16[16,5376]{1,0:T(8,128)(2,1)S(1)}, u32[]{:S(2)}, u32[]{:S(2)}) collective-permute-start(bf16[16,5376]{1,0:T(8,128)(2,1)S(1)} %get-tuple-element.25), channel_id=1, source_target_pairs={{0,22},{1,3},{2,0},{3,5},{4,2},{5,7},{6,4},{7,9},{8,6},{9,11},{10,... | collective-permute-start | bytes 516104 | tf_op jit(solution)/shard_map/ppermute | solution.py:148
  39.6 4.9 %collective-permute-start.5 = (bf16[16,5376]{1,0:T(8,128)(2,1)S(1)}, bf16[16,5376]{1,0:T(8,128)(2,1)S(1)}, u32[]{:S(2)}, u32[]{:S(2)}) collective-permute-start(bf16[16,5376]{1,0:T(8,128)(2,1)S(1)} %get-tuple-element.32), channel_id=1, source_target_pairs={{0,8},{1,17},{2,10},{3,19},{4,12},{5,21},{6,14},{7,23},{8,16},{9,1... | collective-permute-start | bytes 516104 | tf_op jit(solution)/shard_map/ppermute | solution.py:148
  44.5 4.3 %collective-permute-start.6 = (bf16[16,5376]{1,0:T(8,128)(2,1)S(1)}, bf16[16,5376]{1,0:T(8,128)(2,1)S(1)}, u32[]{:S(2)}, u32[]{:S(2)}) collective-permute-start(bf16[16,5376]{1,0:T(8,128)(2,1)S(1)} %get-tuple-element.33), channel_id=1, source_target_pairs={{0,16},{1,9},{2,18},{3,11},{4,20},{5,13},{6,22},{7,15},{8,0},{9,17... | collective-permute-start | bytes 516104 | tf_op jit(solution)/shard_map/ppermute | solution.py:148
  48.9 12.1 %collective-permute-done.5 = bf16[16,5376]{1,0:T(8,128)(2,1)S(1)} collective-permute-done((bf16[16,5376]{1,0:T(8,128)(2,1)S(1)}, bf16[16,5376]{1,0:T(8,128)(2,1)S(1)}, u32[]{:S(2)}, u32[]{:S(2)}) %collective-permute-start.5) | collective-permute-done | bytes 172064 | tf_op jit(solution)/shard_map/ppermute | solution.py:148
  61.0 3.6 %collective-permute-done.6 = bf16[16,5376]{1,0:T(8,128)(2,1)S(1)} collective-permute-done((bf16[16,5376]{1,0:T(8,128)(2,1)S(1)}, bf16[16,5376]{1,0:T(8,128)(2,1)S(1)}, u32[]{:S(2)}, u32[]{:S(2)}) %collective-permute-start.6) | collective-permute-done | bytes 172064 | tf_op jit(solution)/shard_map/ppermute | solution.py:148
  64.9 1.1 reshape.68
  66.1 9.7 %all-to-all-start = ((bf16[32,2,5376]{2,1,0:T(2,128)(2,1)}), bf16[32,2,5376]{2,1,0:T(2,128)(2,1)S(1)}, u32[]{:S(2)}, u32[]{:S(2)}) async-start(bf16[32,2,5376]{2,1,0:T(2,128)(2,1)} %reshape.68), calls=%async_computation | async-start | bytes 1376256 | tf_op jit(solution)/shard_map/all_to_all | solution.py:183
  76.0 16.9 %all-to-all-done = bf16[32,2,5376]{2,1,0:T(2,128)(2,1)S(1)} async-done(((bf16[32,2,5376]{2,1,0:T(2,128)(2,1)}), bf16[32,2,5376]{2,1,0:T(2,128)(2,1)S(1)}, u32[]{:S(2)}, u32[]{:S(2)}) %all-to-all-start) | async-done | bytes 688160 | tf_op jit(solution)/shard_map/all_to_all | solution.py:183
  93.9 1.1 reshape.70
  95.0 8.5 %all-to-all-start.1 = ((bf16[32,2,5376]{2,1,0:T(2,128)(2,1)}), bf16[32,2,5376]{2,1,0:T(2,128)(2,1)S(1)}, u32[]{:S(2)}, u32[]{:S(2)}) async-start(bf16[32,2,5376]{2,1,0:T(2,128)(2,1)} %reshape.70), calls=%async_computation.1 | async-start | bytes 1376256 | tf_op jit(solution)/shard_map/all_to_all | solution.py:183
  103.5 1.1 subtract_select_fusion
  104.6 16.0 %all-to-all-done.1 = bf16[32,2,5376]{2,1,0:T(2,128)(2,1)S(1)} async-done(((bf16[32,2,5376]{2,1,0:T(2,128)(2,1)}), bf16[32,2,5376]{2,1,0:T(2,128)(2,1)S(1)}, u32[]{:S(2)}, u32[]{:S(2)}) %all-to-all-start.1) | async-done | bytes 688160 | tf_op jit(solution)/shard_map/all_to_all | solution.py:183
  121.2 19.7 %all_gather.3 = bf16[64,5376]{1,0:T(8,128)(2,1)S(1)} all-gather(bf16[16,5376]{1,0:T(8,128)(2,1)S(1)} %convolution_convert_fusion.2), channel_id=1, replica_groups={{0,6,12,18},{2,8,14,20},{4,10,16,22},{1,7,13,19},{3,9,15,21},{5,11,17,2..., dimensions={0}, use_global_device_ids=true | all-gather | bytes 860160 | tf_op jit(solution)/shard_map/all_gather | solution.py:202
  140.9 3.2 %collective-permute-start.14 = (bf16[64,2688]{1,0:T(8,128)(2,1)S(1)}, bf16[64,2688]{1,0:T(8,128)(2,1)S(1)}, u32[]{:S(2)}, u32[]{:S(2)}) collective-permute-start(bf16[64,2688]{1,0:T(8,128)(2,1)S(1)} %get-tuple-element.37), channel_id=1, source_target_pairs={{0,2},{1,23},{2,4},{3,1},{4,6},{5,3},{6,8},{7,5},{8,10},{9,7},{10,... | collective-permute-start | bytes 1032200 | tf_op jit(solution)/shard_map/ppermute | solution.py:148
  144.1 2.1 %collective-permute-start.13 = (bf16[64,2688]{1,0:T(8,128)(2,1)S(1)}, bf16[64,2688]{1,0:T(8,128)(2,1)S(1)}, u32[]{:S(2)}, u32[]{:S(2)}) collective-permute-start(bf16[64,2688]{1,0:T(8,128)(2,1)S(1)} %get-tuple-element.37), channel_id=1, source_target_pairs={{0,22},{1,3},{2,0},{3,5},{4,2},{5,7},{6,4},{7,9},{8,6},{9,11},{10,... | collective-permute-start | bytes 1032200 | tf_op jit(solution)/shard_map/ppermute | solution.py:148
  146.3 4.4 %collective-permute-start.11 = (bf16[64,2688]{1,0:T(8,128)(2,1)S(1)}, bf16[64,2688]{1,0:T(8,128)(2,1)S(1)}, u32[]{:S(2)}, u32[]{:S(2)}) collective-permute-start(bf16[64,2688]{1,0:T(8,128)(2,1)S(1)} %get-tuple-element.38), channel_id=1, source_target_pairs={{0,2},{1,23},{2,4},{3,1},{4,6},{5,3},{6,8},{7,5},{8,10},{9,7},{10,... | collective-permute-start | bytes 1032200 | tf_op jit(solution)/shard_map/ppermute | solution.py:148
  150.7 1.9 %collective-permute-start.10 = (bf16[64,2688]{1,0:T(8,128)(2,1)S(1)}, bf16[64,2688]{1,0:T(8,128)(2,1)S(1)}, u32[]{:S(2)}, u32[]{:S(2)}) collective-permute-start(bf16[64,2688]{1,0:T(8,128)(2,1)S(1)} %get-tuple-element.38), channel_id=1, source_target_pairs={{0,22},{1,3},{2,0},{3,5},{4,2},{5,7},{6,4},{7,9},{8,6},{9,11},{10,... | collective-permute-start | bytes 1032200 | tf_op jit(solution)/shard_map/ppermute | solution.py:148
  153.7 12.6 %collective-permute-start.15 = (bf16[128,2688]{1,0:T(8,128)(2,1)S(1)}, bf16[128,2688]{1,0:T(8,128)(2,1)S(1)}, u32[]{:S(2)}, u32[]{:S(2)}) collective-permute-start(bf16[128,2688]{1,0:T(8,128)(2,1)S(1)} %convolution_convert_fusion.3), channel_id=1, source_target_pairs={{0,1},{1,0},{2,3},{3,2},{4,5},{5,4},{6,7},{7,6},{8,9},{9,8},{10,11... | collective-permute-start | bytes 2064392 | tf_op jit(solution)/shard_map/ppermute | solution.py:218
  166.8 4.2 %collective-permute-start.12 = (bf16[128,2688]{1,0:T(8,128)(2,1)S(1)}, bf16[128,2688]{1,0:T(8,128)(2,1)S(1)}, u32[]{:S(2)}, u32[]{:S(2)}) collective-permute-start(bf16[128,2688]{1,0:T(8,128)(2,1)S(1)} %convolution_convert_fusion.5), channel_id=1, source_target_pairs={{0,1},{1,0},{2,3},{3,2},{4,5},{5,4},{6,7},{7,6},{8,9},{9,8},{10,11... | collective-permute-start | bytes 2064392 | tf_op jit(solution)/shard_map/ppermute | solution.py:218
  171.8 0.9 shard_map.112.refs_0_
  172.8 0.9 shard_map.113
  (58 shorter events, 5.2 us)
Async XLA Ops:
  0.6 15.6 %collective-permute-start.1 = (bf16[128,5376]{1,0:T(8,128)(2,1)}, bf16[128,5376]{1,0:T(8,128)(2,1)S(1)}, u32[]{:S(2)}, u32[]{:S(2)}) collective-permute-start(bf16[128,5376]{1,0:T(8,128)(2,1)} %own_ref.1), channel_id=1, source_target_pairs={{0,1},{1,0},{2,3},{3,2},{4,5},{5,4},{6,7},{7,6},{8,9},{9,8},{10,11... | collective-permute-start | bytes 4128776 | tf_op jit(solution)/shard_map/ppermute | solution.py:129
  13.1 3.2 %collective-permute-start = (s32[128]{0:T(128)}, s32[128]{0:T(128)S(1)}, u32[]{:S(2)}, u32[]{:S(2)}) collective-permute-start(s32[128]{0:T(128)} %param.9), channel_id=1, source_target_pairs={{0,1},{1,0},{2,3},{3,2},{4,5},{5,4},{6,7},{7,6},{8,9},{9,8},{10,11... | collective-permute-start | bytes 1544 | tf_op jit(solution)/shard_map/ppermute | solution.py:130
  16.2 1.3 copy-start
  17.6 0.7 copy-start.1
  18.2 6.6 %copy-start.8 = (s32[1,16]{1,0:T(1,128)S(1)}, s32[1,16]{1,0:T(1,128)}, u32[]{:S(2)}) copy-start(s32[1,16]{1,0:T(1,128)} %param.10) | copy-start | bytes 196
  19.5 10.8 %collective-permute-start.3 = (bf16[32,5376]{1,0:T(8,128)(2,1)S(1)}, bf16[32,5376]{1,0:T(8,128)(2,1)S(1)}, u32[]{:S(2)}, u32[]{:S(2)}) collective-permute-start(bf16[32,5376]{1,0:T(8,128)(2,1)S(1)} %get-tuple-element.21), channel_id=1, source_target_pairs={{0,2},{1,23},{2,4},{3,1},{4,6},{5,3},{6,8},{7,5},{8,10},{9,7},{10,... | collective-permute-start | bytes 1032200 | tf_op jit(solution)/shard_map/ppermute | solution.py:148
  25.0 9.1 %collective-permute-start.8 = (bf16[16,5376]{1,0:T(8,128)(2,1)S(1)}, bf16[16,5376]{1,0:T(8,128)(2,1)S(1)}, u32[]{:S(2)}, u32[]{:S(2)}) collective-permute-start(bf16[16,5376]{1,0:T(8,128)(2,1)S(1)} %get-tuple-element.27), channel_id=1, source_target_pairs={{0,2},{1,23},{2,4},{3,1},{4,6},{5,3},{6,8},{7,5},{8,10},{9,7},{10,... | collective-permute-start | bytes 516104 | tf_op jit(solution)/shard_map/ppermute | solution.py:148
  27.2 12.2 %collective-permute-start.2 = (bf16[32,5376]{1,0:T(8,128)(2,1)S(1)}, bf16[32,5376]{1,0:T(8,128)(2,1)S(1)}, u32[]{:S(2)}, u32[]{:S(2)}) collective-permute-start(bf16[32,5376]{1,0:T(8,128)(2,1)S(1)} %get-tuple-element.19), channel_id=1, source_target_pairs={{0,22},{1,3},{2,0},{3,5},{4,2},{5,7},{6,4},{7,9},{8,6},{9,11},{10,... | collective-permute-start | bytes 1032200 | tf_op jit(solution)/shard_map/ppermute | solution.py:148
  30.4 9.0 %collective-permute-start.4 = (bf16[32,5376]{1,0:T(8,128)(2,1)S(1)}, bf16[32,5376]{1,0:T(8,128)(2,1)S(1)}, u32[]{:S(2)}, u32[]{:S(2)}) collective-permute-start(bf16[32,5376]{1,0:T(8,128)(2,1)S(1)} %add_convert_fusion), channel_id=1, source_target_pairs={{0,2},{1,23},{2,4},{3,1},{4,6},{5,3},{6,8},{7,5},{8,10},{9,7},{10,... | collective-permute-start | bytes 1032200 | tf_op jit(solution)/shard_map/ppermute | solution.py:148
  34.1 14.7 %collective-permute-start.9 = (bf16[16,5376]{1,0:T(8,128)(2,1)S(1)}, bf16[16,5376]{1,0:T(8,128)(2,1)S(1)}, u32[]{:S(2)}, u32[]{:S(2)}) collective-permute-start(bf16[16,5376]{1,0:T(8,128)(2,1)S(1)} %add_convert_fusion.2), channel_id=1, source_target_pairs={{0,2},{1,23},{2,4},{3,1},{4,6},{5,3},{6,8},{7,5},{8,10},{9,7},{10,... | collective-permute-start | bytes 516104 | tf_op jit(solution)/shard_map/ppermute | solution.py:148
  36.9 11.9 %collective-permute-start.7 = (bf16[16,5376]{1,0:T(8,128)(2,1)S(1)}, bf16[16,5376]{1,0:T(8,128)(2,1)S(1)}, u32[]{:S(2)}, u32[]{:S(2)}) collective-permute-start(bf16[16,5376]{1,0:T(8,128)(2,1)S(1)} %get-tuple-element.25), channel_id=1, source_target_pairs={{0,22},{1,3},{2,0},{3,5},{4,2},{5,7},{6,4},{7,9},{8,6},{9,11},{10,... | collective-permute-start | bytes 516104 | tf_op jit(solution)/shard_map/ppermute | solution.py:148
  39.6 21.4 %collective-permute-start.5 = (bf16[16,5376]{1,0:T(8,128)(2,1)S(1)}, bf16[16,5376]{1,0:T(8,128)(2,1)S(1)}, u32[]{:S(2)}, u32[]{:S(2)}) collective-permute-start(bf16[16,5376]{1,0:T(8,128)(2,1)S(1)} %get-tuple-element.32), channel_id=1, source_target_pairs={{0,8},{1,17},{2,10},{3,19},{4,12},{5,21},{6,14},{7,23},{8,16},{9,1... | collective-permute-start | bytes 516104 | tf_op jit(solution)/shard_map/ppermute | solution.py:148
  44.5 20.0 %collective-permute-start.6 = (bf16[16,5376]{1,0:T(8,128)(2,1)S(1)}, bf16[16,5376]{1,0:T(8,128)(2,1)S(1)}, u32[]{:S(2)}, u32[]{:S(2)}) collective-permute-start(bf16[16,5376]{1,0:T(8,128)(2,1)S(1)} %get-tuple-element.33), channel_id=1, source_target_pairs={{0,16},{1,9},{2,18},{3,11},{4,20},{5,13},{6,22},{7,15},{8,0},{9,17... | collective-permute-start | bytes 516104 | tf_op jit(solution)/shard_map/ppermute | solution.py:148
  64.9 10.8 %copy-start.6 = (s32[1,32,2]{1,2,0:T(2,128)S(1)}, s32[1,32,2]{1,2,0:T(2,128)}, u32[]{:S(2)}) copy-start(s32[1,32,2]{1,2,0:T(2,128)} %param.12) | copy-start | bytes 772
  64.9 11.0 %copy-start.7 = (s32[16]{0:T(128)S(1)}, s32[16]{0:T(128)}, u32[]{:S(2)}) copy-start(s32[16]{0:T(128)} %param.11) | copy-start | bytes 196
  66.1 26.9 %all-to-all-start = ((bf16[32,2,5376]{2,1,0:T(2,128)(2,1)}), bf16[32,2,5376]{2,1,0:T(2,128)(2,1)S(1)}, u32[]{:S(2)}, u32[]{:S(2)}) async-start(bf16[32,2,5376]{2,1,0:T(2,128)(2,1)} %reshape.68), calls=%async_computation | async-start | bytes 1376256 | tf_op jit(solution)/shard_map/all_to_all | solution.py:183
  75.7 17.7 %copy-start.3 = (f32[16,5376]{1,0:T(8,128)S(1)}, f32[16,5376]{1,0:T(8,128)}, u32[]{:S(2)}) copy-start(f32[16,5376]{1,0:T(8,128)} %param.15) | copy-start | bytes 1032196
  75.8 17.7 %copy-start.4 = (f32[16,5376]{1,0:T(8,128)S(1)}, f32[16,5376]{1,0:T(8,128)}, u32[]{:S(2)}) copy-start(f32[16,5376]{1,0:T(8,128)} %param.14) | copy-start | bytes 1032196
  75.8 17.7 %copy-start.5 = (f32[16,5376]{1,0:T(8,128)S(1)}, f32[16,5376]{1,0:T(8,128)}, u32[]{:S(2)}) copy-start(f32[16,5376]{1,0:T(8,128)} %param.13) | copy-start | bytes 1032196
  95.0 25.6 %all-to-all-start.1 = ((bf16[32,2,5376]{2,1,0:T(2,128)(2,1)}), bf16[32,2,5376]{2,1,0:T(2,128)(2,1)S(1)}, u32[]{:S(2)}, u32[]{:S(2)}) async-start(bf16[32,2,5376]{2,1,0:T(2,128)(2,1)} %reshape.70), calls=%async_computation.1 | async-start | bytes 1376256 | tf_op jit(solution)/shard_map/all_to_all | solution.py:183
  140.9 11.8 %collective-permute-start.14 = (bf16[64,2688]{1,0:T(8,128)(2,1)S(1)}, bf16[64,2688]{1,0:T(8,128)(2,1)S(1)}, u32[]{:S(2)}, u32[]{:S(2)}) collective-permute-start(bf16[64,2688]{1,0:T(8,128)(2,1)S(1)} %get-tuple-element.37), channel_id=1, source_target_pairs={{0,2},{1,23},{2,4},{3,1},{4,6},{5,3},{6,8},{7,5},{8,10},{9,7},{10,... | collective-permute-start | bytes 1032200 | tf_op jit(solution)/shard_map/ppermute | solution.py:148
  144.1 9.2 %collective-permute-start.13 = (bf16[64,2688]{1,0:T(8,128)(2,1)S(1)}, bf16[64,2688]{1,0:T(8,128)(2,1)S(1)}, u32[]{:S(2)}, u32[]{:S(2)}) collective-permute-start(bf16[64,2688]{1,0:T(8,128)(2,1)S(1)} %get-tuple-element.37), channel_id=1, source_target_pairs={{0,22},{1,3},{2,0},{3,5},{4,2},{5,7},{6,4},{7,9},{8,6},{9,11},{10,... | collective-permute-start | bytes 1032200 | tf_op jit(solution)/shard_map/ppermute | solution.py:148
  146.3 20.0 %collective-permute-start.11 = (bf16[64,2688]{1,0:T(8,128)(2,1)S(1)}, bf16[64,2688]{1,0:T(8,128)(2,1)S(1)}, u32[]{:S(2)}, u32[]{:S(2)}) collective-permute-start(bf16[64,2688]{1,0:T(8,128)(2,1)S(1)} %get-tuple-element.38), channel_id=1, source_target_pairs={{0,2},{1,23},{2,4},{3,1},{4,6},{5,3},{6,8},{7,5},{8,10},{9,7},{10,... | collective-permute-start | bytes 1032200 | tf_op jit(solution)/shard_map/ppermute | solution.py:148
  150.7 15.7 %collective-permute-start.10 = (bf16[64,2688]{1,0:T(8,128)(2,1)S(1)}, bf16[64,2688]{1,0:T(8,128)(2,1)S(1)}, u32[]{:S(2)}, u32[]{:S(2)}) collective-permute-start(bf16[64,2688]{1,0:T(8,128)(2,1)S(1)} %get-tuple-element.38), channel_id=1, source_target_pairs={{0,22},{1,3},{2,0},{3,5},{4,2},{5,7},{6,4},{7,9},{8,6},{9,11},{10,... | collective-permute-start | bytes 1032200 | tf_op jit(solution)/shard_map/ppermute | solution.py:148
  153.7 17.3 %copy-start.2 = (s32[128]{0:T(128)S(1)}, s32[128]{0:T(128)}, u32[]{:S(2)}) copy-start(s32[128]{0:T(128)} %param.9) | copy-start | bytes 1540
  153.7 18.1 %collective-permute-start.15 = (bf16[128,2688]{1,0:T(8,128)(2,1)S(1)}, bf16[128,2688]{1,0:T(8,128)(2,1)S(1)}, u32[]{:S(2)}, u32[]{:S(2)}) collective-permute-start(bf16[128,2688]{1,0:T(8,128)(2,1)S(1)} %convolution_convert_fusion.3), channel_id=1, source_target_pairs={{0,1},{1,0},{2,3},{3,2},{4,5},{5,4},{6,7},{7,6},{8,9},{9,8},{10,11... | collective-permute-start | bytes 2064392 | tf_op jit(solution)/shard_map/ppermute | solution.py:218
  166.8 6.0 %collective-permute-start.12 = (bf16[128,2688]{1,0:T(8,128)(2,1)S(1)}, bf16[128,2688]{1,0:T(8,128)(2,1)S(1)}, u32[]{:S(2)}, u32[]{:S(2)}) collective-permute-start(bf16[128,2688]{1,0:T(8,128)(2,1)S(1)} %convolution_convert_fusion.5), channel_id=1, source_target_pairs={{0,1},{1,0},{2,3},{3,2},{4,5},{5,4},{6,7},{7,6},{8,9},{9,8},{10,11... | collective-permute-start | bytes 2064392 | tf_op jit(solution)/shard_map/ppermute | solution.py:218

commit v11 on v10

--- a/solution.py
+++ b/solution.py
@@ -23,7 +23,7 @@
 GROUP = Z_SIZE // APART
 GROUPS = [[r + APART * k for k in range(GROUP)] for r in range(APART)]
 BLOCK_COLS = 896
-LAST_PARTS = 2
+LAST_CUTS = (0, 3584, 5376)
 
 SWAP = [(0, 1), (1, 0)]
 
@@ -201,22 +201,14 @@
 
     here = lax.all_gather(rows, "z", axis=0, tiled=True, axis_index_groups=GROUPS)
     own_choice, other_choice = matches(token_slot, listed), matches(other_slot, listed)
-    step = width // LAST_PARTS
-    halves = [here[:, i * step : (i + 1) * step] for i in range(LAST_PARTS)]
-    arrived = [
-        (
-            half,
-            send(half, -1),
-            send(half, 1),
-        )
-        for half in halves
-    ]
+    pieces = [here[:, start:end] for start, end in zip(LAST_CUTS, LAST_CUTS[1:])]
+    arrived = [(piece, send(piece, -1), send(piece, 1)) for piece in pieces]
     token_rows = None
     for i, gathered in enumerate(map(jnp.concatenate, arrived)):
         theirs = dot32(other_choice, gathered).astype(jnp.bfloat16)
         mine = dot32(own_choice, gathered).astype(jnp.bfloat16)
         theirs = lax.ppermute(theirs, "c", SWAP)
-        token_rows = place_sum(mine, theirs, i * step, width, token_rows)
+        token_rows = place_sum(mine, theirs, LAST_CUTS[i], width, token_rows)
     return token_rows, moment_out, second_out, master_out
 
 

time: 174 us -> 175 us (level)
    ppermute x2, starting transfers between devices: 16.8 us -> 13.2 us  [on_device(): theirs = lax.ppermute(theirs, 'c', SWAP)]
    ppermute x12, starting transfers between devices: 40.3 us -> 43.8 us  [send(): return lax.ppermute(rows, ('z', 'c'), neighbour(steps))]
where the time goes in v11:
time: 175 us; the launch traced here: 174 us
  starting transfers between devices  89.3 us (51%)
  waiting for transfers between devices  50.9 us (29%)
  blocking collectives  19.3 us (11%)
  local copies, waits for them, and re-layouts  5.13 us (3%)
  Pallas kernels  3.16 us (2%)
  matrix products  2.83 us (2%)
  other arithmetic  1.87 us (1%)
    ppermute x12, starting transfers between devices, send(): return lax.ppermute(rows, ('z', 'c'), neighbour(steps))  43.8 us
    all_to_all x2, waiting for transfers between devices, exchange(): lax.all_to_all(rows.astype(jnp.bfloat16).reshape(node_count, capacity, wi...  33 us
    all_gather x1, blocking collectives, on_device(): lax.all_gather(rows, 'z', axis=0, tiled=True, axis_index_groups=GROUPS)  19.3 us
    all_to_all x2, starting transfers between devices, exchange(): lax.all_to_all(rows.astype(jnp.bfloat16).reshape(node_count, capacity, wi...  18 us
    ppermute x12, waiting for transfers between devices, send(): return lax.ppermute(rows, ('z', 'c'), neighbour(steps))  16.9 us
    ppermute x2, starting transfers between devices, on_device(): theirs = lax.ppermute(theirs, 'c', SWAP)  13.2 us
    ppermute x1, starting transfers between devices, on_device(): other_grads = lax.ppermute(grads, 'c', SWAP)  12.4 us
  transfers between devices with their start and end apart: 18, of which 6 were waited for; matrix products, arithmetic and copies ran while one was open for 2% of the time, Pallas kernels for 1%

profile of v11, /device:TPU:1, one launch (start us, length us, event | category | flops | bytes accessed | tf_op | source)
XLA Modules:
  0.0 173.6 jit_solution(12140842380814828408)
XLA Ops:
  0.6 12.4 %collective-permute-start.1 = (bf16[128,5376]{1,0:T(8,128)(2,1)}, bf16[128,5376]{1,0:T(8,128)(2,1)S(1)}, u32[]{:S(2)}, u32[]{:S(2)}) collective-permute-start(bf16[128,5376]{1,0:T(8,128)(2,1)} %own_ref.1), channel_id=1, source_target_pairs={{0,1},{1,0},{2,3},{3,2},{4,5},{5,4},{6,7},{7,6},{8,9},{9,8},{10,11... | collective-permute-start | bytes 4128776 | tf_op jit(solution)/shard_map/ppermute | solution.py:129
  13.1 1.9 %collective-permute-start = (s32[128]{0:T(128)}, s32[128]{0:T(128)S(1)}, u32[]{:S(2)}, u32[]{:S(2)}) collective-permute-start(s32[128]{0:T(128)} %param.9), channel_id=1, source_target_pairs={{0,1},{1,0},{2,3},{3,2},{4,5},{5,4},{6,7},{7,6},{8,9},{9,8},{10,11... | collective-permute-start | bytes 1544 | tf_op jit(solution)/shard_map/ppermute | solution.py:130
  15.3 1.0 collective-permute-done
  16.2 1.3 copy-done
  18.2 1.3 shard_map.111
  19.5 5.3 %collective-permute-start.3 = (bf16[32,5376]{1,0:T(8,128)(2,1)S(1)}, bf16[32,5376]{1,0:T(8,128)(2,1)S(1)}, u32[]{:S(2)}, u32[]{:S(2)}) collective-permute-start(bf16[32,5376]{1,0:T(8,128)(2,1)S(1)} %get-tuple-element.21), channel_id=1, source_target_pairs={{0,2},{1,23},{2,4},{3,1},{4,6},{5,3},{6,8},{7,5},{8,10},{9,7},{10,... | collective-permute-start | bytes 1032200 | tf_op jit(solution)/shard_map/ppermute | solution.py:148
  25.0 1.9 %collective-permute-start.2 = (bf16[32,5376]{1,0:T(8,128)(2,1)S(1)}, bf16[32,5376]{1,0:T(8,128)(2,1)S(1)}, u32[]{:S(2)}, u32[]{:S(2)}) collective-permute-start(bf16[32,5376]{1,0:T(8,128)(2,1)S(1)} %get-tuple-element.19), channel_id=1, source_target_pairs={{0,22},{1,3},{2,0},{3,5},{4,2},{5,7},{6,4},{7,9},{8,6},{9,11},{10,... | collective-permute-start | bytes 1032200 | tf_op jit(solution)/shard_map/ppermute | solution.py:148
  26.9 4.6 %collective-permute-start.8 = (bf16[16,5376]{1,0:T(8,128)(2,1)S(1)}, bf16[16,5376]{1,0:T(8,128)(2,1)S(1)}, u32[]{:S(2)}, u32[]{:S(2)}) collective-permute-start(bf16[16,5376]{1,0:T(8,128)(2,1)S(1)} %get-tuple-element.27), channel_id=1, source_target_pairs={{0,2},{1,23},{2,4},{3,1},{4,6},{5,3},{6,8},{7,5},{8,10},{9,7},{10,... | collective-permute-start | bytes 516104 | tf_op jit(solution)/shard_map/ppermute | solution.py:148
  31.6 3.6 %collective-permute-start.4 = (bf16[32,5376]{1,0:T(8,128)(2,1)S(1)}, bf16[32,5376]{1,0:T(8,128)(2,1)S(1)}, u32[]{:S(2)}, u32[]{:S(2)}) collective-permute-start(bf16[32,5376]{1,0:T(8,128)(2,1)S(1)} %add_convert_fusion), channel_id=1, source_target_pairs={{0,2},{1,23},{2,4},{3,1},{4,6},{5,3},{6,8},{7,5},{8,10},{9,7},{10,... | collective-permute-start | bytes 1032200 | tf_op jit(solution)/shard_map/ppermute | solution.py:148
  35.2 4.3 %collective-permute-start.9 = (bf16[16,5376]{1,0:T(8,128)(2,1)S(1)}, bf16[16,5376]{1,0:T(8,128)(2,1)S(1)}, u32[]{:S(2)}, u32[]{:S(2)}) collective-permute-start(bf16[16,5376]{1,0:T(8,128)(2,1)S(1)} %add_convert_fusion.2), channel_id=1, source_target_pairs={{0,2},{1,23},{2,4},{3,1},{4,6},{5,3},{6,8},{7,5},{8,10},{9,7},{10,... | collective-permute-start | bytes 516104 | tf_op jit(solution)/shard_map/ppermute | solution.py:148
  39.6 1.9 %collective-permute-start.7 = (bf16[16,5376]{1,0:T(8,128)(2,1)S(1)}, bf16[16,5376]{1,0:T(8,128)(2,1)S(1)}, u32[]{:S(2)}, u32[]{:S(2)}) collective-permute-start(bf16[16,5376]{1,0:T(8,128)(2,1)S(1)} %get-tuple-element.25), channel_id=1, source_target_pairs={{0,22},{1,3},{2,0},{3,5},{4,2},{5,7},{6,4},{7,9},{8,6},{9,11},{10,... | collective-permute-start | bytes 516104 | tf_op jit(solution)/shard_map/ppermute | solution.py:148
  41.7 3.9 %collective-permute-start.5 = (bf16[16,5376]{1,0:T(8,128)(2,1)S(1)}, bf16[16,5376]{1,0:T(8,128)(2,1)S(1)}, u32[]{:S(2)}, u32[]{:S(2)}) collective-permute-start(bf16[16,5376]{1,0:T(8,128)(2,1)S(1)} %get-tuple-element.32), channel_id=1, source_target_pairs={{0,8},{1,17},{2,10},{3,19},{4,12},{5,21},{6,14},{7,23},{8,16},{9,1... | collective-permute-start | bytes 516104 | tf_op jit(solution)/shard_map/ppermute | solution.py:148
  45.6 5.2 %collective-permute-start.6 = (bf16[16,5376]{1,0:T(8,128)(2,1)S(1)}, bf16[16,5376]{1,0:T(8,128)(2,1)S(1)}, u32[]{:S(2)}, u32[]{:S(2)}) collective-permute-start(bf16[16,5376]{1,0:T(8,128)(2,1)S(1)} %get-tuple-element.33), channel_id=1, source_target_pairs={{0,16},{1,9},{2,18},{3,11},{4,20},{5,13},{6,22},{7,15},{8,0},{9,17... | collective-permute-start | bytes 516104 | tf_op jit(solution)/shard_map/ppermute | solution.py:148
  50.9 10.3 %collective-permute-done.5 = bf16[16,5376]{1,0:T(8,128)(2,1)S(1)} collective-permute-done((bf16[16,5376]{1,0:T(8,128)(2,1)S(1)}, bf16[16,5376]{1,0:T(8,128)(2,1)S(1)}, u32[]{:S(2)}, u32[]{:S(2)}) %collective-permute-start.5) | collective-permute-done | bytes 172064 | tf_op jit(solution)/shard_map/ppermute | solution.py:148
  61.2 5.9 %collective-permute-done.6 = bf16[16,5376]{1,0:T(8,128)(2,1)S(1)} collective-permute-done((bf16[16,5376]{1,0:T(8,128)(2,1)S(1)}, bf16[16,5376]{1,0:T(8,128)(2,1)S(1)}, u32[]{:S(2)}, u32[]{:S(2)}) %collective-permute-start.6) | collective-permute-done | bytes 172064 | tf_op jit(solution)/shard_map/ppermute | solution.py:148
  67.5 1.1 reshape.68
  68.6 9.7 %all-to-all-start = ((bf16[32,2,5376]{2,1,0:T(2,128)(2,1)}), bf16[32,2,5376]{2,1,0:T(2,128)(2,1)S(1)}, u32[]{:S(2)}, u32[]{:S(2)}) async-start(bf16[32,2,5376]{2,1,0:T(2,128)(2,1)} %reshape.68), calls=%async_computation | async-start | bytes 1376256 | tf_op jit(solution)/shard_map/all_to_all | solution.py:183
  78.6 17.0 %all-to-all-done = bf16[32,2,5376]{2,1,0:T(2,128)(2,1)S(1)} async-done(((bf16[32,2,5376]{2,1,0:T(2,128)(2,1)}), bf16[32,2,5376]{2,1,0:T(2,128)(2,1)S(1)}, u32[]{:S(2)}, u32[]{:S(2)}) %all-to-all-start) | async-done | bytes 688160 | tf_op jit(solution)/shard_map/all_to_all | solution.py:183
  96.6 1.1 reshape.70
  97.7 8.3 %all-to-all-start.1 = ((bf16[32,2,5376]{2,1,0:T(2,128)(2,1)}), bf16[32,2,5376]{2,1,0:T(2,128)(2,1)S(1)}, u32[]{:S(2)}, u32[]{:S(2)}) async-start(bf16[32,2,5376]{2,1,0:T(2,128)(2,1)} %reshape.70), calls=%async_computation.1 | async-start | bytes 1376256 | tf_op jit(solution)/shard_map/all_to_all | solution.py:183
  106.0 1.1 subtract_select_fusion
  107.2 16.0 %all-to-all-done.1 = bf16[32,2,5376]{2,1,0:T(2,128)(2,1)S(1)} async-done(((bf16[32,2,5376]{2,1,0:T(2,128)(2,1)}), bf16[32,2,5376]{2,1,0:T(2,128)(2,1)S(1)}, u32[]{:S(2)}, u32[]{:S(2)}) %all-to-all-start.1) | async-done | bytes 688160 | tf_op jit(solution)/shard_map/all_to_all | solution.py:183
  123.7 19.3 %all_gather.3 = bf16[64,5376]{1,0:T(8,128)(2,1)S(1)} all-gather(bf16[16,5376]{1,0:T(8,128)(2,1)S(1)} %convolution_convert_fusion.2), channel_id=1, replica_groups={{0,6,12,18},{2,8,14,20},{4,10,16,22},{1,7,13,19},{3,9,15,21},{5,11,17,2..., dimensions={0}, use_global_device_ids=true | all-gather | bytes 860160 | tf_op jit(solution)/shard_map/all_gather | solution.py:202
  143.0 1.9 %collective-permute-start.13 = (bf16[64,3584]{1,0:T(8,128)(2,1)S(1)}, bf16[64,3584]{1,0:T(8,128)(2,1)S(1)}, u32[]{:S(2)}, u32[]{:S(2)}) collective-permute-start(bf16[64,3584]{1,0:T(8,128)(2,1)S(1)} %slice.37), channel_id=1, source_target_pairs={{0,22},{1,3},{2,0},{3,5},{4,2},{5,7},{6,4},{7,9},{8,6},{9,11},{10,... | collective-permute-start | bytes 1376264 | tf_op jit(solution)/shard_map/ppermute | solution.py:148
  144.9 4.6 %collective-permute-start.14 = (bf16[64,3584]{1,0:T(8,128)(2,1)S(1)}, bf16[64,3584]{1,0:T(8,128)(2,1)S(1)}, u32[]{:S(2)}, u32[]{:S(2)}) collective-permute-start(bf16[64,3584]{1,0:T(8,128)(2,1)S(1)} %slice.37), channel_id=1, source_target_pairs={{0,2},{1,23},{2,4},{3,1},{4,6},{5,3},{6,8},{7,5},{8,10},{9,7},{10,... | collective-permute-start | bytes 1376264 | tf_op jit(solution)/shard_map/ppermute | solution.py:148
  149.7 1.9 %collective-permute-start.10 = (bf16[64,1792]{1,0:T(8,128)(2,1)S(1)}, bf16[64,1792]{1,0:T(8,128)(2,1)S(1)}, u32[]{:S(2)}, u32[]{:S(2)}) collective-permute-start(bf16[64,1792]{1,0:T(8,128)(2,1)S(1)} %slice.36), channel_id=1, source_target_pairs={{0,22},{1,3},{2,0},{3,5},{4,2},{5,7},{6,4},{7,9},{8,6},{9,11},{10,... | collective-permute-start | bytes 688136 | tf_op jit(solution)/shard_map/ppermute | solution.py:148
  151.6 4.6 %collective-permute-start.11 = (bf16[64,1792]{1,0:T(8,128)(2,1)S(1)}, bf16[64,1792]{1,0:T(8,128)(2,1)S(1)}, u32[]{:S(2)}, u32[]{:S(2)}) collective-permute-start(bf16[64,1792]{1,0:T(8,128)(2,1)S(1)} %slice.36), channel_id=1, source_target_pairs={{0,2},{1,23},{2,4},{3,1},{4,6},{5,3},{6,8},{7,5},{8,10},{9,7},{10,... | collective-permute-start | bytes 688136 | tf_op jit(solution)/shard_map/ppermute | solution.py:148
  156.2 0.7 collective-permute-done.14
  157.3 8.9 %collective-permute-start.15 = (bf16[128,3584]{1,0:T(8,128)(2,1)S(1)}, bf16[128,3584]{1,0:T(8,128)(2,1)S(1)}, u32[]{:S(2)}, u32[]{:S(2)}) collective-permute-start(bf16[128,3584]{1,0:T(8,128)(2,1)S(1)} %convolution_convert_fusion.3), channel_id=1, source_target_pairs={{0,1},{1,0},{2,3},{3,2},{4,5},{5,4},{6,7},{7,6},{8,9},{9,8},{10,11... | collective-permute-start | bytes 2752520 | tf_op jit(solution)/shard_map/ppermute | solution.py:210
  166.6 4.3 %collective-permute-start.12 = (bf16[128,1792]{1,0:T(8,128)(2,1)S(1)}, bf16[128,1792]{1,0:T(8,128)(2,1)S(1)}, u32[]{:S(2)}, u32[]{:S(2)}) collective-permute-start(bf16[128,1792]{1,0:T(8,128)(2,1)S(1)} %convolution_convert_fusion.5), channel_id=1, source_target_pairs={{0,1},{1,0},{2,3},{3,2},{4,5},{5,4},{6,7},{7,6},{8,9},{9,8},{10,11... | collective-permute-start | bytes 1376264 | tf_op jit(solution)/shard_map/ppermute | solution.py:210
  171.7 1.1 shard_map.112.refs_0_
  172.7 0.8 shard_map.113
  (59 shorter events, 5.2 us)
Async XLA Ops:
  0.6 15.6 %collective-permute-start.1 = (bf16[128,5376]{1,0:T(8,128)(2,1)}, bf16[128,5376]{1,0:T(8,128)(2,1)S(1)}, u32[]{:S(2)}, u32[]{:S(2)}) collective-permute-start(bf16[128,5376]{1,0:T(8,128)(2,1)} %own_ref.1), channel_id=1, source_target_pairs={{0,1},{1,0},{2,3},{3,2},{4,5},{5,4},{6,7},{7,6},{8,9},{9,8},{10,11... | collective-permute-start | bytes 4128776 | tf_op jit(solution)/shard_map/ppermute | solution.py:129
  13.1 3.2 %collective-permute-start = (s32[128]{0:T(128)}, s32[128]{0:T(128)S(1)}, u32[]{:S(2)}, u32[]{:S(2)}) collective-permute-start(s32[128]{0:T(128)} %param.9), channel_id=1, source_target_pairs={{0,1},{1,0},{2,3},{3,2},{4,5},{5,4},{6,7},{7,6},{8,9},{9,8},{10,11... | collective-permute-start | bytes 1544 | tf_op jit(solution)/shard_map/ppermute | solution.py:130
  16.2 1.3 copy-start
  17.6 0.7 copy-start.1
  18.2 6.6 %copy-start.8 = (s32[1,16]{1,0:T(1,128)S(1)}, s32[1,16]{1,0:T(1,128)}, u32[]{:S(2)}) copy-start(s32[1,16]{1,0:T(1,128)} %param.10) | copy-start | bytes 196
  19.5 12.0 %collective-permute-start.3 = (bf16[32,5376]{1,0:T(8,128)(2,1)S(1)}, bf16[32,5376]{1,0:T(8,128)(2,1)S(1)}, u32[]{:S(2)}, u32[]{:S(2)}) collective-permute-start(bf16[32,5376]{1,0:T(8,128)(2,1)S(1)} %get-tuple-element.21), channel_id=1, source_target_pairs={{0,2},{1,23},{2,4},{3,1},{4,6},{5,3},{6,8},{7,5},{8,10},{9,7},{10,... | collective-permute-start | bytes 1032200 | tf_op jit(solution)/shard_map/ppermute | solution.py:148
  25.0 16.5 %collective-permute-start.2 = (bf16[32,5376]{1,0:T(8,128)(2,1)S(1)}, bf16[32,5376]{1,0:T(8,128)(2,1)S(1)}, u32[]{:S(2)}, u32[]{:S(2)}) collective-permute-start(bf16[32,5376]{1,0:T(8,128)(2,1)S(1)} %get-tuple-element.19), channel_id=1, source_target_pairs={{0,22},{1,3},{2,0},{3,5},{4,2},{5,7},{6,4},{7,9},{8,6},{9,11},{10,... | collective-permute-start | bytes 1032200 | tf_op jit(solution)/shard_map/ppermute | solution.py:148
  26.9 8.2 %collective-permute-start.8 = (bf16[16,5376]{1,0:T(8,128)(2,1)S(1)}, bf16[16,5376]{1,0:T(8,128)(2,1)S(1)}, u32[]{:S(2)}, u32[]{:S(2)}) collective-permute-start(bf16[16,5376]{1,0:T(8,128)(2,1)S(1)} %get-tuple-element.27), channel_id=1, source_target_pairs={{0,2},{1,23},{2,4},{3,1},{4,6},{5,3},{6,8},{7,5},{8,10},{9,7},{10,... | collective-permute-start | bytes 516104 | tf_op jit(solution)/shard_map/ppermute | solution.py:148
  31.6 9.9 %collective-permute-start.4 = (bf16[32,5376]{1,0:T(8,128)(2,1)S(1)}, bf16[32,5376]{1,0:T(8,128)(2,1)S(1)}, u32[]{:S(2)}, u32[]{:S(2)}) collective-permute-start(bf16[32,5376]{1,0:T(8,128)(2,1)S(1)} %add_convert_fusion), channel_id=1, source_target_pairs={{0,2},{1,23},{2,4},{3,1},{4,6},{5,3},{6,8},{7,5},{8,10},{9,7},{10,... | collective-permute-start | bytes 1032200 | tf_op jit(solution)/shard_map/ppermute | solution.py:148
  35.2 15.6 %collective-permute-start.9 = (bf16[16,5376]{1,0:T(8,128)(2,1)S(1)}, bf16[16,5376]{1,0:T(8,128)(2,1)S(1)}, u32[]{:S(2)}, u32[]{:S(2)}) collective-permute-start(bf16[16,5376]{1,0:T(8,128)(2,1)S(1)} %add_convert_fusion.2), channel_id=1, source_target_pairs={{0,2},{1,23},{2,4},{3,1},{4,6},{5,3},{6,8},{7,5},{8,10},{9,7},{10,... | collective-permute-start | bytes 516104 | tf_op jit(solution)/shard_map/ppermute | solution.py:148
  39.6 11.3 %collective-permute-start.7 = (bf16[16,5376]{1,0:T(8,128)(2,1)S(1)}, bf16[16,5376]{1,0:T(8,128)(2,1)S(1)}, u32[]{:S(2)}, u32[]{:S(2)}) collective-permute-start(bf16[16,5376]{1,0:T(8,128)(2,1)S(1)} %get-tuple-element.25), channel_id=1, source_target_pairs={{0,22},{1,3},{2,0},{3,5},{4,2},{5,7},{6,4},{7,9},{8,6},{9,11},{10,... | collective-permute-start | bytes 516104 | tf_op jit(solution)/shard_map/ppermute | solution.py:148
  41.7 19.6 %collective-permute-start.5 = (bf16[16,5376]{1,0:T(8,128)(2,1)S(1)}, bf16[16,5376]{1,0:T(8,128)(2,1)S(1)}, u32[]{:S(2)}, u32[]{:S(2)}) collective-permute-start(bf16[16,5376]{1,0:T(8,128)(2,1)S(1)} %get-tuple-element.32), channel_id=1, source_target_pairs={{0,8},{1,17},{2,10},{3,19},{4,12},{5,21},{6,14},{7,23},{8,16},{9,1... | collective-permute-start | bytes 516104 | tf_op jit(solution)/shard_map/ppermute | solution.py:148
  45.6 21.5 %collective-permute-start.6 = (bf16[16,5376]{1,0:T(8,128)(2,1)S(1)}, bf16[16,5376]{1,0:T(8,128)(2,1)S(1)}, u32[]{:S(2)}, u32[]{:S(2)}) collective-permute-start(bf16[16,5376]{1,0:T(8,128)(2,1)S(1)} %get-tuple-element.33), channel_id=1, source_target_pairs={{0,16},{1,9},{2,18},{3,11},{4,20},{5,13},{6,22},{7,15},{8,0},{9,17... | collective-permute-start | bytes 516104 | tf_op jit(solution)/shard_map/ppermute | solution.py:148
  67.5 10.8 %copy-start.6 = (s32[1,32,2]{1,2,0:T(2,128)S(1)}, s32[1,32,2]{1,2,0:T(2,128)}, u32[]{:S(2)}) copy-start(s32[1,32,2]{1,2,0:T(2,128)} %param.12) | copy-start | bytes 772
  67.5 11.0 %copy-start.7 = (s32[16]{0:T(128)S(1)}, s32[16]{0:T(128)}, u32[]{:S(2)}) copy-start(s32[16]{0:T(128)} %param.11) | copy-start | bytes 196
  68.6 27.0 %all-to-all-start = ((bf16[32,2,5376]{2,1,0:T(2,128)(2,1)}), bf16[32,2,5376]{2,1,0:T(2,128)(2,1)S(1)}, u32[]{:S(2)}, u32[]{:S(2)}) async-start(bf16[32,2,5376]{2,1,0:T(2,128)(2,1)} %reshape.68), calls=%async_computation | async-start | bytes 1376256 | tf_op jit(solution)/shard_map/all_to_all | solution.py:183
  78.3 17.8 %copy-start.3 = (f32[16,5376]{1,0:T(8,128)S(1)}, f32[16,5376]{1,0:T(8,128)}, u32[]{:S(2)}) copy-start(f32[16,5376]{1,0:T(8,128)} %param.15) | copy-start | bytes 1032196
  78.3 17.8 %copy-start.4 = (f32[16,5376]{1,0:T(8,128)S(1)}, f32[16,5376]{1,0:T(8,128)}, u32[]{:S(2)}) copy-start(f32[16,5376]{1,0:T(8,128)} %param.14) | copy-start | bytes 1032196
  78.3 17.8 %copy-start.5 = (f32[16,5376]{1,0:T(8,128)S(1)}, f32[16,5376]{1,0:T(8,128)}, u32[]{:S(2)}) copy-start(f32[16,5376]{1,0:T(8,128)} %param.13) | copy-start | bytes 1032196
  97.7 25.5 %all-to-all-start.1 = ((bf16[32,2,5376]{2,1,0:T(2,128)(2,1)}), bf16[32,2,5376]{2,1,0:T(2,128)(2,1)S(1)}, u32[]{:S(2)}, u32[]{:S(2)}) async-start(bf16[32,2,5376]{2,1,0:T(2,128)(2,1)} %reshape.70), calls=%async_computation.1 | async-start | bytes 1376256 | tf_op jit(solution)/shard_map/all_to_all | solution.py:183
  143.0 13.2 %collective-permute-start.13 = (bf16[64,3584]{1,0:T(8,128)(2,1)S(1)}, bf16[64,3584]{1,0:T(8,128)(2,1)S(1)}, u32[]{:S(2)}, u32[]{:S(2)}) collective-permute-start(bf16[64,3584]{1,0:T(8,128)(2,1)S(1)} %slice.37), channel_id=1, source_target_pairs={{0,22},{1,3},{2,0},{3,5},{4,2},{5,7},{6,4},{7,9},{8,6},{9,11},{10,... | collective-permute-start | bytes 1376264 | tf_op jit(solution)/shard_map/ppermute | solution.py:148
  144.9 11.9 %collective-permute-start.14 = (bf16[64,3584]{1,0:T(8,128)(2,1)S(1)}, bf16[64,3584]{1,0:T(8,128)(2,1)S(1)}, u32[]{:S(2)}, u32[]{:S(2)}) collective-permute-start(bf16[64,3584]{1,0:T(8,128)(2,1)S(1)} %slice.37), channel_id=1, source_target_pairs={{0,2},{1,23},{2,4},{3,1},{4,6},{5,3},{6,8},{7,5},{8,10},{9,7},{10,... | collective-permute-start | bytes 1376264 | tf_op jit(solution)/shard_map/ppermute | solution.py:148
  149.7 16.5 %collective-permute-start.10 = (bf16[64,1792]{1,0:T(8,128)(2,1)S(1)}, bf16[64,1792]{1,0:T(8,128)(2,1)S(1)}, u32[]{:S(2)}, u32[]{:S(2)}) collective-permute-start(bf16[64,1792]{1,0:T(8,128)(2,1)S(1)} %slice.36), channel_id=1, source_target_pairs={{0,22},{1,3},{2,0},{3,5},{4,2},{5,7},{6,4},{7,9},{8,6},{9,11},{10,... | collective-permute-start | bytes 688136 | tf_op jit(solution)/shard_map/ppermute | solution.py:148
  151.6 14.6 %collective-permute-start.11 = (bf16[64,1792]{1,0:T(8,128)(2,1)S(1)}, bf16[64,1792]{1,0:T(8,128)(2,1)S(1)}, u32[]{:S(2)}, u32[]{:S(2)}) collective-permute-start(bf16[64,1792]{1,0:T(8,128)(2,1)S(1)} %slice.36), channel_id=1, source_target_pairs={{0,2},{1,23},{2,4},{3,1},{4,6},{5,3},{6,8},{7,5},{8,10},{9,7},{10,... | collective-permute-start | bytes 688136 | tf_op jit(solution)/shard_map/ppermute | solution.py:148
  157.3 13.5 %copy-start.2 = (s32[128]{0:T(128)S(1)}, s32[128]{0:T(128)}, u32[]{:S(2)}) copy-start(s32[128]{0:T(128)} %param.9) | copy-start | bytes 1540
  157.3 14.3 %collective-permute-start.15 = (bf16[128,3584]{1,0:T(8,128)(2,1)S(1)}, bf16[128,3584]{1,0:T(8,128)(2,1)S(1)}, u32[]{:S(2)}, u32[]{:S(2)}) collective-permute-start(bf16[128,3584]{1,0:T(8,128)(2,1)S(1)} %convolution_convert_fusion.3), channel_id=1, source_target_pairs={{0,1},{1,0},{2,3},{3,2},{4,5},{5,4},{6,7},{7,6},{8,9},{9,8},{10,11... | collective-permute-start | bytes 2752520 | tf_op jit(solution)/shard_map/ppermute | solution.py:210
  166.6 6.2 %collective-permute-start.12 = (bf16[128,1792]{1,0:T(8,128)(2,1)S(1)}, bf16[128,1792]{1,0:T(8,128)(2,1)S(1)}, u32[]{:S(2)}, u32[]{:S(2)}) collective-permute-start(bf16[128,1792]{1,0:T(8,128)(2,1)S(1)} %convolution_convert_fusion.5), channel_id=1, source_target_pairs={{0,1},{1,0},{2,3},{3,2},{4,5},{5,4},{6,7},{7,6},{8,9},{9,8},{10,11... | collective-permute-start | bytes 1376264 | tf_op jit(solution)/shard_map/ppermute | solution.py:210
